TPU v7x, 32 devices: a whole 2x2x4 slice. The times are simulated.
32 devices in a mesh: dp: 8 (over z, x), tensor: 4 (over y, core).
Axes of the slice: x: 2, y: 2, z: 4, core: 2. Of those that a mesh axis runs over, the one named last changes fastest.
Arguments:
- tokens: bfloat16 [16384, 768], P(('dp', 'tensor')), may hold values from -6 to 6
- segment_ids: int32 [16384], P('dp'), may hold values from -1 to 7, as said below
- ln1_gain: float32 [768], replicated, may hold values from 0.5 to 1.5
- ln1_bias: float32 [768], replicated, may hold values from -1.25 to 1.25
- ln2_gain: float32 [768], replicated, may hold values from 0.5 to 1.5
- ln2_bias: float32 [768], replicated, may hold values from -1.25 to 1.25
- w_qkv: bfloat16 [768, 2304], P('dp', 'tensor'), may hold values from -0.21875 to 0.21875
- b_qkv: float32 [2304], P('tensor'), may hold values from -1.25 to 1.25
- w_dense: bfloat16 [768, 768], P('dp', 'tensor'), may hold values from -2.5 to 2.5
- b_dense: float32 [768], replicated, may hold values from -1.25 to 1.25
- w_fc1: bfloat16 [768, 3072], P('dp', 'tensor'), may hold values from -0.21875 to 0.21875
- b_fc1: float32 [3072], P('tensor'), may hold values from -1.25 to 1.25
- w_fc2: bfloat16 [768, 3072], P('dp', 'tensor'), may hold values from -0.109375 to 0.109375
- b_fc2: float32 [768], replicated, may hold values from -1.25 to 1.25
- cotangent: bfloat16 [16384, 768], P(('dp', 'tensor')), may hold values from -6 to 6
Outputs:
- out: bfloat16 [16384, 768], P(('dp', 'tensor'))
- input_grad: float32 [16384, 768], P(('dp', 'tensor'))
- ln1_gain_grad: float32 [768], P(('dp', 'tensor'))
- ln1_bias_grad: float32 [768], P(('dp', 'tensor'))
- ln2_gain_grad: float32 [768], P(('dp', 'tensor'))
- ln2_bias_grad: float32 [768], P(('dp', 'tensor'))
- w_qkv_grad: float32 [768, 2304], P('dp', 'tensor')
- b_qkv_grad: float32 [2304], P(('tensor', 'dp'))
- w_dense_grad: float32 [768, 768], P('dp', 'tensor')
- b_dense_grad: float32 [768], P(('dp', 'tensor'))
- w_fc1_grad: float32 [768, 3072], P('dp', 'tensor')
- b_fc1_grad: float32 [3072], P(('tensor', 'dp'))
- w_fc2_grad: float32 [768, 3072], P('dp', 'tensor')
- b_fc2_grad: float32 [768], P(('dp', 'tensor'))
Inputs may be any that keep to these rules, and one draw needn't show every extreme that they name: `segment_ids`: each group of 2048 rows (one index of dp) holds one whole sequence from its first row, of more than 1536 rows, and padding rows with id -1 after it; the sequences' ids are distinct; in every draw some group's sequence fills all 2048 rows.
All inputs are finite; a program needn't handle non-finite values.
Results may differ from a plain program's by a relative error of at most 0.013.
Values may be sent and summed in bfloat16 or wider, within the bound.
No kernel may reach another device: no remote copies, remote signals or barrier semaphores. Data moves between devices by JAX's collectives and lax.ppermute only.
A program may use at most 128 MiB of HBM per device.

v0:
```python
import jax
import jax.numpy as jnp
from jax import lax
from jax.sharding import PartitionSpec as P

HEAD = 64
ROT = 16


EPS = 1e-05
NEG = -1e30


def layer_norm(values, gain, bias):
    center = values - jnp.mean(values, axis=-1, keepdims=True)
    spread = jnp.mean(center * center, axis=-1, keepdims=True)
    return center * lax.rsqrt(spread + EPS) * gain + bias


def norm_pair(values, gain_one, bias_one, gain_two, bias_two):
    return (layer_norm(values, gain_one, bias_one), layer_norm(values, gain_two, bias_two))


def angle_tables(seg_rows):
    count = seg_rows.shape[0]
    row_index = jnp.arange(count, dtype=jnp.int32)
    prior = jnp.concatenate([seg_rows[:1] - 1, seg_rows[:-1]])
    starts = lax.cummax(jnp.where(seg_rows != prior, row_index, 0), axis=0)
    places = (row_index - starts).astype(jnp.float32)
    inverse = 10000.0 ** (-jnp.arange(0, ROT, 2, dtype=jnp.float32) / ROT)
    angles = places[:, None] * inverse[None, :]
    angles = jnp.concatenate([angles, angles], axis=-1)
    return (jnp.cos(angles)[:, None, :], jnp.sin(angles)[:, None, :])


def rotate(parts, cosine, sine):
    half = ROT // 2
    front = parts[..., :ROT]
    turned = jnp.concatenate([-front[..., half:], front[..., :half]], axis=-1)
    return jnp.concatenate([front * cosine + turned * sine, parts[..., ROT:]], axis=-1)


def unrotate(grads, cosine, sine):
    half = ROT // 2
    front = grads[..., :ROT]
    turned = front * sine
    back = front * cosine + jnp.concatenate([turned[..., half:], -turned[..., :half]], axis=-1)
    return jnp.concatenate([back, grads[..., ROT:]], axis=-1)


def masked_scores(query_block, keys, query_segs, seg_rows, begin, block_rows):
    raw = jnp.einsum("qhd,khd->hqk", query_block, keys, preferred_element_type=jnp.float32)
    query_index = begin + jnp.arange(block_rows, dtype=jnp.int32)
    key_index = jnp.arange(keys.shape[0], dtype=jnp.int32)
    allowed = (query_segs[:, None] == seg_rows[None, :]) & (
        key_index[None, :] <= query_index[:, None]
    )
    return jnp.where(allowed[None], raw * HEAD ** (-0.5), NEG)


def attend(queries, keys, values, seg_rows, block_rows):
    count, head_count = (keys.shape[0], keys.shape[1])

    def one_block(begin):
        query_block = lax.dynamic_slice_in_dim(queries, begin, block_rows, 0)
        query_segs = lax.dynamic_slice_in_dim(seg_rows, begin, block_rows, 0)
        scores = masked_scores(query_block, keys, query_segs, seg_rows, begin, block_rows)
        top = jnp.max(scores, axis=-1, keepdims=True)
        expo = jnp.exp(scores - top)
        total = jnp.sum(expo, axis=-1, keepdims=True)
        probs = (expo / total).astype(jnp.bfloat16)
        result = jnp.einsum("hqk,khd->qhd", probs, values, preferred_element_type=jnp.float32)
        return (result, (top + jnp.log(total))[..., 0])

    begins = jnp.arange(count // block_rows, dtype=jnp.int32) * block_rows
    results, logsum = lax.map(one_block, begins)
    return (results.reshape(count, head_count, HEAD), logsum)


def attend_back(queries, keys, values, out_grads, logsum, seg_rows, block_rows):
    count, head_count = (keys.shape[0], keys.shape[1])
    scale = HEAD ** (-0.5)

    def one_block(carry, pieces):
        key_total, value_total = carry
        begin, logsum_block = pieces
        query_block = lax.dynamic_slice_in_dim(queries, begin, block_rows, 0)
        grad_block = lax.dynamic_slice_in_dim(out_grads, begin, block_rows, 0)
        query_segs = lax.dynamic_slice_in_dim(seg_rows, begin, block_rows, 0)
        scores = masked_scores(query_block, keys, query_segs, seg_rows, begin, block_rows)
        probs = jnp.exp(scores - logsum_block[..., None])
        prob_grad = jnp.einsum(
            "qhd,khd->hqk", grad_block, values, preferred_element_type=jnp.float32
        )
        inner = jnp.sum(probs * prob_grad, axis=-1, keepdims=True)
        score_grad = (probs * (prob_grad - inner) * scale).astype(jnp.bfloat16)
        query_grad = jnp.einsum(
            "hqk,khd->qhd", score_grad, keys, preferred_element_type=jnp.float32
        )
        key_total = key_total + jnp.einsum(
            "hqk,qhd->khd", score_grad, query_block, preferred_element_type=jnp.float32
        )
        value_total = value_total + jnp.einsum(
            "hqk,qhd->khd",
            probs.astype(jnp.bfloat16),
            grad_block,
            preferred_element_type=jnp.float32,
        )
        return ((key_total, value_total), query_grad)

    begins = jnp.arange(count // block_rows, dtype=jnp.int32) * block_rows
    zeros = jnp.zeros((count, head_count, HEAD), jnp.float32)
    (key_grad, value_grad), query_grad = lax.scan(one_block, (zeros, zeros), (begins, logsum))
    return (query_grad.reshape(count, head_count, HEAD), key_grad, value_grad)


def body(
    tokens,
    segment_ids,
    ln1_gain,
    ln1_bias,
    ln2_gain,
    ln2_bias,
    w_qkv,
    b_qkv,
    w_dense,
    b_dense,
    w_fc1,
    b_fc1,
    w_fc2,
    b_fc2,
    cotangent,
):
    group_rows = segment_ids.shape[0]
    head_count = w_qkv.shape[1] // (3 * HEAD)
    block_rows = min(512, group_rows)
    cosine, sine = angle_tables(segment_ids)
    qkv_full, dense_full, up_full, down_full = (
        lax.all_gather(w_qkv, "dp", axis=0, tiled=True),
        lax.all_gather(w_dense, "dp", axis=0, tiled=True),
        lax.all_gather(w_fc1, "dp", axis=0, tiled=True),
        lax.all_gather(w_fc2, "dp", axis=0, tiled=True),
    )
    own_input = tokens.astype(jnp.float32)
    own_one, own_two = norm_pair(own_input, ln1_gain, ln1_bias, ln2_gain, ln2_bias)
    normed_one, normed_two = (
        lax.all_gather(own_one.astype(jnp.bfloat16), "tensor", axis=0, tiled=True),
        lax.all_gather(own_two.astype(jnp.bfloat16), "tensor", axis=0, tiled=True),
    )
    mixed = (jnp.dot(normed_one, qkv_full, preferred_element_type=jnp.float32) + b_qkv).reshape(
        group_rows, head_count, 3 * HEAD
    )
    queries = rotate(mixed[..., :HEAD], cosine, sine).astype(jnp.bfloat16)
    keys = rotate(mixed[..., HEAD : 2 * HEAD], cosine, sine).astype(jnp.bfloat16)
    values = mixed[..., 2 * HEAD :].astype(jnp.bfloat16)
    attended, logsum = attend(queries, keys, values, segment_ids, block_rows)
    attended = attended.astype(jnp.bfloat16).reshape(group_rows, head_count * HEAD)
    hidden = jnp.dot(normed_two, up_full, preferred_element_type=jnp.float32) + b_fc1
    active = jax.nn.gelu(hidden, approximate=False).astype(jnp.bfloat16)
    first = jnp.einsum("gi,oi->go", attended, dense_full, preferred_element_type=jnp.float32)
    second = jnp.einsum("gf,of->go", active, down_full, preferred_element_type=jnp.float32)
    summed = lax.psum_scatter(
        (first + second).astype(jnp.bfloat16), "tensor", scatter_dimension=0, tiled=True
    ).astype(jnp.float32)
    out = (own_input + summed + b_dense + b_fc2).astype(jnp.bfloat16)
    qkv_full, dense_full, up_full, down_full = (
        lax.all_gather(w_qkv, "dp", axis=0, tiled=True),
        lax.all_gather(w_dense, "dp", axis=0, tiled=True),
        lax.all_gather(w_fc1, "dp", axis=0, tiled=True),
        lax.all_gather(w_fc2, "dp", axis=0, tiled=True),
    )
    grad_rows = lax.all_gather(cotangent, "tensor", axis=0, tiled=True)
    own_grad = cotangent.astype(jnp.float32)
    out_bias_grad = jnp.sum(own_grad, axis=0)
    down_grad = jnp.einsum("gd,gf->df", grad_rows, active, preferred_element_type=jnp.float32)
    active_grad = jnp.einsum("gd,df->gf", grad_rows, down_full, preferred_element_type=jnp.float32)
    _, gelu_pull = jax.vjp(lambda inner: jax.nn.gelu(inner, approximate=False), hidden)
    hidden_grad = gelu_pull(active_grad)[0].astype(jnp.bfloat16)
    up_grad = jnp.einsum("gd,gf->df", normed_two, hidden_grad, preferred_element_type=jnp.float32)
    up_bias_grad = jnp.sum(hidden_grad.astype(jnp.float32), axis=0)
    normed_two_grad = jnp.einsum(
        "gf,df->gd", hidden_grad, up_full, preferred_element_type=jnp.float32
    )
    dense_grad = jnp.einsum("gd,gi->di", grad_rows, attended, preferred_element_type=jnp.float32)
    attended_grad = jnp.einsum(
        "gd,di->gi", grad_rows, dense_full, preferred_element_type=jnp.float32
    )
    attended_grad = attended_grad.astype(jnp.bfloat16).reshape(group_rows, head_count, HEAD)
    query_grad, key_grad, value_grad = attend_back(
        queries, keys, values, attended_grad, logsum, segment_ids, block_rows
    )
    mixed_grad = jnp.concatenate(
        [unrotate(query_grad, cosine, sine), unrotate(key_grad, cosine, sine), value_grad], axis=-1
    )
    mixed_grad = mixed_grad.astype(jnp.bfloat16).reshape(group_rows, 3 * head_count * HEAD)
    qkv_grad = jnp.einsum("gd,gc->dc", normed_one, mixed_grad, preferred_element_type=jnp.float32)
    qkv_bias_grad = jnp.sum(mixed_grad.astype(jnp.float32), axis=0)
    normed_one_grad = jnp.einsum(
        "gc,dc->gd", mixed_grad, qkv_full, preferred_element_type=jnp.float32
    )
    qkv_owned, qkv_bias_owned, dense_owned, up_owned, up_bias_owned, down_owned = (
        lax.psum_scatter(qkv_grad, "dp", scatter_dimension=0, tiled=True),
        lax.psum_scatter(qkv_bias_grad, "dp", scatter_dimension=0, tiled=True),
        lax.psum_scatter(dense_grad, "dp", scatter_dimension=0, tiled=True),
        lax.psum_scatter(up_grad, "dp", scatter_dimension=0, tiled=True),
        lax.psum_scatter(up_bias_grad, "dp", scatter_dimension=0, tiled=True),
        lax.psum_scatter(down_grad, "dp", scatter_dimension=0, tiled=True),
    )
    own_one_grad, own_two_grad = (
        lax.psum_scatter(
            normed_one_grad.astype(jnp.bfloat16), "tensor", scatter_dimension=0, tiled=True
        ).astype(jnp.float32),
        lax.psum_scatter(
            normed_two_grad.astype(jnp.bfloat16), "tensor", scatter_dimension=0, tiled=True
        ).astype(jnp.float32),
    )
    _, norm_pull = jax.vjp(norm_pair, own_input, ln1_gain, ln1_bias, ln2_gain, ln2_bias)
    input_part, gain_one, bias_one, gain_two, bias_two = norm_pull((own_one_grad, own_two_grad))
    input_grad = own_grad + input_part
    gain_one, bias_one, gain_two, bias_two, out_bias_owned = (
        lax.psum_scatter(gain_one, ("dp", "tensor"), scatter_dimension=0, tiled=True),
        lax.psum_scatter(bias_one, ("dp", "tensor"), scatter_dimension=0, tiled=True),
        lax.psum_scatter(gain_two, ("dp", "tensor"), scatter_dimension=0, tiled=True),
        lax.psum_scatter(bias_two, ("dp", "tensor"), scatter_dimension=0, tiled=True),
        lax.psum_scatter(out_bias_grad, ("dp", "tensor"), scatter_dimension=0, tiled=True),
    )
    return (
        out,
        input_grad,
        gain_one,
        bias_one,
        gain_two,
        bias_two,
        qkv_owned,
        qkv_bias_owned,
        dense_owned,
        out_bias_owned,
        up_owned,
        up_bias_owned,
        down_owned,
        out_bias_owned,
    )


def solution(mesh):
    placed = (
        P(("dp", "tensor"), None),
        P("dp"),
        P(),
        P(),
        P(),
        P(),
        P("dp", "tensor"),
        P("tensor"),
        P("dp", "tensor"),
        P(),
        P("dp", "tensor"),
        P("tensor"),
        P("dp", "tensor"),
        P(),
        P(("dp", "tensor"), None),
    )
    return jax.shard_map(
        body,
        mesh=mesh,
        in_specs=placed,
        out_specs=(
            P(("dp", "tensor"), None),
            P(("dp", "tensor"), None),
            P(("dp", "tensor")),
            P(("dp", "tensor")),
            P(("dp", "tensor")),
            P(("dp", "tensor")),
            P("dp", "tensor"),
            P(("tensor", "dp")),
            P("dp", "tensor"),
            P(("dp", "tensor")),
            P("dp", "tensor"),
            P(("tensor", "dp")),
            P("dp", "tensor"),
            P(("dp", "tensor")),
        ),
        check_vma=False,
    )
```

profile of v0, /device:TPU:0, one launch (start us, length us, event | category | flops | bytes accessed | tf_op | source)
XLA Modules:
  0.0 908.0 jit_solution(2787302655301106015)
XLA Ops:
  10.2 2.8 fusion.96
  18.0 32.9 %all_gather.27 = bf16[768,192]{1,0:T(8,128)(2,1)S(1)} all-gather(bf16[96,192]{1,0:T(8,128)(2,1)S(1)} %copy-done.30), channel_id=1, replica_groups=mesh['dp'=8,'tensor'=4] {'dp'}, dimensions={0}, use_global_device_ids=true | all-gather | bytes 331776 | tf_op jit(solution)/shard_map/all_gather | solution.py:140
  50.9 32.3 %all_gather.26 = bf16[768,576]{1,0:T(8,128)(2,1)S(1)} all-gather(bf16[96,576]{1,0:T(8,128)(2,1)S(1)} %copy-done.25), channel_id=1, replica_groups=mesh['dp'=8,'tensor'=4] {'dp'}, dimensions={0}, use_global_device_ids=true | all-gather | bytes 995328 | tf_op jit(solution)/shard_map/all_gather | solution.py:139
  83.2 4.3 convolution_add_fusion
  89.3 104.4 %while.27 = (s32[]{:T(128)}, bf16[4,512,3,64]{1,3,2,0:T(8,128)(2,1)}, f32[4,3,512]{2,1,0:T(4,128)S(1)}, s32[4]{0:T(128)S(1)}, s32[2048]{0:T(1024)S(1)}, /*index=...) while((s32[]{:T(128)}, ...), condition=%wide.region_7.8_spmd, body=%wide.region_4.0_spmd.sunk | while | flops 846199808 | bytes 50475248 | solution.py:76
  93.8 7.0 fusion.181
  100.8 7.0 fusion.182
  107.8 6.7 fusion.183
  119.9 7.5 fusion.181
  127.3 6.9 fusion.182
  134.2 6.7 fusion.183
  146.3 7.0 fusion.181
  153.3 6.9 fusion.182
  160.2 6.7 fusion.183
  172.3 7.0 fusion.181
  179.3 6.9 fusion.182
  186.1 6.7 fusion.183
  193.8 4.0 convolution_convert_fusion.2
  197.7 290.5 %while.28 = (s32[]{:T(128)}, f32[2048,3,64]{0,2,1:T(8,128)}, f32[2048,3,64]{0,2,1:T(8,128)}, f32[4,512,3,64]{1,0,3,2:T(4,128)}, s32[4]{0:T(128)S(1)}, /*index=5*...) while((s32[]{:T(128)}, f32[2048,3,64]{0,2,1:T(8,128)}, ...), condition=%wide.region_14.15_spmd.clone, body=%wide.region_12.14_spmd.clone.sunk | while | flops 2099781120 | bytes 192866624 | solution.py:113
  202.5 3.0 fusion.195
  205.6 4.9 fusion.198
  211.7 7.3 fusion.194
  219.0 20.0 %fusion.199 = f32[1,512,3,64]{1,3,2,0:T(8,128)S(1)} fusion(bf16[2048,3,64]{0,2,1:T(8,128)(2,1)S(1)} %get-tuple-element.472, f32[3,512,2048]{2,1,0:T(8,128)} %fusion.194, f32[3,512,2048]{2,1,0:T(8,128)} %copy-done, f32[3,512]{1,0:T(4,128)S(1)} %dynamic-slice_bitcast_fusion.2, pred[512,2048]{1,0:T(8,128)(4,1)S(1)} %fusion.196), kind=kOutput, calls=%fused_computation.41.clone.1 | convolution fusion | flops 437259776 | bytes 27400192 | tf_op jit(solution)/shard_map/while/body/eval_jaxpr/hqk,khd->qhd/dot_general | solution.py:97
  239.1 22.2 %fusion.197 = f32[2048,3,64]{0,2,1:T(8,128)} fusion(f32[3,512,2048]{2,1,0:T(8,128)} %fusion.194, f32[3,512,2048]{2,1,0:T(8,128)} %copy-done, f32[3,512]{1,0:T(4,128)S(1)} %dynamic-slice_bitcast_fusion.2, pred[512,2048]{1,0:T(8,128)(4,1)S(1)} %fusion.196, f32[2048,3,64]{0,2,1:T(8,128)} %get-tuple-element.452, pred[]{:T(512)S(6)} %compare.3, ...), kind=kOutput, calls=%fused_computation.39.clone.1 | convolution fusion | flops 438046208 | bytes 55787524 | tf_op jit(solution)/shard_map/while/body/eval_jaxpr/hqk,qhd->khd/dot_general | solution.py:100
  261.7 8.6 dynamic_update_slice.19
  274.8 3.0 fusion.195
  277.8 4.9 fusion.198
  283.9 7.3 fusion.194
  291.3 20.0 %fusion.199 = f32[1,512,3,64]{1,3,2,0:T(8,128)S(1)} fusion(bf16[2048,3,64]{0,2,1:T(8,128)(2,1)S(1)} %get-tuple-element.472, f32[3,512,2048]{2,1,0:T(8,128)} %fusion.194, f32[3,512,2048]{2,1,0:T(8,128)} %copy-done, f32[3,512]{1,0:T(4,128)S(1)} %dynamic-slice_bitcast_fusion.2, pred[512,2048]{1,0:T(8,128)(4,1)S(1)} %fusion.196), kind=kOutput, calls=%fused_computation.41.clone.1 | convolution fusion | flops 437259776 | bytes 27400192 | tf_op jit(solution)/shard_map/while/body/eval_jaxpr/hqk,khd->qhd/dot_general | solution.py:97
  311.3 22.6 %fusion.197 = f32[2048,3,64]{0,2,1:T(8,128)} fusion(f32[3,512,2048]{2,1,0:T(8,128)} %fusion.194, f32[3,512,2048]{2,1,0:T(8,128)} %copy-done, f32[3,512]{1,0:T(4,128)S(1)} %dynamic-slice_bitcast_fusion.2, pred[512,2048]{1,0:T(8,128)(4,1)S(1)} %fusion.196, f32[2048,3,64]{0,2,1:T(8,128)} %get-tuple-element.452, pred[]{:T(512)S(6)} %compare.3, ...), kind=kOutput, calls=%fused_computation.39.clone.1 | convolution fusion | flops 438046208 | bytes 55787524 | tf_op jit(solution)/shard_map/while/body/eval_jaxpr/hqk,qhd->khd/dot_general | solution.py:100
  334.3 8.6 dynamic_update_slice.19
  347.4 3.0 fusion.195
  350.4 4.9 fusion.198
  356.6 7.3 fusion.194
  363.9 20.0 %fusion.199 = f32[1,512,3,64]{1,3,2,0:T(8,128)S(1)} fusion(bf16[2048,3,64]{0,2,1:T(8,128)(2,1)S(1)} %get-tuple-element.472, f32[3,512,2048]{2,1,0:T(8,128)} %fusion.194, f32[3,512,2048]{2,1,0:T(8,128)} %copy-done, f32[3,512]{1,0:T(4,128)S(1)} %dynamic-slice_bitcast_fusion.2, pred[512,2048]{1,0:T(8,128)(4,1)S(1)} %fusion.196), kind=kOutput, calls=%fused_computation.41.clone.1 | convolution fusion | flops 437259776 | bytes 27400192 | tf_op jit(solution)/shard_map/while/body/eval_jaxpr/hqk,khd->qhd/dot_general | solution.py:97
  384.0 22.6 %fusion.197 = f32[2048,3,64]{0,2,1:T(8,128)} fusion(f32[3,512,2048]{2,1,0:T(8,128)} %fusion.194, f32[3,512,2048]{2,1,0:T(8,128)} %copy-done, f32[3,512]{1,0:T(4,128)S(1)} %dynamic-slice_bitcast_fusion.2, pred[512,2048]{1,0:T(8,128)(4,1)S(1)} %fusion.196, f32[2048,3,64]{0,2,1:T(8,128)} %get-tuple-element.452, pred[]{:T(512)S(6)} %compare.3, ...), kind=kOutput, calls=%fused_computation.39.clone.1 | convolution fusion | flops 438046208 | bytes 55787524 | tf_op jit(solution)/shard_map/while/body/eval_jaxpr/hqk,qhd->khd/dot_general | solution.py:100
  407.0 8.6 dynamic_update_slice.19
  420.0 3.0 fusion.195
  423.1 4.8 fusion.198
  429.1 7.3 fusion.194
  436.4 20.0 %fusion.199 = f32[1,512,3,64]{1,3,2,0:T(8,128)S(1)} fusion(bf16[2048,3,64]{0,2,1:T(8,128)(2,1)S(1)} %get-tuple-element.472, f32[3,512,2048]{2,1,0:T(8,128)} %fusion.194, f32[3,512,2048]{2,1,0:T(8,128)} %copy-done, f32[3,512]{1,0:T(4,128)S(1)} %dynamic-slice_bitcast_fusion.2, pred[512,2048]{1,0:T(8,128)(4,1)S(1)} %fusion.196), kind=kOutput, calls=%fused_computation.41.clone.1 | convolution fusion | flops 437259776 | bytes 27400192 | tf_op jit(solution)/shard_map/while/body/eval_jaxpr/hqk,khd->qhd/dot_general | solution.py:97
  456.5 22.6 %fusion.197 = f32[2048,3,64]{0,2,1:T(8,128)} fusion(f32[3,512,2048]{2,1,0:T(8,128)} %fusion.194, f32[3,512,2048]{2,1,0:T(8,128)} %copy-done, f32[3,512]{1,0:T(4,128)S(1)} %dynamic-slice_bitcast_fusion.2, pred[512,2048]{1,0:T(8,128)(4,1)S(1)} %fusion.196, f32[2048,3,64]{0,2,1:T(8,128)} %get-tuple-element.452, pred[]{:T(512)S(6)} %compare.3, ...), kind=kOutput, calls=%fused_computation.39.clone.1 | convolution fusion | flops 438046208 | bytes 55787524 | tf_op jit(solution)/shard_map/while/body/eval_jaxpr/hqk,qhd->khd/dot_general | solution.py:100
  479.5 8.6 dynamic_update_slice.19
  493.9 4.1 convolution_convert_fusion
  498.1 7.6 fusion.123
  505.8 20.6 %convert_reduce_fusion = (f32[768]{0:T(1024)S(1)}, bf16[2048,768]{1,0:T(8,128)(2,1)S(1)}, f32[2048,768]{1,0:T(8,128)}) fusion(f32[2048,768]{1,0:T(8,128)} %fusion.123, f32[768]{0:T(1024)S(1)} %copy-done.35, bf16[2048,768]{1,0:T(8,128)(2,1)S(1)} %copy-done.2, bf16[768,768]{1,0:T(8,128)(2,1)} %all-gather.12.cloned.1.call-done), kind=kOutput, calls=%fused_computation.64 | convolution fusion | flops 2533883136 | bytes 20060160 | tf_op jit(solution)/shard_map/gd,df->gf/dot_general | solution.py:176
  528.1 4.0 convolution_convert_fusion.1
  534.3 5.9 multiply_convert_fusion.1
  540.2 2.6 fusion.124
  542.9 2.7 add_convert_fusion.1
  545.7 2.8 convolution_bitcast_fusion.1
  550.9 6.6 fusion.125
  557.6 6.3 convolution_bitcast_fusion
  563.9 3.2 copy.41
  567.4 7.1 fusion.126
  577.0 22.3 %all-reduce.8 = (f32[576]{0:T(1024)S(1)}, f32[768]{0:T(1024)S(1)}) all-reduce(f32[576]{0:T(1024)S(1)} %reduce_sum.156, f32[768]{0:T(1024)S(1)} %get-tuple-element.254), channel_id=10, replica_groups=mesh['dp'=8,'tensor'=4] {'dp'}, use_global_device_ids=true, to_apply=%region_28.29.clone | all-reduce | flops 1344 | bytes 10752
  602.9 3.0 fusion.105
  605.9 13.0 %reduce-scatter.12.cloned.1.call-done = bf16[512,768]{1,0:T(8,128)(2,1)} async-done(((bf16[2048,768]{1,0:T(8,128)(2,1)}), bf16[512,768]{1,0:T(8,128)(2,1)}) %reduce-scatter.12.cloned.1.call-update) | async-done | bytes 786448 | tf_op jit(solution)/shard_map/reduce_scatter | solution.py:162
  618.9 3.5 convert_reduce_fusion.5
  622.4 39.9 %all-reduce.7 = (f32[768]{0:T(1024)S(1)}, f32[768]{0:T(1024)S(1)}, f32[768]{0:T(1024)S(1)}, f32[768]{0:T(1024)S(1)}, f32[768]{0:T(1024)S(1)}) all-reduce(f32[768]{0:T(1024)S(1)} %get-tuple-element.204, f32[768]{0:T(1024)S(1)} %get-tuple-element.207, ...), channel_id=5, replica_groups=mesh['dp'=8,'tensor'=4] {'dp','tensor'}, use_global_device_ids=true, to_apply=%region_19.20.clone | all-reduce | flops 3840 | bytes 30720
  664.7 20.9 %reduce-scatter.22.cloned.1.call-done = f32[96,192]{1,0:T(8,128)} async-done(((f32[768,192]{1,0:T(8,128)}), f32[96,192]{1,0:T(8,128)}) %reduce-scatter.22.cloned.1.call-update) | async-done | bytes 73744
  685.6 69.8 %reduce-scatter.18.cloned.1.call-done = f32[96,576]{1,0:T(8,128)} async-done(((f32[768,576]{1,0:T(8,128)}), f32[96,576]{1,0:T(8,128)}) %reduce-scatter.18.cloned.1.call-update) | async-done | bytes 221200 | tf_op jit(solution)/shard_map/reduce_scatter | solution.py:202
  755.4 72.4 %reduce-scatter.24.cloned.1.call-done = f32[96,768]{1,0:T(8,128)} async-done(((f32[768,768]{1,0:T(8,128)}), f32[96,768]{1,0:T(8,128)}) %reduce-scatter.24.cloned.1.call-update) | async-done | bytes 294928
  827.8 72.4 %reduce-scatter.20.cloned.1.call-done = f32[96,768]{1,0:T(8,128)} async-done(((f32[768,768]{1,0:T(8,128)}), f32[96,768]{1,0:T(8,128)}) %reduce-scatter.20.cloned.1.call-update) | async-done | bytes 294928 | tf_op jit(solution)/shard_map/reduce_scatter | solution.py:205
  (246 shorter events, 58.7 us)
Async XLA Ops:
  7.2 8.6 copy-start.14
  7.2 10.8 %copy-start.30 = (bf16[96,192]{1,0:T(8,128)(2,1)S(1)}, bf16[96,192]{1,0:T(8,128)(2,1)}, u32[]{:S(2)}) copy-start(bf16[96,192]{1,0:T(8,128)(2,1)} %param.27) | copy-start | bytes 110596
  7.2 43.7 %copy-start.25 = (bf16[96,576]{1,0:T(8,128)(2,1)S(1)}, bf16[96,576]{1,0:T(8,128)(2,1)}, u32[]{:S(2)}) copy-start(bf16[96,576]{1,0:T(8,128)(2,1)} %param.25) | copy-start | bytes 331780
  7.2 76.0 %copy-start.40 = (f32[576]{0:T(1024)S(1)}, f32[576]{0:T(1024)}, u32[]{:S(2)}) copy-start(f32[576]{0:T(1024)} %param.26) | copy-start | bytes 6916
  7.2 76.0 %all-gather.6.cloned.1.call-start = ((), (), s32[]{:S(2)}) async-start(), calls=%async_computation.7 | async-start | bytes 3932160 | tf_op jit(solution)/shard_map/all_gather | solution.py:147
  8.6 78.9 %copy-start.26 = (f32[512]{0:T(512)}, f32[512]{0:T(512)S(1)}, u32[]{:S(2)}) copy-start(f32[512]{0:T(512)S(1)} %broadcast_multiply_fusion.1) | copy-start | bytes 6148
  10.1 77.4 %copy-start.33 = (f32[512]{0:T(512)}, f32[512]{0:T(512)S(1)}, u32[]{:S(2)}) copy-start(f32[512]{0:T(512)S(1)} %fusion.99) | copy-start | bytes 6148
  10.1 77.4 %copy-start.31 = (f32[512]{0:T(512)}, f32[512]{0:T(512)S(1)}, u32[]{:S(2)}) copy-start(f32[512]{0:T(512)S(1)} %fusion.118) | copy-start | bytes 6148
  13.0 180.8 %all-gather.14.cloned.1.call-start = ((), (), s32[]{:S(2)}) async-start(), calls=%async_computation.12 | async-start | bytes 3932160 | tf_op jit(solution)/shard_map/all_gather | solution.py:172
  13.8 484.3 %all-gather.10.cloned.1.call-start = ((), (), s32[]{:S(2)}) async-start(), calls=%async_computation.9 | async-start | bytes 1327104 | tf_op jit(solution)/shard_map/all_gather | solution.py:141
  14.5 483.6 %all-gather.8.cloned.1.call-start = ((), (), s32[]{:S(2)}) async-start(), calls=%async_computation.8 | async-start | bytes 3932160 | tf_op jit(solution)/shard_map/all_gather | solution.py:148
  15.1 490.7 %all-gather.12.cloned.1.call-start = ((), (), s32[]{:S(2)}) async-start(), calls=%async_computation.10 | async-start | bytes 1327104 | tf_op jit(solution)/shard_map/all_gather | solution.py:142
  15.7 584.8 %reduce-scatter.16.cloned.1.call-start = ((), (), s32[]{:S(2)}) async-start(), calls=%async_computation.14 | async-start | bytes 3932160 | tf_op jit(solution)/shard_map/reduce_scatter | solution.py:210
  18.0 70.2 %copy-start.12 = (f32[2048,16]{0,1:T(8,128)}, f32[2048,16]{0,1:T(8,128)S(1)}, u32[]{:S(2)}) copy-start(f32[2048,16]{0,1:T(8,128)S(1)} %get-tuple-element.278) | copy-start | bytes 393220
  18.0 70.2 %copy-start.19 = (f32[2048,16]{0,1:T(8,128)}, f32[2048,16]{0,1:T(8,128)S(1)}, u32[]{:S(2)}) copy-start(f32[2048,16]{0,1:T(8,128)S(1)} %get-tuple-element.279) | copy-start | bytes 393220
  50.9 142.9 %copy-start.6 = (bf16[768,192]{1,0:T(8,128)(2,1)}, bf16[768,192]{1,0:T(8,128)(2,1)S(1)}, u32[]{:S(2)}) copy-start(bf16[768,192]{1,0:T(8,128)(2,1)S(1)} %all_gather.27) | copy-start | bytes 884740
  83.2 4.4 copy-start.21
  100.8 7.0 copy-start.23
  127.3 6.9 copy-start.23
  153.3 6.9 copy-start.23
  179.3 6.9 copy-start.23
  197.7 293.1 %copy-start.20 = (f32[2048,16]{0,1:T(8,128)S(1)}, f32[2048,16]{0,1:T(8,128)}, u32[]{:S(2)}) copy-start(f32[2048,16]{0,1:T(8,128)} %copy-done.19) | copy-start | bytes 393220
  202.5 3.0 copy-start.15
  205.5 4.9 copy-start
  210.5 1.2 copy-start.16
  274.8 3.0 copy-start.15
  277.8 4.9 copy-start
  347.4 3.0 copy-start.15
  350.4 4.9 copy-start
  420.0 3.0 copy-start.15
  423.0 4.9 copy-start
  488.3 3.8 copy-start.13
  488.3 3.9 copy-start.18
  490.8 1.6 copy-start.17
  492.0 1.9 copy-start.22
  492.5 1.4 copy-start.8
  498.0 7.8 copy-start.2
  498.0 7.8 copy-start.35
  498.0 102.4 %reduce-scatter.14.cloned.1.call-start = ((), (), s32[]{:S(2)}) async-start(), calls=%async_computation.13 | async-start | bytes 3932160 | tf_op jit(solution)/shard_map/reduce_scatter | solution.py:213
  505.8 22.3 %copy-start.39 = (bf16[768,768]{1,0:T(8,128)(2,1)S(1)}, bf16[768,768]{1,0:T(8,128)(2,1)}, u32[]{:S(2)}) copy-start(bf16[768,768]{1,0:T(8,128)(2,1)} %all-gather.10.cloned.1.call-done) | copy-start | bytes 3538948
  526.4 1.7 copy-start.43
  532.1 86.7 %reduce-scatter.12.cloned.1.call-start = ((), (), s32[]{:S(2)}) async-start(), calls=%async_computation.11 | async-start | bytes 3932160 | tf_op jit(solution)/shard_map/reduce_scatter | solution.py:162
  534.3 8.6 copy-start.5
  534.3 5.9 copy-start.38
  540.2 2.7 copy-start.11
  540.2 2.7 copy-start.7
  545.7 139.9 %reduce-scatter.22.cloned.1.call-start = ((), (), s32[]{:S(2)}) async-start(), calls=%async_computation.17 | async-start | bytes 884736
  550.9 204.5 %reduce-scatter.18.cloned.1.call-start = ((), (), s32[]{:S(2)}) async-start(), calls=%async_computation.15 | async-start | bytes 2211840 | tf_op jit(solution)/shard_map/reduce_scatter | solution.py:202
  557.5 270.3 %reduce-scatter.24.cloned.1.call-start = ((), (), s32[]{:S(2)}) async-start(), calls=%async_computation.18 | async-start | bytes 2654208
  567.1 7.5 copy-start.41
  567.1 9.4 %copy-start.9 = (bf16[2048,3,192]{0,2,1:T(8,128)(2,1)S(1)}, bf16[2048,3,192]{0,2,1:T(8,128)(2,1)}, u32[]{:S(2)}) copy-start(bf16[2048,3,192]{0,2,1:T(8,128)(2,1)} %copy-done.8) | copy-start | bytes 7077892
  567.1 333.1 %reduce-scatter.20.cloned.1.call-start = ((), (), s32[]{:S(2)}) async-start(), calls=%async_computation.16 | async-start | bytes 2654208 | tf_op jit(solution)/shard_map/reduce_scatter | solution.py:205
  574.5 25.9 %copy-start.1 = (bf16[512,768]{1,0:T(8,128)(2,1)S(1)}, bf16[512,768]{1,0:T(8,128)(2,1)}, u32[]{:S(2)}) copy-start(bf16[512,768]{1,0:T(8,128)(2,1)} %param.19) | copy-start | bytes 2359300
  574.5 25.9 %copy-start.27 = (f32[512]{0:T(512)S(1)}, f32[512]{0:T(512)}, u32[]{:S(2)}) copy-start(f32[512]{0:T(512)} %copy-done.26) | copy-start | bytes 6148
  574.5 25.9 %copy-start.28 = (f32[768]{0:T(1024)S(1)}, f32[768]{0:T(1024)}, u32[]{:S(2)}) copy-start(f32[768]{0:T(1024)} %param.21) | copy-start | bytes 9220
  574.5 25.9 %copy-start.29 = (f32[768]{0:T(1024)S(1)}, f32[768]{0:T(1024)}, u32[]{:S(2)}) copy-start(f32[768]{0:T(1024)} %param.23) | copy-start | bytes 9220
  574.5 28.3 %copy-start.34 = (f32[512]{0:T(512)S(1)}, f32[512]{0:T(512)}, u32[]{:S(2)}) copy-start(f32[512]{0:T(512)} %copy-done.33) | copy-start | bytes 6148
  574.5 28.4 %copy-start.32 = (f32[512]{0:T(512)S(1)}, f32[512]{0:T(512)}, u32[]{:S(2)}) copy-start(f32[512]{0:T(512)} %copy-done.31) | copy-start | bytes 6148
  574.6 44.3 %copy-start.36 = (f32[768]{0:T(1024)S(1)}, f32[768]{0:T(1024)}, u32[]{:S(2)}) copy-start(f32[768]{0:T(1024)} %param.32) | copy-start | bytes 9220
  574.6 44.3 %copy-start.37 = (f32[768]{0:T(1024)S(1)}, f32[768]{0:T(1024)}, u32[]{:S(2)}) copy-start(f32[768]{0:T(1024)} %param.28) | copy-start | bytes 9220
  576.9 42.0 %copy-start.10 = (bf16[512,768]{1,0:T(8,128)(2,1)S(1)}, bf16[512,768]{1,0:T(8,128)(2,1)}, u32[]{:S(2)}) copy-start(bf16[512,768]{1,0:T(8,128)(2,1)} %param.33) | copy-start | bytes 2359300
  600.4 18.4 %copy-start.3 = (bf16[512,768]{1,0:T(8,128)(2,1)S(1)}, bf16[512,768]{1,0:T(8,128)(2,1)}, u32[]{:S(2)}) copy-start(bf16[512,768]{1,0:T(8,128)(2,1)} %reduce-scatter.16.cloned.1.call-done) | copy-start | bytes 2359300
  600.5 18.4 %copy-start.4 = (bf16[512,768]{1,0:T(8,128)(2,1)S(1)}, bf16[512,768]{1,0:T(8,128)(2,1)}, u32[]{:S(2)}) copy-start(bf16[512,768]{1,0:T(8,128)(2,1)} %reduce-scatter.14.cloned.1.call-done) | copy-start | bytes 2359300
  663.0 237.7 %copy-start.42 = (f32[24]{0:T(128)}, f32[24]{0:T(128)S(1)}, u32[]{:S(2)}) copy-start(f32[24]{0:T(128)S(1)} %dynamic-slice.6) | copy-start | bytes 292
  (7 other events, 7.2 us)
Sparse Core Ops, SparseCore 0:
  13.1 31.2 all-gather.5
  46.0 28.5 all-gather.13
  76.7 41.0 all-gather.9
  119.2 27.2 all-gather.7
  148.6 41.1 all-gather.11
  498.1 39.4 reduce-scatter.15
  540.3 37.9 reduce-scatter.13
  580.9 37.9 reduce-scatter.11
  623.1 62.4 reduce-scatter.21
  689.5 65.8 reduce-scatter.17
  759.9 67.8 reduce-scatter.23
  832.1 68.0 reduce-scatter.19
where the time goes:
time: 919 us; the launch traced here: 908 us
  matrix products  359 us (39%)
  waiting for transfers between devices  251 us (27%)
  blocking collectives  127 us (14%)
  local copies, waits for them, and re-layouts  68.7 us (7%)
  other arithmetic  66.9 us (7%)
  between operations  17.3 us (2%)
  loops' own time  16.5 us (2%)
    unnamed x14, waiting for transfers between devices  95.8 us
    dot_general x4, matrix products, one_block(): jnp.einsum('hqk,qhd->khd', score_grad, query_block, preferred_element_typ...  90.1 us
    dot_general x4, matrix products, one_block(): jnp.einsum('hqk,khd->qhd', score_grad, keys, preferred_element_type=jnp.f...  80.2 us
    reduce_scatter x1, waiting for transfers between devices, body(): lax.psum_scatter(up_grad, 'dp', scatter_dimension=0, tiled=True)  72.4 us
    reduce_scatter x1, waiting for transfers between devices, body(): lax.psum_scatter(qkv_grad, 'dp', scatter_dimension=0, tiled=True)  69.8 us
    unnamed x2, blocking collectives  62.2 us
    dot_general x8, matrix products, masked_scores(): jnp.einsum('qhd,khd->hqk', query_block, keys, preferred_element_type=jnp....  40.4 us
    dynamic_update_slice x8, local copies, waits for them, and re-layouts, attend(): results, logsum = lax.map(one_block, begins)  36 us
  transfers between devices with their start and end apart: 12, of which 5 were waited for; matrix products, arithmetic and copies ran while one was open for 53% of the time, Pallas kernels for 0%

commit v1 on v0

v1 whole, which is shorter than its diff:
```python
import functools

import jax
import jax.numpy as jnp
from jax import lax
from jax.experimental import pallas as pl
from jax.experimental.pallas import tpu as pltpu
from jax.sharding import PartitionSpec as P

HEAD = 64
ROT = 16
HALF = ROT // 2
EPS = 1e-05
NEG = -1e30
SCALE = HEAD ** (-0.5)
WHOLE = 1536
BLOCK = 512
F32 = jnp.float32
BF16 = jnp.bfloat16
VMEM_LIMIT = 56 * 1024 * 1024


def dot(left, right):
    return jnp.dot(left, right, preferred_element_type=F32)


def dot_nt(left, right):
    return lax.dot_general(left, right, (((1,), (1,)), ((), ())), preferred_element_type=F32)


def call(kernel, grid, in_specs, out_specs, out_shape, scratch, name, prefetch=0):
    return pl.pallas_call(
        kernel,
        grid_spec=pltpu.PrefetchScalarGridSpec(
            num_scalar_prefetch=prefetch,
            grid=grid,
            in_specs=in_specs,
            out_specs=out_specs,
            scratch_shapes=scratch,
        ),
        out_shape=out_shape,
        compiler_params=pltpu.CompilerParams(vmem_limit_bytes=VMEM_LIMIT),
        name=name,
    )


def whole_spec(shape):
    return pl.BlockSpec(shape, lambda *_: (0,) * len(shape))


def standardize(block):
    values = block.astype(F32)
    center = values - jnp.mean(values, axis=0, keepdims=True)
    spread = jnp.mean(center * center, axis=0, keepdims=True)
    return center * lax.rsqrt(spread + EPS)


def project_kernel(place, x_ref, w_ref, b_ref, gain_ref, bias_ref, cos_ref, sin_ref, out_ref, wt):
    @pl.when(pl.program_id(0) == 0)
    def _():
        wt[...] = w_ref[...].T

    normed = (standardize(x_ref[0]) * gain_ref[...] + bias_ref[...]).astype(BF16)
    cosine, sine = cos_ref[...], sin_ref[...]
    for head in range(w_ref.shape[1] // (3 * HEAD)):
        base = head * 3 * HEAD
        mixed = dot(wt[base : base + 3 * HEAD, :], normed) + b_ref[base : base + 3 * HEAD, :]
        for part, factor in ((0, SCALE), (HEAD, 1.0)):
            one, two = mixed[part : part + HALF], mixed[part + HALF : part + ROT]
            turned = jnp.concatenate(
                [one * cosine - two * sine, two * cosine + one * sine, mixed[part + ROT : part + HEAD]],
                axis=0,
            )
            out_ref[base + part : base + part + HEAD, :] = (turned * factor).astype(BF16)
        out_ref[base + 2 * HEAD : base + 3 * HEAD, :] = mixed[2 * HEAD :].astype(BF16)


def project(place, x_all, w, b, gain, bias, cosine, sine):
    parts, width, slab = x_all.shape
    cols = w.shape[1]
    return call(
        project_kernel,
        (parts,),
        [
            pl.BlockSpec((1, width, slab), lambda s, t: (s ^ t[0], 0, 0)),
            whole_spec(w.shape),
            whole_spec(b.shape),
            whole_spec(gain.shape),
            whole_spec(bias.shape),
            pl.BlockSpec((HALF, slab), lambda s, t: (0, s)),
            pl.BlockSpec((HALF, slab), lambda s, t: (0, s)),
        ],
        pl.BlockSpec((cols, slab), lambda s, t: (0, s)),
        jax.ShapeDtypeStruct((cols, parts * slab), BF16),
        [pltpu.VMEM((cols, width), BF16)],
        "project",
        prefetch=1,
    )(place, x_all, w, b, gain, bias, cosine, sine)


def masked(scores, first_key, first_query, starts):
    diagonal = first_key + scores.shape[0] > first_query
    ragged = first_query + scores.shape[1] > WHOLE
    if not (diagonal or ragged):
        return scores
    key = first_key + lax.broadcasted_iota(jnp.int32, scores.shape, 0)
    allowed = key >= starts
    if diagonal:
        allowed &= key <= first_query + lax.broadcasted_iota(jnp.int32, scores.shape, 1)
    return jnp.where(allowed, scores, NEG)


def attend_kernel(start_ref, qkv_ref, out_ref, lse_ref, keys, held):
    rows = qkv_ref.shape[1]
    block = min(BLOCK, rows)
    keys[...] = qkv_ref[HEAD : 2 * HEAD, :].T
    for begin in range(0, rows, block):
        here = slice(begin, begin + block)
        queries, starts = qkv_ref[0:HEAD, here], start_ref[0:1, here]
        top = jnp.full((1, block), NEG, F32)
        for first in range(0, begin + block, block):
            scores = masked(dot(keys[first : first + block, :], queries), first, begin, starts)
            held[first : first + block, :] = scores
            top = jnp.maximum(top, jnp.max(scores, axis=0, keepdims=True))
        total = jnp.zeros((1, block), F32)
        result = jnp.zeros((HEAD, block), F32)
        for first in range(0, begin + block, block):
            expo = jnp.exp(held[first : first + block, :] - top)
            total += jnp.sum(expo, axis=0, keepdims=True)
            result += dot(qkv_ref[2 * HEAD : 3 * HEAD, first : first + block], expo.astype(BF16))
        out_ref[:, here] = (result / total).astype(BF16)
        lse_ref[0, 0:1, here] = top + jnp.log(total)


def attend(starts, qkv):
    rows = qkv.shape[1]
    heads = qkv.shape[0] // (3 * HEAD)
    return call(
        attend_kernel,
        (heads,),
        [whole_spec(starts.shape), pl.BlockSpec((3 * HEAD, rows), lambda h: (h, 0))],
        [pl.BlockSpec((HEAD, rows), lambda h: (h, 0)), pl.BlockSpec((1, 1, rows), lambda h: (h, 0, 0))],
        [jax.ShapeDtypeStruct((heads * HEAD, rows), BF16), jax.ShapeDtypeStruct((heads, 1, rows), F32)],
        [pltpu.VMEM((rows, HEAD), BF16), pltpu.VMEM((rows, min(BLOCK, rows)), F32)],
        "attend",
    )(starts, qkv)


def attend_back_kernel(
    start_ref, cos_ref, sin_ref, qkv_ref, grad_ref, out_ref, lse_ref, mixed_ref, keys, values, key_sum, value_sum
):
    rows = qkv_ref.shape[1]
    block = min(BLOCK, rows)
    keys[...] = qkv_ref[HEAD : 2 * HEAD, :].T
    values[...] = qkv_ref[2 * HEAD : 3 * HEAD, :].T
    key_sum[...] = jnp.zeros_like(key_sum)
    value_sum[...] = jnp.zeros_like(value_sum)

    def put_unrotated(base, here, grads):
        cosine, sine = cos_ref[:, here], sin_ref[:, here]
        one, two = grads[0:HALF, :], grads[HALF:ROT, :]
        turned = jnp.concatenate(
            [one * cosine + two * sine, two * cosine - one * sine, grads[ROT:, :]], axis=0
        )
        mixed_ref[base : base + HEAD, here] = turned.astype(BF16)

    for begin in range(0, rows, block):
        here = slice(begin, begin + block)
        queries, grads, starts = qkv_ref[0:HEAD, here], grad_ref[:, here], start_ref[0:1, here]
        lse = lse_ref[0, 0:1, here]
        inner = jnp.sum(grads.astype(F32) * out_ref[:, here].astype(F32), axis=0, keepdims=True)
        query_rows, grad_rows = queries.T, grads.T
        query_sum = jnp.zeros((HEAD, block), F32)
        for first in range(0, begin + block, block):
            there = slice(first, first + block)
            scores = masked(dot(keys[there, :], queries), first, begin, starts)
            probs = jnp.exp(scores - lse)
            score_grads = (probs * (dot(values[there, :], grads) - inner)).astype(BF16)
            query_sum += dot(qkv_ref[HEAD : 2 * HEAD, there], score_grads)
            key_sum[there, :] += dot(score_grads, query_rows)
            value_sum[there, :] += dot(probs.astype(BF16), grad_rows)
        put_unrotated(0, here, query_sum * SCALE)
    put_unrotated(HEAD, slice(0, rows), key_sum[...].T)
    mixed_ref[2 * HEAD : 3 * HEAD, :] = value_sum[...].T.astype(BF16)


def attend_back(starts, cosine, sine, qkv, grads, out, lse):
    rows = qkv.shape[1]
    heads = qkv.shape[0] // (3 * HEAD)
    head_block = pl.BlockSpec((HEAD, rows), lambda h: (h, 0))
    three_block = pl.BlockSpec((3 * HEAD, rows), lambda h: (h, 0))
    return call(
        attend_back_kernel,
        (heads,),
        [
            whole_spec(starts.shape),
            whole_spec(cosine.shape),
            whole_spec(sine.shape),
            three_block,
            head_block,
            head_block,
            pl.BlockSpec((1, 1, rows), lambda h: (h, 0, 0)),
        ],
        three_block,
        jax.ShapeDtypeStruct((heads * 3 * HEAD, rows), BF16),
        [pltpu.VMEM((rows, HEAD), BF16)] * 2 + [pltpu.VMEM((rows, HEAD), F32)] * 2,
        "attend_back",
    )(starts, cosine, sine, qkv, grads, out, lse)


def feed_kernel(
    place,
    x_ref,
    dy_ref,
    att_ref,
    up_ref,
    down_ref,
    dense_ref,
    b_ref,
    gain_ref,
    bias_ref,
    branch_ref,
    normed_ref,
    att_grad_ref,
    weights_ref,
    vector_ref,
    up_t,
    down_t,
    dense_t,
    active,
    hidden_grad,
    sums,
    vectors,
):
    step = pl.program_id(0)
    width, hidden_count = up_ref.shape
    dense_count = dense_ref.shape[1]

    @pl.when(step == 0)
    def _():
        up_t[...] = up_ref[...].T
        down_t[...] = down_ref[...].T
        dense_t[...] = dense_ref[...].T
        sums[...] = jnp.zeros_like(sums)
        vectors[...] = jnp.zeros_like(vectors)

    unit = standardize(x_ref[0])
    normed = (unit * gain_ref[...] + bias_ref[...]).astype(BF16)
    dy = dy_ref[0]
    attended = att_ref[...]
    att_grad_ref[...] = dot(dense_t[...], dy).astype(BF16)
    chunk = min(256, hidden_count)
    for first in range(0, hidden_count, chunk):
        units = slice(first, first + chunk)
        hidden = dot(up_t[units, :], normed) + b_ref[units, :]
        chance = 0.5 + 0.5 * lax.erf(hidden * (0.5**0.5))
        density = jnp.exp(hidden * hidden * -0.5) * (hidden * 0.3989422804014327)
        now = (hidden * chance).astype(BF16)
        back = (dot(down_t[units, :], dy) * (chance + density)).astype(BF16)
        active[units, :] = now
        hidden_grad[units, :] = back
        sums[:, units] += dot_nt(normed, back)
        sums[:, hidden_count + first : hidden_count + first + chunk] += dot_nt(dy, now)
        vectors[units, 3:4] += jnp.sum(back.astype(F32), axis=1, keepdims=True)
    sums[:, 2 * hidden_count :] += dot_nt(dy, attended)
    branch_ref[0] = (dot(dense_ref[...], attended) + dot(down_ref[...], active[...])).astype(BF16)
    normed_grad = dot(up_ref[...], hidden_grad[...])
    normed_ref[0] = normed_grad * gain_ref[...]
    vectors[:, 0:1] += jnp.sum(normed_grad * unit, axis=1, keepdims=True)
    vectors[:, 1:2] += jnp.sum(normed_grad, axis=1, keepdims=True)
    vectors[:, 2:3] += jnp.sum(dy.astype(F32), axis=1, keepdims=True)

    @pl.when(step == pl.num_programs(0) - 1)
    def _():
        weights_ref[...] = sums[...].astype(BF16)
        vector_ref[...] = vectors[...]


def feed(place, x_all, dy_all, attended, up, down, dense, b, gain, bias):
    parts, width, slab = x_all.shape
    hidden_count, dense_count = up.shape[1], dense.shape[1]
    grad_cols = 2 * hidden_count + dense_count
    slab_block = pl.BlockSpec((1, width, slab), lambda s, t: (s ^ t[0], 0, 0))
    out_block = pl.BlockSpec((1, width, slab), lambda s, t: (s, 0, 0))
    rows_block = pl.BlockSpec((dense_count, slab), lambda s, t: (0, s))
    return call(
        feed_kernel,
        (parts,),
        [
            slab_block,
            slab_block,
            rows_block,
            whole_spec(up.shape),
            whole_spec(down.shape),
            whole_spec(dense.shape),
            whole_spec(b.shape),
            whole_spec(gain.shape),
            whole_spec(bias.shape),
        ],
        [out_block, out_block, rows_block, whole_spec((width, grad_cols)), whole_spec((hidden_count, 4))],
        [
            jax.ShapeDtypeStruct((parts, width, slab), BF16),
            jax.ShapeDtypeStruct((parts, width, slab), F32),
            jax.ShapeDtypeStruct((dense_count, parts * slab), BF16),
            jax.ShapeDtypeStruct((width, grad_cols), BF16),
            jax.ShapeDtypeStruct((hidden_count, 4), F32),
        ],
        [
            pltpu.VMEM((hidden_count, width), BF16),
            pltpu.VMEM((hidden_count, width), BF16),
            pltpu.VMEM((dense_count, width), BF16),
            pltpu.VMEM((hidden_count, slab), BF16),
            pltpu.VMEM((hidden_count, slab), BF16),
            pltpu.VMEM((width, grad_cols), F32),
            pltpu.VMEM((hidden_count, 4), F32),
        ],
        "feed",
        prefetch=1,
    )(place, x_all, dy_all, attended, up, down, dense, b, gain, bias)


def project_back_kernel(
    place, x_ref, mixed_ref, part_ref, w_ref, gain_ref, bias_ref, unit_ref, weights_ref, vector_ref, count_ref, sums, vectors, counts
):
    step = pl.program_id(0)

    @pl.when(step == 0)
    def _():
        sums[...] = jnp.zeros_like(sums)
        vectors[...] = jnp.zeros_like(vectors)
        counts[...] = jnp.zeros_like(counts)

    unit = standardize(x_ref[0])
    normed = (unit * gain_ref[...] + bias_ref[...]).astype(BF16)
    mixed = mixed_ref[...]
    sums[...] += dot_nt(normed, mixed)
    counts[...] += jnp.sum(mixed.astype(F32), axis=1, keepdims=True)
    normed_grad = dot(w_ref[...], mixed)
    unit_ref[0] = (part_ref[0] + normed_grad * gain_ref[...]).astype(BF16)
    vectors[:, 0:1] += jnp.sum(normed_grad * unit, axis=1, keepdims=True)
    vectors[:, 1:2] += jnp.sum(normed_grad, axis=1, keepdims=True)

    @pl.when(step == pl.num_programs(0) - 1)
    def _():
        weights_ref[...] = sums[...].astype(BF16)
        vector_ref[...] = vectors[...]
        count_ref[...] = counts[...]


def project_back(place, x_all, mixed, part, w, gain, bias):
    parts, width, slab = x_all.shape
    cols = w.shape[1]
    slab_block = pl.BlockSpec((1, width, slab), lambda s, t: (s ^ t[0], 0, 0))
    out_block = pl.BlockSpec((1, width, slab), lambda s, t: (s, 0, 0))
    return call(
        project_back_kernel,
        (parts,),
        [
            slab_block,
            pl.BlockSpec((cols, slab), lambda s, t: (0, s)),
            out_block,
            whole_spec(w.shape),
            whole_spec(gain.shape),
            whole_spec(bias.shape),
        ],
        [out_block, whole_spec((width, cols)), whole_spec((width, 2)), whole_spec((cols, 1))],
        [
            jax.ShapeDtypeStruct((parts, width, slab), BF16),
            jax.ShapeDtypeStruct((width, cols), BF16),
            jax.ShapeDtypeStruct((width, 2), F32),
            jax.ShapeDtypeStruct((cols, 1), F32),
        ],
        [pltpu.VMEM((width, cols), F32), pltpu.VMEM((width, 2), F32), pltpu.VMEM((cols, 1), F32)],
        "project_back",
        prefetch=1,
    )(place, x_all, mixed, part, w, gain, bias)


def swap(value, bit):
    count = lax.axis_size("tensor")
    return lax.ppermute(value, "tensor", [(i, i ^ bit) for i in range(count)])


def gather_group(own):
    far = swap(own, 2)
    near = swap(own, 1)
    return jnp.stack([own, near, far, swap(far, 1)])


def scatter_group(slabs, mine):
    def pick(r):
        return lax.dynamic_index_in_dim(slabs, mine ^ r, 0, keepdims=False)

    far = pick(2).astype(F32) + swap(pick(3), 1).astype(F32)
    near = pick(0).astype(F32) + swap(pick(1), 1).astype(F32)
    return near + swap(far.astype(BF16), 2).astype(F32)


def body(
    tokens,
    segment_ids,
    ln1_gain,
    ln1_bias,
    ln2_gain,
    ln2_bias,
    w_qkv,
    b_qkv,
    w_dense,
    b_dense,
    w_fc1,
    b_fc1,
    w_fc2,
    b_fc2,
    cotangent,
):
    group_rows = segment_ids.shape[0]
    width = tokens.shape[1]
    own_width = w_qkv.shape[0]
    mine = lax.axis_index("tensor").astype(jnp.int32)
    place = mine.reshape(1)

    x_all = gather_group(tokens.T)
    qkv_full = lax.all_gather(w_qkv, "dp", axis=0, tiled=True)
    dense_full = lax.all_gather(w_dense, "dp", axis=0, tiled=True)
    dy_all = gather_group(cotangent.T)
    up_full = lax.all_gather(w_fc1, "dp", axis=0, tiled=True)
    down_full = lax.all_gather(w_fc2, "dp", axis=0, tiled=True)

    row = jnp.arange(group_rows, dtype=jnp.int32)
    padding = segment_ids != segment_ids[0]
    length = jnp.sum(jnp.where(padding, 0, 1))
    starts = jnp.where(padding, length, 0)
    inverse = 10000.0 ** (-jnp.arange(0, ROT, 2, dtype=F32) / ROT)
    angles = inverse[:, None] * (row - starts).astype(F32)[None, :]
    cosine, sine = jnp.cos(angles), jnp.sin(angles)
    starts = starts[None, :]

    gain_one, bias_one = ln1_gain[:, None], ln1_bias[:, None]
    gain_two, bias_two = ln2_gain[:, None], ln2_bias[:, None]
    qkv = project(place, x_all, qkv_full, b_qkv[:, None], gain_one, bias_one, cosine, sine)
    attended, lse = attend(starts, qkv)
    branch, part, att_grad, feed_grads, feed_vectors = feed(
        place, x_all, dy_all, attended, up_full, down_full, dense_full, b_fc1[:, None], gain_two, bias_two
    )
    extra = jnp.pad(feed_vectors.astype(BF16), ((0, 0), (0, 124)))
    feed_owned = lax.psum_scatter(
        jnp.concatenate([feed_grads, extra], axis=1), "dp", scatter_dimension=0, tiled=True
    ).astype(F32)
    summed = scatter_group(branch, mine)
    own_input = tokens.astype(F32)
    out = (own_input + summed.T + b_dense + b_fc2).astype(BF16)

    mixed_grad = attend_back(starts, cosine, sine, qkv, att_grad, attended, lse)
    unit_grad, qkv_grad, qkv_vectors, qkv_bias_grad = project_back(
        place, x_all, mixed_grad, part, qkv_full, gain_one, bias_one
    )
    bias_own = qkv_bias_grad.shape[0] // lax.axis_size("dp")
    bias_rows = jnp.pad(qkv_bias_grad.reshape(-1, bias_own), ((0, 0), (0, own_width - bias_own)))
    extra = jnp.concatenate([qkv_vectors, bias_rows.reshape(width, 1)], axis=1)
    extra = jnp.pad(extra.astype(BF16), ((0, 0), (0, 125)))
    qkv_owned = lax.psum_scatter(
        jnp.concatenate([qkv_grad, extra], axis=1), "dp", scatter_dimension=0, tiled=True
    ).astype(F32)
    unit_sum = scatter_group(unit_grad, mine).T

    center = own_input - jnp.mean(own_input, axis=-1, keepdims=True)
    inverse_scale = lax.rsqrt(jnp.mean(center * center, axis=-1, keepdims=True) + EPS)
    unit = center * inverse_scale
    input_grad = cotangent.astype(F32) + inverse_scale * (
        unit_sum
        - jnp.mean(unit_sum, axis=-1, keepdims=True)
        - unit * jnp.mean(unit_sum * unit, axis=-1, keepdims=True)
    )

    cols = w_qkv.shape[1]
    hidden_count = w_fc1.shape[1]
    dense_count = w_dense.shape[1]
    up_end, down_end = hidden_count, 2 * hidden_count
    dense_end = down_end + dense_count
    norms = jnp.concatenate(
        [qkv_owned[:, cols : cols + 2], feed_owned[:, dense_end : dense_end + 2]], axis=1
    )
    norms = norms.T.reshape(4, lax.axis_size("tensor"), -1).transpose(1, 0, 2)
    norms = jnp.sum(lax.all_to_all(norms, "tensor", 0, 0, tiled=True), axis=0)
    bias_grad = lax.dynamic_index_in_dim(
        feed_owned[:, dense_end + 2].reshape(lax.axis_size("tensor"), -1), mine, 0, keepdims=False
    )
    return (
        out,
        input_grad,
        norms[0],
        norms[1],
        norms[2],
        norms[3],
        qkv_owned[:, :cols],
        qkv_owned[:bias_own, cols + 2],
        feed_owned[:, down_end:dense_end],
        bias_grad,
        feed_owned[:, :up_end],
        feed_owned[:, dense_end + 3],
        feed_owned[:, up_end:down_end],
        bias_grad,
    )


def solution(mesh):
    placed = (
        P(("dp", "tensor"), None),
        P("dp"),
        P(),
        P(),
        P(),
        P(),
        P("dp", "tensor"),
        P("tensor"),
        P("dp", "tensor"),
        P(),
        P("dp", "tensor"),
        P("tensor"),
        P("dp", "tensor"),
        P(),
        P(("dp", "tensor"), None),
    )
    return jax.shard_map(
        body,
        mesh=mesh,
        in_specs=placed,
        out_specs=(
            P(("dp", "tensor"), None),
            P(("dp", "tensor"), None),
            P(("dp", "tensor")),
            P(("dp", "tensor")),
            P(("dp", "tensor")),
            P(("dp", "tensor")),
            P("dp", "tensor"),
            P(("tensor", "dp")),
            P("dp", "tensor"),
            P(("dp", "tensor")),
            P("dp", "tensor"),
            P(("tensor", "dp")),
            P("dp", "tensor"),
            P(("dp", "tensor")),
        ),
        check_vma=False,
    )
```

time: 919 us -> 354 us (0.39); the launches traced: 908 us -> 353 us
  matrix products: 359 us -> 0 us
  waiting for transfers between devices: 251 us -> 109 us
  Pallas kernels: 0 us -> 92 us
  blocking collectives: 127 us -> 70.5 us
  local copies, waits for them, and re-layouts: 68.7 us -> 25.6 us
  other arithmetic: 66.9 us -> 31.3 us
  loops' own time: 16.5 us -> 0 us
  starting transfers between devices: 0.95 us -> 10.7 us
    dot_general x40 -> x0, matrix products: 359 us -> none  [the longest x4 90.1 us: one_block(): jnp.einsum('hqk,qhd->khd', score_grad, query_block, preferred_element_typ...]
    unnamed x14 -> x4, waiting for transfers between devices: 95.8 us -> 0.73 us
    pallas_call x0 -> x5, Pallas kernels: none -> 92 us  [the longest x1 30.2 us: feed(): call(feed_kernel, (parts,), [slab_block, slab_block, rows_block, whole_sp...]
    reduce_scatter x5 -> x2, waiting for transfers between devices: 155 us -> 78.5 us  [the longest x1 70.8 us: body(): lax.psum_scatter(jnp.concatenate([feed_grads, extra], axis=1), 'dp', scat...]
    unnamed x2 -> x0, blocking collectives: 62.2 us -> none
    dynamic_update_slice x8 -> x0, local copies, waits for them, and re-layouts: 36 us -> none  [attend(): results, logsum = lax.map(one_block, begins)]
    reduce_sum x10 -> x6, other arithmetic: 39.7 us -> 4.86 us  [the longest x1 1.67 us: body(): jnp.mean(unit_sum * unit, axis=-1, keepdims=True)]
    ppermute x0 -> x12, waiting for transfers between devices: none -> 29.1 us  [swap(): return lax.ppermute(value, 'tensor', [(i, i ^ bit) for i in range(count)])]
  transfers between devices with their start and end apart: 12 -> 17, of which waited for: 5 -> 5; matrix products, arithmetic and copies ran while one was open for 53% -> 14% of each run, Pallas kernels for 0% -> 6%
where the time goes in v1:
time: 354 us; the launch traced here: 353 us
  waiting for transfers between devices  109 us (31%)
  Pallas kernels  92 us (26%)
  blocking collectives  70.5 us (20%)
  other arithmetic  31.3 us (9%)
  local copies, waits for them, and re-layouts  25.6 us (7%)
  between operations  14 us (4%)
  starting transfers between devices  10.7 us (3%)
    reduce_scatter x1, waiting for transfers between devices, body(): lax.psum_scatter(jnp.concatenate([feed_grads, extra], axis=1), 'dp', scat...  70.8 us
    all_gather x1, blocking collectives, body(): qkv_full = lax.all_gather(w_qkv, 'dp', axis=0, tiled=True)  36.3 us
    all_gather x1, blocking collectives, body(): dense_full = lax.all_gather(w_dense, 'dp', axis=0, tiled=True)  34.2 us
    pallas_call x1, Pallas kernels, feed(): call(feed_kernel, (parts,), [slab_block, slab_block, rows_block, whole_sp...  30.2 us
    ppermute x12, waiting for transfers between devices, swap(): return lax.ppermute(value, 'tensor', [(i, i ^ bit) for i in range(count)])  29.1 us
    pallas_call x1, Pallas kernels, attend_back(): call(attend_back_kernel, (heads,), [whole_spec(starts.shape), whole_spec(...  26.5 us
    pallas_call x1, Pallas kernels, attend(): call(attend_kernel, (heads,), [whole_spec(starts.shape), pl.BlockSpec((3...  14.3 us
    pallas_call x1, Pallas kernels, project_back(): call(project_back_kernel, (parts,), [slab_block, pl.BlockSpec((cols, slab...  13.1 us
  transfers between devices with their start and end apart: 17, of which 5 were waited for; matrix products, arithmetic and copies ran while one was open for 14% of the time, Pallas kernels for 6%

profile of v1, /device:TPU:0, one launch (start us, length us, event | category | flops | bytes accessed | tf_op | source)
XLA Modules:
  0.0 353.0 jit_solution(12574835917553322589)
XLA Ops:
  7.2 0.7 all-gather.3.cloned.1.call-update
  8.0 1.4 copy.89
  9.4 3.0 collective-permute-start.1
  12.5 0.3 copy.91
  12.8 0.2 collective-permute-start.4
  12.9 0.5 collective-permute-start.3
  13.5 0.5 slice.42
  14.0 1.3 select_reduce_fusion
  15.3 34.2 %all_gather.15.dense_ref = bf16[768,192]{1,0:T(8,128)(2,1)} all-gather(bf16[96,192]{1,0:T(8,128)(2,1)S(1)} %copy-done.6), channel_id=1, replica_groups=mesh['dp'=8,'tensor'=4] {'dp'}, dimensions={0}, use_global_device_ids=true | all-gather | bytes 331776 | tf_op jit(solution)/shard_map/all_gather | solution.py:424
  49.5 36.3 %all_gather.12.w_ref = bf16[768,576]{1,0:T(8,128)(2,1)} all-gather(bf16[96,576]{1,0:T(8,128)(2,1)S(1)} %copy-done.5), channel_id=1, replica_groups=mesh['dp'=8,'tensor'=4] {'dp'}, dimensions={0}, use_global_device_ids=true | all-gather | bytes 995328 | tf_op jit(solution)/shard_map/all_gather | solution.py:423
  85.8 1.3 subtract_convert_fusion
  87.1 0.5 collective-permute-start.5
  87.6 0.9 broadcast_in_dim.54.gain_ref
  88.5 1.0 broadcast_in_dim.55.bias_ref
  89.5 0.9 broadcast_in_dim.53.b_ref
  90.3 0.9 broadcast_in_dim.56.b_ref
  91.3 0.9 broadcast_in_dim.57.gain_ref
  92.2 0.9 broadcast_in_dim.58.bias_ref
  93.1 1.0 multiply_sine_fusion
  94.1 3.2 pad_maximum_fusion.x_ref
  97.3 7.9 %project.1.qkv_ref = bf16[576,2048]{1,0:T(8,128)(2,1)} custom-call(s32[1]{0:T(128)} %bitcast.place, bf16[4,768,512]{2,1,0:T(8,128)(2,1)} %pad_maximum_fusion.x_ref, bf16[768,576]{1,0:T(8,128)(2,1)} %all_gather.12.w_ref, f32[576,1]{1,0:T(8,128)} %broadcast_in_dim.53.b_ref, f32[768,1]{1,0:T(8,128)} %broadcast_in_dim.54.gain_ref, ...), custom_call_target="tpu_custom_call" | custom-call | tf_op jit(solution)/shard_map/project/pallas_call | solution.py:81
  105.2 14.3 %attend.1 = (bf16[192,2048]{1,0:T(8,128)(2,1)}, f32[3,1,2048]{2,1,0:T(1,128)}) custom-call(s32[1,2048]{1,0:T(1,128)} %bitcast.71, bf16[576,2048]{1,0:T(8,128)(2,1)} %project.1.qkv_ref), custom_call_target="tpu_custom_call" | custom-call | tf_op jit(solution)/shard_map/attend/pallas_call | solution.py:138
  119.5 2.8 pad_maximum_fusion.1.dy_ref
  122.4 30.2 %feed.1 = (bf16[4,768,512]{2,1,0:T(8,128)(2,1)}, f32[4,768,512]{2,1,0:T(8,128)}, bf16[192,2048]{1,0:T(8,128)(2,1)}, bf16[768,1728]{1,0:T(8,128)(2,1)}, f32[768,4]{1,0:T(8,128)}) custom-call(s32[1]{0:T(128)} %bitcast.place, bf16[4,768,512]{2,1,0:T(8,128)(2,1)} %pad_maximum_fusion.x_ref, bf16[4,768,512]{2,1,0:T(8,128)(2,1)} %pad_maximum_fusion.1.dy_ref, ...), custom_call_target="tpu_custom_call" | custom-call | tf_op jit(solution)/shard_map/feed/pallas_call | solution.py:286
  152.6 26.5 %attend_back.1.mixed_ref = bf16[576,2048]{1,0:T(8,128)(2,1)} custom-call(s32[1,2048]{1,0:T(1,128)} %bitcast.72, f32[8,2048]{1,0:T(8,128)} %get-tuple-element.119.cos_ref, f32[8,2048]{1,0:T(8,128)} %get-tuple-element.118.sin_ref, bf16[576,2048]{1,0:T(8,128)(2,1)} %project.1.qkv_ref, bf16[192,2048]{1,0:T(8,128)(2,1)} %get-tuple-element.27.grad_ref, ...), custom_call_target="tpu_custom_call" | custom-call | tf_op jit(solution)/shard_map/attend_back/pallas_call | solution.py:192
  179.0 13.1 %project_back.1 = (bf16[4,768,512]{2,1,0:T(8,128)(2,1)}, bf16[768,576]{1,0:T(8,128)(2,1)}, f32[768,2]{1,0:T(8,128)}, f32[576,1]{1,0:T(8,128)}) custom-call(s32[1]{0:T(128)} %bitcast.place, bf16[4,768,512]{2,1,0:T(8,128)(2,1)} %pad_maximum_fusion.x_ref, bf16[576,2048]{1,0:T(8,128)(2,1)} %attend_back.1.mixed_ref, f32[4,768,512]{2,1,0:T(8,128)} %get-tuple-element.29.part_ref, ...), custom_call_target="tpu_custom_call" | custom-call | tf_op jit(solution)/shard_map/project_back/pallas_call | solution.py:355
  192.2 1.2 convert_reduce_fusion.1
  193.5 0.3 reshape.88
  193.8 1.0 convert.14
  195.0 1.2 pad_maximum_fusion.2
  196.2 0.3 reduce-scatter.5.cloned.1.call-start
  196.6 3.7 %fusion.1 = bf16[768,1856]{1,0:T(8,128)(2,1)} fusion(bf16[768,4]{1,0:T(8,128)(2,1)S(1)} %convert_element_type.97, bf16[768,1728]{1,0:T(8,128)(2,1)} %get-tuple-element.34), kind=kLoop, calls=%fused_computation.4 | loop fusion | flops 8552448 | bytes 5511168 | tf_op jit(solution)/shard_map/concatenate | solution.py:447
  200.3 2.6 dynamic-slice_bitcast_fusion.1
  202.9 2.4 dynamic-slice_bitcast_fusion.3
  205.3 0.5 collective-permute-start.7
  206.0 2.2 fusion.14
  208.3 1.2 collective-permute-start.11
  209.5 0.3 fusion.10
  209.7 0.3 collective-permute-start.6
  210.0 2.3 fusion.16
  212.3 0.8 collective-permute-start.8
  213.1 15.7 %collective-permute-done.11 = bf16[768,512]{1,0:T(8,128)(2,1)S(1)} collective-permute-done((bf16[768,512]{1,0:T(8,128)(2,1)}, bf16[768,512]{1,0:T(8,128)(2,1)S(1)}, u32[]{:S(2)}, u32[]{:S(2)}) %collective-permute-start.11) | collective-permute-done | bytes 786464 | tf_op jit(solution)/shard_map/ppermute | solution.py:381
  228.8 1.5 fusion.21
  230.3 1.7 fusion.6
  232.0 13.4 %collective-permute-done.8 = bf16[768,512]{1,0:T(8,128)(2,1)} collective-permute-done((bf16[768,512]{1,0:T(8,128)(2,1)}, bf16[768,512]{1,0:T(8,128)(2,1)}, u32[]{:S(2)}, u32[]{:S(2)}) %collective-permute-start.8) | collective-permute-done | bytes 786464 | tf_op jit(solution)/shard_map/ppermute | solution.py:381
  245.4 4.4 %fusion.9 = (f32[512,768]{0,1:T(8,128)}, bf16[512,768]{0,1:T(8,128)(2,1)}) fusion(bf16[512,768]{0,1:T(8,128)(2,1)S(1)} %copy.89, bf16[512,768]{0,1:T(8,128)(2,1)S(1)} %copy.91, f32[512]{0:T(512)S(1)} %get-tuple-element.126, f32[512]{0:T(512)S(1)} %get-tuple-element.127, f32[512]{0:T(512)S(1)} %add_rsqrt_fusion, f32[512]{0:T(512)S(1)} %broadcast_multiply_fusion.2, ...), kind=kLoop, calls=%fused_computation.15 | loop fusion | flops 9043968 | bytes 8665092 | tf_op jit(solution)/shard_map/add | solution.py:469
  249.8 3.1 copy.107
  252.9 1.2 copy.106
  254.1 7.7 %reduce-scatter.3.cloned.1.call-done = bf16[96,704]{1,0:T(8,128)(2,1)} async-done(((bf16[768,704]{1,0:T(8,128)(2,1)}), bf16[96,704]{1,0:T(8,128)(2,1)}) %reduce-scatter.3.cloned.1.call-update) | async-done | bytes 135184 | tf_op jit(solution)/shard_map/reduce_scatter | solution.py:461
  261.8 0.8 slice.56
  262.6 0.9 convert_element_type.96
  263.6 1.6 slice.58
  265.2 0.7 slice_reduce_fusion.2
  265.9 70.8 %reduce-scatter.5.cloned.1.call-done = bf16[96,1856]{1,0:T(8,128)(2,1)} async-done(((bf16[768,1856]{1,0:T(8,128)(2,1)}), bf16[96,1856]{1,0:T(8,128)(2,1)}) %reduce-scatter.5.cloned.1.call-update) | async-done | bytes 356368 | tf_op jit(solution)/shard_map/reduce_scatter | solution.py:446
  336.7 0.9 slice.57
  337.8 0.6 copy.104
  338.4 3.2 all-to-all-start
  341.6 1.0 convert_element_type.98
  342.7 0.7 slice_reduce_fusion
  343.5 0.9 fusion.24
  344.3 0.6 slice.60
  345.0 0.5 all-to-all-done
  345.4 0.5 slice_bitcast_fusion
  346.0 0.5 copy.118
  (72 shorter events, 1.2 us)
Async XLA Ops:
  7.2 5.3 %copy-start.3 = (bf16[512,768]{1,0:T(8,128)(2,1)S(1)}, bf16[512,768]{1,0:T(8,128)(2,1)}, u32[]{:S(2)}) copy-start(bf16[512,768]{1,0:T(8,128)(2,1)} %param.29) | copy-start | bytes 2359300
  7.2 115.2 %all-gather.3.cloned.1.call-start = ((), (), s32[]{:S(2)}) async-start(), calls=%async_computation.3 | async-start | bytes 1327104 | tf_op jit(solution)/shard_map/all_gather | solution.py:426
  7.9 5.6 %copy-start.7 = (s32[2048]{0:T(1024)S(1)}, s32[2048]{0:T(1024)}, u32[]{:S(2)}) copy-start(s32[2048]{0:T(1024)} %param.16) | copy-start | bytes 24580
  7.9 7.4 %copy-start.6 = (bf16[96,192]{1,0:T(8,128)(2,1)S(1)}, bf16[96,192]{1,0:T(8,128)(2,1)}, u32[]{:S(2)}) copy-start(bf16[96,192]{1,0:T(8,128)(2,1)} %param.23) | copy-start | bytes 110596
  7.9 41.5 %copy-start.5 = (bf16[96,576]{1,0:T(8,128)(2,1)S(1)}, bf16[96,576]{1,0:T(8,128)(2,1)}, u32[]{:S(2)}) copy-start(bf16[96,576]{1,0:T(8,128)(2,1)} %param.21) | copy-start | bytes 331780
  8.0 114.4 %all-gather.5.cloned.1.call-start = ((), (), s32[]{:S(2)}) async-start(), calls=%async_computation.4 | async-start | bytes 1327104 | tf_op jit(solution)/shard_map/all_gather | solution.py:427
  9.4 78.2 %copy-start.8 = (f32[768]{0:T(1024)S(1)}, f32[768]{0:T(1024)}, u32[]{:S(2)}) copy-start(f32[768]{0:T(1024)} %param.17) | copy-start | bytes 9220
  9.4 79.1 %copy-start.9 = (f32[768]{0:T(1024)S(1)}, f32[768]{0:T(1024)}, u32[]{:S(2)}) copy-start(f32[768]{0:T(1024)} %param.18) | copy-start | bytes 9220
  9.4 76.4 %collective-permute-start.1 = (bf16[768,512]{1,0:T(8,128)(2,1)S(1)}, bf16[768,512]{1,0:T(8,128)(2,1)}, u32[]{:S(2)}, u32[]{:S(2)}) collective-permute-start(bf16[768,512]{1,0:T(8,128)(2,1)S(1)} %bitcast.63), channel_id=1, source_target_pairs={{0,2},{1,3},{2,0},{3,1},{4,6},{5,7},{6,4},{7,5},{8,10},{9,11},{10,... | collective-permute-start | bytes 2359304 | tf_op jit(solution)/shard_map/ppermute | solution.py:381
  12.5 81.6 %collective-permute-start = (bf16[768,512]{1,0:T(8,128)(2,1)S(1)}, bf16[768,512]{1,0:T(8,128)(2,1)}, u32[]{:S(2)}, u32[]{:S(2)}) collective-permute-start(bf16[768,512]{1,0:T(8,128)(2,1)S(1)} %bitcast.64), channel_id=1, source_target_pairs={{0,1},{1,0},{2,3},{3,2},{4,5},{5,4},{6,7},{7,6},{8,9},{9,8},{10,11... | collective-permute-start | bytes 2359304 | tf_op jit(solution)/shard_map/ppermute | solution.py:381
  12.8 76.7 %copy-start.10 = (f32[576]{0:T(1024)S(1)}, f32[576]{0:T(1024)}, u32[]{:S(2)}) copy-start(f32[576]{0:T(1024)} %param.22) | copy-start | bytes 6916
  12.8 77.6 %copy-start.11 = (f32[768]{0:T(1024)S(1)}, f32[768]{0:T(1024)}, u32[]{:S(2)}) copy-start(f32[768]{0:T(1024)} %param.26) | copy-start | bytes 9220
  12.8 74.3 %collective-permute-start.4 = (bf16[768,512]{1,0:T(8,128)(2,1)S(1)}, bf16[768,512]{1,0:T(8,128)(2,1)S(1)}, u32[]{:S(2)}, u32[]{:S(2)}) collective-permute-start(bf16[768,512]{1,0:T(8,128)(2,1)S(1)} %bitcast.66), channel_id=1, source_target_pairs={{0,2},{1,3},{2,0},{3,1},{4,6},{5,7},{6,4},{7,5},{8,10},{9,11},{10,... | collective-permute-start | bytes 2359304 | tf_op jit(solution)/shard_map/ppermute | solution.py:381
  12.9 106.6 %collective-permute-start.3 = (bf16[768,512]{1,0:T(8,128)(2,1)S(1)}, bf16[768,512]{1,0:T(8,128)(2,1)S(1)}, u32[]{:S(2)}, u32[]{:S(2)}) collective-permute-start(bf16[768,512]{1,0:T(8,128)(2,1)S(1)} %bitcast.67), channel_id=1, source_target_pairs={{0,1},{1,0},{2,3},{3,2},{4,5},{5,4},{6,7},{7,6},{8,9},{9,8},{10,11... | collective-permute-start | bytes 2359304 | tf_op jit(solution)/shard_map/ppermute | solution.py:381
  13.5 77.8 %copy-start.12 = (f32[768]{0:T(1024)S(1)}, f32[768]{0:T(1024)}, u32[]{:S(2)}) copy-start(f32[768]{0:T(1024)} %param.19) | copy-start | bytes 9220
  13.5 248.3 %reduce-scatter.3.cloned.1.call-start = ((), (), s32[]{:S(2)}) async-start(), calls=%async_computation.5 | async-start | bytes 1327104 | tf_op jit(solution)/shard_map/reduce_scatter | solution.py:461
  49.5 42.7 %copy-start.13 = (f32[768]{0:T(1024)S(1)}, f32[768]{0:T(1024)}, u32[]{:S(2)}) copy-start(f32[768]{0:T(1024)} %param.20) | copy-start | bytes 9220
  85.8 8.3 %collective-permute-start.2 = (bf16[768,512]{1,0:T(8,128)(2,1)}, bf16[768,512]{1,0:T(8,128)(2,1)}, u32[]{:S(2)}, u32[]{:S(2)}) collective-permute-start(bf16[768,512]{1,0:T(8,128)(2,1)} %collective-permute-done.1), channel_id=1, source_target_pairs={{0,1},{1,0},{2,3},{3,2},{4,5},{5,4},{6,7},{7,6},{8,9},{9,8},{10,11... | collective-permute-start | bytes 2359304 | tf_op jit(solution)/shard_map/ppermute | solution.py:381
  87.1 32.5 %collective-permute-start.5 = (bf16[768,512]{1,0:T(8,128)(2,1)S(1)}, bf16[768,512]{1,0:T(8,128)(2,1)}, u32[]{:S(2)}, u32[]{:S(2)}) collective-permute-start(bf16[768,512]{1,0:T(8,128)(2,1)S(1)} %collective-permute-done.4), channel_id=1, source_target_pairs={{0,1},{1,0},{2,3},{3,2},{4,5},{5,4},{6,7},{7,6},{8,9},{9,8},{10,11... | collective-permute-start | bytes 2359304 | tf_op jit(solution)/shard_map/ppermute | solution.py:381
  192.1 2.8 copy-start.2
  195.0 1.6 copy-start.4
  196.2 140.5 %reduce-scatter.5.cloned.1.call-start = ((), (), s32[]{:S(2)}) async-start(), calls=%async_computation.6 | async-start | bytes 3317760 | tf_op jit(solution)/shard_map/reduce_scatter | solution.py:446
  202.9 3.1 collective-permute-start.10
  205.3 4.7 %collective-permute-start.7 = (bf16[768,512]{1,0:T(8,128)(2,1)S(1)}, bf16[768,512]{1,0:T(8,128)(2,1)S(1)}, u32[]{:S(2)}, u32[]{:S(2)}) collective-permute-start(bf16[768,512]{1,0:T(8,128)(2,1)S(1)} %get-tuple-element.113), channel_id=1, source_target_pairs={{0,1},{1,0},{2,3},{3,2},{4,5},{5,4},{6,7},{7,6},{8,9},{9,8},{10,11... | collective-permute-start | bytes 2359304 | tf_op jit(solution)/shard_map/ppermute | solution.py:381
  206.0 7.1 %collective-permute-start.9 = (bf16[768,512]{1,0:T(8,128)(2,1)}, bf16[768,512]{1,0:T(8,128)(2,1)S(1)}, u32[]{:S(2)}, u32[]{:S(2)}) collective-permute-start(bf16[768,512]{1,0:T(8,128)(2,1)} %get-tuple-element.110), channel_id=1, source_target_pairs={{0,1},{1,0},{2,3},{3,2},{4,5},{5,4},{6,7},{7,6},{8,9},{9,8},{10,11... | collective-permute-start | bytes 2359304 | tf_op jit(solution)/shard_map/ppermute | solution.py:381
  208.3 20.5 %collective-permute-start.11 = (bf16[768,512]{1,0:T(8,128)(2,1)}, bf16[768,512]{1,0:T(8,128)(2,1)S(1)}, u32[]{:S(2)}, u32[]{:S(2)}) collective-permute-start(bf16[768,512]{1,0:T(8,128)(2,1)} %fusion.14), channel_id=1, source_target_pairs={{0,2},{1,3},{2,0},{3,1},{4,6},{5,7},{6,4},{7,5},{8,10},{9,11},{10,... | collective-permute-start | bytes 2359304 | tf_op jit(solution)/shard_map/ppermute | solution.py:381
  209.7 22.2 %collective-permute-start.6 = (bf16[768,512]{1,0:T(8,128)(2,1)}, bf16[768,512]{1,0:T(8,128)(2,1)}, u32[]{:S(2)}, u32[]{:S(2)}) collective-permute-start(bf16[768,512]{1,0:T(8,128)(2,1)} %get-tuple-element.112), channel_id=1, source_target_pairs={{0,1},{1,0},{2,3},{3,2},{4,5},{5,4},{6,7},{7,6},{8,9},{9,8},{10,11... | collective-permute-start | bytes 2359304 | tf_op jit(solution)/shard_map/ppermute | solution.py:381
  212.3 33.1 %collective-permute-start.8 = (bf16[768,512]{1,0:T(8,128)(2,1)}, bf16[768,512]{1,0:T(8,128)(2,1)}, u32[]{:S(2)}, u32[]{:S(2)}) collective-permute-start(bf16[768,512]{1,0:T(8,128)(2,1)} %fusion.16), channel_id=1, source_target_pairs={{0,2},{1,3},{2,0},{3,1},{4,6},{5,7},{6,4},{7,5},{8,10},{9,11},{10,... | collective-permute-start | bytes 2359304 | tf_op jit(solution)/shard_map/ppermute | solution.py:381
  230.3 15.1 %copy-start.14 = (f32[768]{0:T(1024)S(1)}, f32[768]{0:T(1024)}, u32[]{:S(2)}) copy-start(f32[768]{0:T(1024)} %param.28) | copy-start | bytes 9220
  230.3 15.1 %copy-start.15 = (f32[768]{0:T(1024)S(1)}, f32[768]{0:T(1024)}, u32[]{:S(2)}) copy-start(f32[768]{0:T(1024)} %param.24) | copy-start | bytes 9220
  249.8 3.1 copy-start.1
  336.7 6.7 %copy-start = (bf16[96,1856]{1,0:T(8,128)(2,1)S(1)}, bf16[96,1856]{1,0:T(8,128)(2,1)}, u32[]{:S(2)}) copy-start(bf16[96,1856]{1,0:T(8,128)(2,1)} %reduce-scatter.5.cloned.1.call-done) | copy-start | bytes 1069060
  338.4 7.0 %all-to-all-start = ((f32[4,4,24]{2,1,0:T(4,128)}), f32[4,4,24]{2,1,0:T(4,128)S(1)}, u32[]{:S(2)}, u32[]{:S(2)}) async-start(f32[4,4,24]{2,1,0:T(4,128)} %copy.104), calls=%async_computation.2 | async-start | bytes 16384 | tf_op jit(solution)/shard_map/all_to_all | solution.py:484
  344.3 2.2 copy-start.16
Sparse Core Ops, SparseCore 0:
  10.2 48.0 all-gather.2
  60.5 41.8 all-gather.4
  196.4 65.3 reduce-scatter.2
  265.2 71.4 reduce-scatter.4

commit v2 on v1

v2 whole, which is shorter than its diff:
```python
import functools

import jax
import jax.numpy as jnp
from jax import lax
from jax.experimental import pallas as pl
from jax.experimental.pallas import tpu as pltpu
from jax.sharding import PartitionSpec as P

HEAD = 64
ROT = 16
HALF = ROT // 2
EPS = 1e-05
NEG = -1e30
SCALE = HEAD ** (-0.5)
WHOLE = 1536
BLOCK = 512
F32 = jnp.float32
BF16 = jnp.bfloat16
VMEM_LIMIT = 56 * 1024 * 1024
MICROSECOND = 1_150_000_000


def dot(left, right):
    return jnp.dot(left, right, preferred_element_type=F32)


def dot_nt(left, right):
    return lax.dot_general(left, right, (((1,), (1,)), ((), ())), preferred_element_type=F32)


def call(kernel, grid, in_specs, out_specs, out_shape, scratch, name, prefetch=0, work=0, aliases={}):
    return pl.pallas_call(
        kernel,
        grid_spec=pltpu.PrefetchScalarGridSpec(
            num_scalar_prefetch=prefetch,
            grid=grid,
            in_specs=in_specs,
            out_specs=out_specs,
            scratch_shapes=scratch,
        ),
        out_shape=out_shape,
        compiler_params=pltpu.CompilerParams(vmem_limit_bytes=VMEM_LIMIT),
        cost_estimate=pl.CostEstimate(flops=work, bytes_accessed=0, transcendentals=0),
        input_output_aliases=aliases,
        name=name,
    )


def whole_spec(shape):
    return pl.BlockSpec(shape, lambda *_: (0,) * len(shape))


def column(ref, index):
    return ref[:, index : index + 1]


def join(pieces, first, count):
    return jnp.concatenate([piece[:, first : first + count] for piece in pieces], axis=0)


def blocks_of(order, rows):
    count = order.shape[0]
    size = rows // count
    return [
        (slice(at * size, (at + 1) * size), pl.ds(pl.multiple_of(order[at] * size, size), size))
        for at in range(count)
    ]


def choose(refs, step, held):
    for index, ref in enumerate(refs):

        @pl.when(step == index)
        def _(ref=ref):
            held[...] = ref[...]

    return held[...]


def fold(values):
    return sum(values[:, at : at + 128] for at in range(0, values.shape[1], 128))


def as_rows(parts, order=None, held=None):
    sums = [jnp.sum(part, axis=1, keepdims=True) for part in parts]
    lane = lax.broadcasted_iota(jnp.int32, parts[0].shape, 1)
    total = jnp.zeros(parts[0].shape, F32)
    for index, item in enumerate(sums):
        total = jnp.where(lane == index, item, total)
    if order is None:
        return total.T[0:8, :]
    return turn_back(order, held, total)[0:8, :]


def kept(items):
    return [pl.BlockSpec(memory_space=pl.ANY) for _ in items]


def standardize(block):
    values = block.astype(F32)
    center = values - jnp.mean(values, axis=0, keepdims=True)
    spread = jnp.mean(center * center, axis=0, keepdims=True)
    return center * lax.rsqrt(spread + EPS)


def turn_kernel(order, rows_ref, *refs):
    out_ref, held = refs[-2:]
    held[...] = rows_ref[...].T
    for here, there in blocks_of(order, out_ref.shape[0]):
        out_ref[here, :] = held[there, :]


def turn(order, rows, wait=()):
    count, width = rows.shape
    part = min(256, count)
    return call(
        turn_kernel,
        (count // part,),
        [pl.BlockSpec((part, width), lambda i, _: (i, 0)), *kept(wait)],
        pl.BlockSpec((width, part), lambda i, _: (0, i)),
        jax.ShapeDtypeStruct((width, count), rows.dtype),
        [pltpu.VMEM((width, part), rows.dtype)],
        "turn",
        prefetch=1,
    )(order, rows, *wait)


def turn_back(order, held, grads):
    for here, there in blocks_of(order, grads.shape[0]):
        held[there, :] = grads[here, :]
    return held[...].T


NORM_ROWS = 4


def stand_kernel(order, rows_ref, *refs):
    out_ref, held = refs[-2:]
    rows = rows_ref[...]
    held[...] = jnp.concatenate([rows, jnp.zeros((128 - rows.shape[0], rows.shape[1]), F32)], axis=0).T
    count = order.shape[0]
    size = rows.shape[1] // count
    lane = lax.broadcasted_iota(jnp.int32, (size, 128), 1)
    for index in range(count):
        first = pl.multiple_of(order[index] * size, size)
        here = slice(index * size, (index + 1) * size)
        out_ref[here, :] = jnp.where(lane < NORM_ROWS, held[pl.ds(first, size), :], held[here, :])


def stand(order, rows, wait):
    shape = (rows.shape[1], 128)
    return call(
        stand_kernel,
        (1,),
        [whole_spec(rows.shape), *kept(wait)],
        whole_spec(shape),
        jax.ShapeDtypeStruct(shape, F32),
        [pltpu.VMEM(shape, F32)],
        "stand",
        prefetch=1,
    )(order, rows, *wait)


def project_kernel(count, place, *refs):
    x_refs, pieces, refs = refs[:4], refs[4 : 4 + count], refs[4 + count :]
    col_ref, cos_ref, sin_ref = refs[:3]
    out_ref, x_now, wt = refs[-3:]
    step = pl.program_id(0)
    cols = out_ref.shape[0]

    @pl.when(step == 0)
    def _():
        wt[...] = join(pieces, 0, cols).T

    unit = standardize(choose(x_refs, step, x_now))
    normed = (unit * column(col_ref, 0) + column(col_ref, 1)).astype(BF16)
    cosine, sine = cos_ref[...], sin_ref[...]
    for head in range(cols // (3 * HEAD)):
        base = head * 3 * HEAD
        mixed = dot(wt[base : base + 3 * HEAD, :], normed) + col_ref[base : base + 3 * HEAD, 5:6]
        for part, factor in ((0, SCALE), (HEAD, 1.0)):
            one, two = mixed[part : part + HALF], mixed[part + HALF : part + ROT]
            turned = jnp.concatenate(
                [one * cosine - two * sine, two * cosine + one * sine, mixed[part + ROT : part + HEAD]],
                axis=0,
            )
            out_ref[base + part : base + part + HEAD, :] = (turned * factor).astype(BF16)
        out_ref[base + 2 * HEAD : base + 3 * HEAD, :] = mixed[2 * HEAD :].astype(BF16)


def project(place, x_all, pieces, columns, cosine, sine, wait):
    width, slab = x_all[0].shape
    cols = pieces[0].shape[1]
    by_place = lambda s, t: (0, s ^ t[0])
    return call(
        functools.partial(project_kernel, len(pieces)),
        (len(x_all),),
        [whole_spec(item.shape) for item in (*x_all, *pieces, columns)]
        + [pl.BlockSpec((HALF, slab), by_place), pl.BlockSpec((HALF, slab), by_place), *kept(wait)],
        pl.BlockSpec((cols, slab), by_place),
        jax.ShapeDtypeStruct((cols, len(x_all) * slab), BF16),
        [pltpu.VMEM((width, slab), BF16), pltpu.VMEM((cols, width), BF16)],
        "project",
        prefetch=1,
        work=1 * MICROSECOND,
    )(place, *x_all, *pieces, columns, cosine, sine, *wait)


def masked(scores, first_key, first_query, starts):
    diagonal = first_key + scores.shape[0] > first_query
    ragged = first_query + scores.shape[1] > WHOLE
    if not (diagonal or ragged):
        return scores
    key = first_key + lax.broadcasted_iota(jnp.int32, scores.shape, 0)
    allowed = key >= starts
    if diagonal:
        allowed &= key <= first_query + lax.broadcasted_iota(jnp.int32, scores.shape, 1)
    return jnp.where(allowed, scores, NEG)


def attend_kernel(handed, start_ref, qkv_ref, *refs):
    out_ref, lse_ref = refs[-4 - handed : len(refs) - 2 - handed]
    keys, held = refs[-2:]
    rows = qkv_ref.shape[1]
    block = min(BLOCK, rows)
    keys[...] = qkv_ref[HEAD : 2 * HEAD, :].T
    for begin in range(0, rows, block):
        here = slice(begin, begin + block)
        queries, starts = qkv_ref[0:HEAD, here], start_ref[0:1, here]
        top = jnp.full((1, block), NEG, F32)
        for first in range(0, begin + block, block):
            scores = masked(dot(keys[first : first + block, :], queries), first, begin, starts)
            held[first : first + block, :] = scores
            top = jnp.maximum(top, jnp.max(scores, axis=0, keepdims=True))
        total = jnp.zeros((1, block), F32)
        result = jnp.zeros((HEAD, block), F32)
        for first in range(0, begin + block, block):
            expo = jnp.exp(held[first : first + block, :] - top)
            total += jnp.sum(expo, axis=0, keepdims=True)
            result += dot(qkv_ref[2 * HEAD : 3 * HEAD, first : first + block], expo.astype(BF16))
        out_ref[:, here] = (result / total).astype(BF16)
        lse_ref[0, 0:1, here] = top + jnp.log(total)


def attend(starts, qkv, first, heads, wait, through):
    rows = qkv.shape[1]
    return call(
        functools.partial(attend_kernel, len(through)),
        (heads,),
        [whole_spec(starts.shape), pl.BlockSpec((3 * HEAD, rows), lambda h: (h + first, 0))]
        + kept((*through, *wait)),
        [pl.BlockSpec((HEAD, rows), lambda h: (h, 0)), pl.BlockSpec((1, 1, rows), lambda h: (h, 0, 0))]
        + kept(through),
        [jax.ShapeDtypeStruct((heads * HEAD, rows), BF16), jax.ShapeDtypeStruct((heads, 1, rows), F32)]
        + [jax.ShapeDtypeStruct(item.shape, item.dtype) for item in through],
        [pltpu.VMEM((rows, HEAD), BF16), pltpu.VMEM((rows, min(BLOCK, rows)), F32)],
        "attend",
        work=heads * MICROSECOND,
        aliases={2 + index: 2 + index for index in range(len(through))},
    )(starts, qkv, *through, *wait)


def attend_back_kernel(start_ref, cos_ref, sin_ref, qkv_ref, grad_ref, out_ref, lse_ref, *refs):
    mixed_ref, keys, values, key_sum, value_sum = refs[-5:]
    rows = qkv_ref.shape[1]
    block = min(BLOCK, rows)
    keys[...] = qkv_ref[HEAD : 2 * HEAD, :].T
    values[...] = qkv_ref[2 * HEAD : 3 * HEAD, :].T
    key_sum[...] = jnp.zeros_like(key_sum)
    value_sum[...] = jnp.zeros_like(value_sum)

    def put_unrotated(base, here, grads):
        cosine, sine = cos_ref[:, here], sin_ref[:, here]
        one, two = grads[0:HALF, :], grads[HALF:ROT, :]
        turned = jnp.concatenate(
            [one * cosine + two * sine, two * cosine - one * sine, grads[ROT:, :]], axis=0
        )
        mixed_ref[base : base + HEAD, here] = turned.astype(BF16)

    for begin in range(0, rows, block):
        here = slice(begin, begin + block)
        queries, grads, starts = qkv_ref[0:HEAD, here], grad_ref[:, here], start_ref[0:1, here]
        lse = lse_ref[0, 0:1, here]
        inner = jnp.sum(grads.astype(F32) * out_ref[:, here].astype(F32), axis=0, keepdims=True)
        query_rows, grad_rows = queries.T, grads.T
        query_sum = jnp.zeros((HEAD, block), F32)
        for first in range(0, begin + block, block):
            there = slice(first, first + block)
            scores = masked(dot(keys[there, :], queries), first, begin, starts)
            probs = jnp.exp(scores - lse)
            score_grads = (probs * (dot(values[there, :], grads) - inner)).astype(BF16)
            query_sum += dot(qkv_ref[HEAD : 2 * HEAD, there], score_grads)
            key_sum[there, :] += dot(score_grads, query_rows)
            value_sum[there, :] += dot(probs.astype(BF16), grad_rows)
        put_unrotated(0, here, query_sum * SCALE)
    put_unrotated(HEAD, slice(0, rows), key_sum[...].T)
    mixed_ref[2 * HEAD : 3 * HEAD, :] = value_sum[...].T.astype(BF16)


def attend_back(starts, cosine, sine, qkv, grads, out, lse, first, wait):
    rows = qkv.shape[1]
    heads = lse.shape[0]
    return call(
        attend_back_kernel,
        (heads,),
        [
            whole_spec(starts.shape),
            whole_spec(cosine.shape),
            whole_spec(sine.shape),
            pl.BlockSpec((3 * HEAD, rows), lambda h: (h + first, 0)),
            pl.BlockSpec((HEAD, rows), lambda h: (h + first, 0)),
            pl.BlockSpec((HEAD, rows), lambda h: (h, 0)),
            pl.BlockSpec((1, 1, rows), lambda h: (h, 0, 0)),
            *kept(wait),
        ],
        pl.BlockSpec((3 * HEAD, rows), lambda h: (h, 0)),
        jax.ShapeDtypeStruct((heads * 3 * HEAD, rows), BF16),
        [pltpu.VMEM((rows, HEAD), BF16)] * 2 + [pltpu.VMEM((rows, HEAD), F32)] * 2,
        "attend_back",
        work=9 * heads * MICROSECOND,
    )(starts, cosine, sine, qkv, grads, out, lse, *wait)


def feed_kernel(place, order, *refs):
    x_refs, dy_refs, refs = refs[:4], refs[4:8], refs[8:]
    weight_ref, att_refs, refs = refs[0], refs[1:-22], refs[-22:]
    col_ref, *refs = refs
    branch_refs, (normed_ref, att_grad_ref, weights_ref, vector_ref), refs = refs[:4], refs[4:8], refs[8:]
    x_now, dy_now, up, down, dense, up_t, down_t, dense_t, active, hidden_grad, sums, vectors, held = refs
    step = pl.program_id(0)
    hidden_count = up.shape[1]
    dense_count = dense.shape[1]

    @pl.when(step == 0)
    def _():
        for here, there in blocks_of(order, up.shape[0]):
            up[here, :] = weight_ref[there, :hidden_count]
            down[here, :] = weight_ref[there, hidden_count : 2 * hidden_count]
            dense[here, :] = weight_ref[there, 2 * hidden_count :]
        up_t[...] = up[...].T
        down_t[...] = down[...].T
        dense_t[...] = dense[...].T
        sums[...] = jnp.zeros_like(sums)
        vectors[...] = jnp.zeros_like(vectors)

    unit = standardize(choose(x_refs, step, x_now))
    dy = choose(dy_refs, step, dy_now)
    normed = (unit * column(col_ref, 2) + column(col_ref, 3)).astype(BF16)
    attended = jnp.concatenate([ref[...] for ref in att_refs], axis=0)
    att_grad_ref[...] = dot(dense_t[...], dy).astype(BF16)
    chunk = min(256, hidden_count)
    for first in range(0, hidden_count, chunk):
        units = slice(first, first + chunk)
        hidden = dot(up_t[units, :], normed) + col_ref[units, 4:5]
        chance = 0.5 + 0.5 * lax.erf(hidden * (0.5**0.5))
        density = jnp.exp(hidden * hidden * -0.5) * (hidden * 0.3989422804014327)
        now = (hidden * chance).astype(BF16)
        back = (dot(down_t[units, :], dy) * (chance + density)).astype(BF16)
        active[units, :] = now
        hidden_grad[units, :] = back
        sums[:, units] += dot_nt(normed, back)
        sums[:, hidden_count + first : hidden_count + first + chunk] += dot_nt(dy, now)
        vectors[3, units, :] += fold(back.astype(F32))
    sums[:, 2 * hidden_count :] += dot_nt(dy, attended)
    branch = (dot(dense[...], attended) + dot(down[...], active[...])).astype(BF16)
    for index, ref in enumerate(branch_refs):

        @pl.when(step == index)
        def _(ref=ref):
            ref[...] = branch

    normed_grad = dot(up[...], hidden_grad[...])
    normed_ref[0] = normed_grad * column(col_ref, 2)
    vectors[0] += fold(normed_grad * unit)
    vectors[1] += fold(normed_grad)
    vectors[2] += fold(dy.astype(F32))

    @pl.when(step == pl.num_programs(0) - 1)
    def _():
        for here, there in blocks_of(order, sums.shape[0]):
            weights_ref[there, :] = sums[here, :].astype(BF16)
        rows = as_rows([vectors[0], vectors[1], vectors[2]], order, held)
        vector_ref[...] = jnp.concatenate([rows[0:3], as_rows([vectors[3]])[0:5]], axis=0)


def feed(place, order, x_all, dy_all, weights, attended, columns):
    width, slab = x_all[0].shape
    parts = len(x_all)
    dense_count = sum(item.shape[0] for item in attended)
    hidden_count = (weights.shape[1] - dense_count) // 2
    grad_cols = 2 * hidden_count + dense_count
    by_place = lambda s, t, _: (0, s ^ t[0])
    return call(
        feed_kernel,
        (parts,),
        [whole_spec(item.shape) for item in (*x_all, *dy_all, weights)]
        + [pl.BlockSpec((item.shape[0], slab), by_place) for item in attended]
        + [whole_spec(columns.shape)],
        [whole_spec((width, slab))] * parts
        + [
            pl.BlockSpec((1, width, slab), lambda s, *_: (s, 0, 0)),
            pl.BlockSpec((dense_count, slab), by_place),
            whole_spec((width, grad_cols)),
            whole_spec((8, hidden_count)),
        ],
        [jax.ShapeDtypeStruct((width, slab), BF16)] * parts
        + [
            jax.ShapeDtypeStruct((parts, width, slab), F32),
            jax.ShapeDtypeStruct((dense_count, parts * slab), BF16),
            jax.ShapeDtypeStruct((width, grad_cols), BF16),
            jax.ShapeDtypeStruct((8, hidden_count), F32),
        ],
        [
            pltpu.VMEM((width, slab), BF16),
            pltpu.VMEM((width, slab), BF16),
            pltpu.VMEM((width, hidden_count), BF16),
            pltpu.VMEM((width, hidden_count), BF16),
            pltpu.VMEM((width, dense_count), BF16),
            pltpu.VMEM((hidden_count, width), BF16),
            pltpu.VMEM((hidden_count, width), BF16),
            pltpu.VMEM((dense_count, width), BF16),
            pltpu.VMEM((hidden_count, slab), BF16),
            pltpu.VMEM((hidden_count, slab), BF16),
            pltpu.VMEM((width, grad_cols), F32),
            pltpu.VMEM((4, hidden_count, 128), F32),
            pltpu.VMEM((width, 128), F32),
        ],
        "feed",
        prefetch=2,
        work=30 * MICROSECOND,
    )(place, order, *x_all, *dy_all, weights, *attended, columns)


def project_back_kernel(count, heads, place, order, *refs):
    x_refs, pieces, refs = refs[:4], refs[4 : 4 + count], refs[4 + count :]
    mixed_refs, refs = refs[:heads], refs[heads:]
    part_ref, col_ref, refs = refs[0], refs[1], refs[-13:]
    unit_refs, (own_ref, sent_ref, vector_ref), refs = refs[:4], refs[4:7], refs[7:]
    x_now, w, sums, vectors, counts, held = refs
    step = pl.program_id(0)

    @pl.when(step == 0)
    def _():
        w[...] = join(pieces, 0, w.shape[1])
        sums[...] = jnp.zeros_like(sums)
        vectors[...] = jnp.zeros_like(vectors)
        counts[...] = jnp.zeros_like(counts)

    unit = standardize(choose(x_refs, step, x_now))
    normed = (unit * column(col_ref, 0) + column(col_ref, 1)).astype(BF16)
    mixed = jnp.concatenate([ref[...] for ref in mixed_refs], axis=0)
    sums[...] += dot_nt(normed, mixed)
    counts[...] += fold(mixed.astype(F32))
    normed_grad = dot(w[...], mixed)
    total = (part_ref[0] + normed_grad * column(col_ref, 0)).astype(BF16)
    for index, ref in enumerate(unit_refs):

        @pl.when(step == index)
        def _(ref=ref):
            ref[...] = total

    vectors[0] += fold(normed_grad * unit)
    vectors[1] += fold(normed_grad)

    @pl.when(step == pl.num_programs(0) - 1)
    def _():
        half = own_ref.shape[0]
        own_ref[...] = sums[:half, :].astype(BF16)
        sent_ref[...] = sums[half:, :].astype(BF16)
        rows = as_rows([vectors[0], vectors[1]], order, held)
        tail = as_rows([counts[...]])[0:6]
        tail = jnp.concatenate([tail, jnp.zeros((6, rows.shape[1] - tail.shape[1]), F32)], axis=1)
        vector_ref[...] = jnp.concatenate([rows[0:2], tail], axis=0)


def project_back(place, order, x_all, pieces, mixed, part, columns, wait):
    width, slab = x_all[0].shape
    parts = len(x_all)
    cols = sum(item.shape[0] for item in mixed)
    return call(
        functools.partial(project_back_kernel, len(pieces), len(mixed)),
        (parts,),
        [whole_spec(item.shape) for item in (*x_all, *pieces)]
        + [pl.BlockSpec((item.shape[0], slab), lambda s, t, _: (0, s ^ t[0])) for item in mixed]
        + [pl.BlockSpec((1, width, slab), lambda s, *_: (s, 0, 0)), whole_spec(columns.shape)]
        + kept(wait),
        [whole_spec((width, slab))] * parts
        + [
            whole_spec((width // 2, cols)),
            whole_spec((width // 2, cols)),
            whole_spec((8, width)),
        ],
        [jax.ShapeDtypeStruct((width, slab), BF16)] * parts
        + [
            jax.ShapeDtypeStruct((width // 2, cols), BF16),
            jax.ShapeDtypeStruct((width // 2, cols), BF16),
            jax.ShapeDtypeStruct((8, width), F32),
        ],
        [
            pltpu.VMEM((width, slab), BF16),
            pltpu.VMEM((width, cols), BF16),
            pltpu.VMEM((width, cols), F32),
            pltpu.VMEM((2, width, 128), F32),
            pltpu.VMEM((cols, 128), F32),
            pltpu.VMEM((width, 128), F32),
        ],
        "project_back",
        prefetch=2,
        work=13 * MICROSECOND,
    )(place, order, *x_all, *pieces, *mixed, part, columns, *wait)


def finish_out_kernel(order, own_ref, near_ref, far_ref, rows_ref, bias_ref, *refs):
    out_ref, held = refs[-2:]
    branch = own_ref[...].astype(F32) + near_ref[...].astype(F32) + far_ref[...].astype(F32)
    branch = turn_back(order, held, branch)
    out_ref[...] = (rows_ref[...].astype(F32) + branch + bias_ref[...]).astype(BF16)


def finish(kernel, order, summands, rows, others, kind, name, work, wait=()):
    count, width = rows.shape
    part = min(128, count)
    rows_block = pl.BlockSpec((part, width), lambda i, _: (i, 0))
    return call(
        kernel,
        (count // part,),
        [pl.BlockSpec((width, part), lambda i, _: (0, i))] * len(summands)
        + [rows_block]
        + [rows_block if item.shape == rows.shape else whole_spec(item.shape) for item in others]
        + kept(wait),
        rows_block,
        jax.ShapeDtypeStruct(rows.shape, kind),
        [pltpu.VMEM((width, part), F32)],
        name,
        prefetch=1,
        work=work * MICROSECOND,
    )(order, *summands, rows, *others, *wait)


def finish_grad_kernel(order, own_ref, near_ref, far_ref, rows_ref, dy_ref, out_ref, held):
    grads = own_ref[...].astype(F32) + near_ref[...].astype(F32) + far_ref[...].astype(F32)
    grads = turn_back(order, held, grads)
    rows = rows_ref[...].astype(F32)
    center = rows - jnp.mean(rows, axis=1, keepdims=True)
    scale = lax.rsqrt(jnp.mean(center * center, axis=1, keepdims=True) + EPS)
    unit = center * scale
    along = jnp.mean(grads * unit, axis=1, keepdims=True)
    level = jnp.mean(grads, axis=1, keepdims=True)
    out_ref[...] = dy_ref[...].astype(F32) + scale * (grads - level - unit * along)


def share_kernel(own_ref, near_ref, last_ref, first_ref, *refs):
    far_ref, norms_ref, others_ref = refs[-3:]
    far_ref[...] = (own_ref[...].astype(F32) + near_ref[...].astype(F32)).astype(BF16)
    norms_ref[...] = jnp.concatenate([last_ref[0:2, :], first_ref[0:2, :]], axis=0)
    others_ref[...] = jnp.concatenate([first_ref[2:4, :], last_ref[2:4, :]], axis=0)


def share(own, near, last, first, wait):
    pair = (4, last.shape[1])
    return call(
        share_kernel,
        (1,),
        [whole_spec(item.shape) for item in (own, near, last, first)] + kept(wait),
        [whole_spec(own.shape), whole_spec(pair), whole_spec(pair)],
        [jax.ShapeDtypeStruct(own.shape, BF16), jax.ShapeDtypeStruct(pair, F32), jax.ShapeDtypeStruct(pair, F32)],
        [],
        "share",
        work=1 * MICROSECOND,
    )(own, near, last, first, *wait)


def halve_kernel(own_ref, came_ref, *refs):
    outs = refs[-4:]
    size = outs[0].shape[0]
    for index, ref in enumerate(outs):
        rows = slice(index * size, (index + 1) * size)
        ref[...] = (own_ref[rows, :].astype(F32) + came_ref[rows, :].astype(F32)).astype(ref.dtype)


def halve(own, came, wait, work=2):
    shape = (own.shape[0] // 4, own.shape[1])
    return call(
        halve_kernel,
        (1,),
        [whole_spec(own.shape), whole_spec(came.shape), *kept(wait)],
        [whole_spec(shape)] * 4,
        [jax.ShapeDtypeStruct(shape, kind) for kind in (F32, BF16, BF16, BF16)],
        [],
        "halve",
        work=work * MICROSECOND,
    )(own, came, *wait)


def total_kernel(kept_ref, *refs):
    came, (kept_rows, *came_rows), refs = refs[:3], refs[3:7], refs[7:]
    out_ref, rows_ref = refs[-2:]
    out_ref[...] = kept_ref[...] + sum(ref[...].astype(F32) for ref in came)
    rows_ref[...] = kept_rows[...] + sum(ref[...] for ref in came_rows)


def total(items, rows, wait):
    return call(
        total_kernel,
        (1,),
        [whole_spec(item.shape) for item in (*items, *rows)] + kept(wait),
        [whole_spec(items[0].shape), whole_spec(rows[0].shape)],
        [jax.ShapeDtypeStruct(items[0].shape, F32), jax.ShapeDtypeStruct(rows[0].shape, F32)],
        [],
        "total",
        work=1 * MICROSECOND,
    )(*items, *rows, *wait)


def gate_kernel(*refs):
    pass


def gate(item, wait):
    return call(
        gate_kernel,
        (1,),
        kept((item, *wait)),
        kept((item,))[0],
        jax.ShapeDtypeStruct(item.shape, item.dtype),
        [],
        "gate",
        aliases={0: 0},
    )(item, *wait)


def swap(value, axis, bits):
    count = lax.axis_size(axis)
    return lax.ppermute(value, axis, [(i, i ^ bits) for i in range(count)])


def gather_group(own):
    far = swap(own, "tensor", 2)
    near = swap(own, "tensor", 1)
    return (own, near, far, swap(far, "tensor", 1))


def scatter_group(slabs):
    far = (slabs[2].astype(F32) + swap(slabs[3], "tensor", 1).astype(F32)).astype(BF16)
    return (slabs[0], swap(slabs[1], "tensor", 1), swap(far, "tensor", 2)), (far,)


PARTNERS = (0, 2, 4, 6, 1, 3, 5, 7)


def paired():
    return lax.axis_size("dp") == len(PARTNERS)


def feature_order():
    if paired():
        return jnp.array(PARTNERS, jnp.int32) ^ lax.axis_index("dp").astype(jnp.int32)
    return jnp.zeros((1,), jnp.int32)


def gather_rows(own):
    if not paired():
        return (lax.all_gather(own, "dp", axis=0, tiled=True),)
    same = [own] + [swap(own, "dp", bits) for bits in PARTNERS[1:4]]
    return (*same, *(swap(piece, "dp", 1) for piece in same))


def partner_sums(own, sent):
    kept_block, *outward = halve(own, swap(sent, "dp", 1), ())
    return (kept_block, *(swap(half, "dp", bits) for half, bits in zip(outward, PARTNERS[1:4])))


def vector_sums(norms, others):
    norms = norms + swap(norms, "tensor", 1) + swap(norms, "tensor", 2) + swap(norms, "tensor", 3)
    rows = jnp.concatenate([norms, others], axis=0)
    rows = rows + swap(rows, "dp", 1)
    return (rows, *(swap(rows, "dp", bits) for bits in PARTNERS[1:4]))


def body(
    tokens,
    segment_ids,
    ln1_gain,
    ln1_bias,
    ln2_gain,
    ln2_bias,
    w_qkv,
    b_qkv,
    w_dense,
    b_dense,
    w_fc1,
    b_fc1,
    w_fc2,
    b_fc2,
    cotangent,
):
    group_rows = segment_ids.shape[0]
    width = tokens.shape[1]
    own_width = w_qkv.shape[0]
    dp_count = lax.axis_size("dp")
    tensor_count = lax.axis_size("tensor")
    mine = lax.axis_index("tensor").astype(jnp.int32)
    place = mine.reshape(1)
    order = feature_order()

    firsts = gather_rows(w_qkv)
    x_all = gather_group(turn(order, tokens))
    weights = lax.all_gather(jnp.concatenate([w_fc1, w_fc2, w_dense], axis=1), "dp", axis=0, tiled=True)
    rows = jnp.stack([ln1_gain, ln1_bias, ln2_gain, ln2_bias, b_fc1, jnp.pad(b_qkv, (0, width - b_qkv.shape[0]))])
    columns = stand(order, jnp.pad(rows, ((0, 2), (0, 0))), ())
    dy_own = gate(turn(order, cotangent), (x_all[2], *firsts[4:]))
    dy_far, dy_near = swap(dy_own, "tensor", 2), swap(dy_own, "tensor", 1)

    row = jnp.arange(group_rows, dtype=jnp.int32)
    padding = segment_ids != segment_ids[0]
    length = jnp.sum(jnp.where(padding, 0, 1))
    starts = jnp.where(padding, length, 0)
    inverse = 10000.0 ** (-jnp.arange(0, ROT, 2, dtype=F32) / ROT)
    angles = inverse[:, None] * (row - starts).astype(F32)[None, :]
    cosine, sine = jnp.cos(angles), jnp.sin(angles)
    starts = starts[None, :]

    qkv = project(place, x_all, firsts, columns, cosine, sine, (dy_own,))
    heads = range(qkv.shape[0] // (3 * HEAD))
    attended, lse = [], []
    for head in heads:
        through = (dy_far,) if head == 1 else ()
        result, scale, *through = attend(starts, qkv, head, 1, attended[-1:], through)
        attended.append(result)
        lse.append(scale)
        if head == 1:
            (dy_far,) = through
    dy_all = (dy_own, dy_near, dy_far, swap(dy_far, "tensor", 1))
    *branch, part, att_grad, feed_grads, feed_vectors = feed(
        place, order, x_all, dy_all, weights, attended, columns
    )
    feed_grads = lax.psum_scatter(feed_grads, "dp", scatter_dimension=0, tiled=True).astype(F32)
    out_summands, branch_wait = scatter_group(branch)

    mixed_grad = []
    for head in heads:
        wait = (*branch_wait, *mixed_grad[-1:]) if head == 1 else mixed_grad[-1:]
        mixed_grad.append(
            attend_back(starts, cosine, sine, qkv, att_grad, attended[head], lse[head], head, wait)
        )
    *unit_grad, qkv_own, qkv_sent, last_vectors = project_back(
        place, order, x_all, firsts, mixed_grad, part, columns, out_summands[2:]
    )
    far, norms, others = share(
        unit_grad[2], swap(unit_grad[3], "tensor", 1), last_vectors, feed_vectors, ()
    )
    summands = (unit_grad[0], swap(unit_grad[1], "tensor", 1), swap(far, "tensor", 2))
    input_grad = finish(
        finish_grad_kernel, order, summands, tokens, (cotangent,), F32, "finish_grad", 5
    )
    bias = (b_dense + b_fc2)[None, :]
    out = finish(
        finish_out_kernel, order, out_summands, tokens, (bias,), BF16, "finish_out", 4, (input_grad,)
    )
    if paired():
        qkv_grads, vectors = total(
            partner_sums(qkv_own, qkv_sent), vector_sums(norms, others), (input_grad,)
        )
    else:
        qkv_grads = jnp.concatenate([qkv_own, qkv_sent], axis=0)
        qkv_grads = lax.psum_scatter(qkv_grads, "dp", scatter_dimension=0, tiled=True).astype(F32)
        vectors = lax.psum(jnp.concatenate([lax.psum(norms, "tensor"), others], axis=0), "dp")
    at = lax.axis_index("dp") * own_width + mine * (own_width // tensor_count)
    norm_grads = lax.dynamic_slice_in_dim(vectors[:5], at, own_width // tensor_count, 1)
    hidden_bias = lax.dynamic_slice_in_dim(vectors[5], lax.axis_index("dp") * own_width, own_width, 0)
    bias_own = b_qkv.shape[0] // dp_count
    qkv_bias = lax.dynamic_slice_in_dim(vectors[6], lax.axis_index("dp") * bias_own, bias_own, 0)
    hidden_count = w_fc1.shape[1]
    return (
        out,
        input_grad,
        norm_grads[0],
        norm_grads[1],
        norm_grads[2],
        norm_grads[3],
        qkv_grads,
        qkv_bias,
        feed_grads[:, 2 * hidden_count :],
        norm_grads[4],
        feed_grads[:, :hidden_count],
        hidden_bias,
        feed_grads[:, hidden_count : 2 * hidden_count],
        norm_grads[4],
    )


def solution(mesh):
    placed = (
        P(("dp", "tensor"), None),
        P("dp"),
        P(),
        P(),
        P(),
        P(),
        P("dp", "tensor"),
        P("tensor"),
        P("dp", "tensor"),
        P(),
        P("dp", "tensor"),
        P("tensor"),
        P("dp", "tensor"),
        P(),
        P(("dp", "tensor"), None),
    )
    return jax.shard_map(
        body,
        mesh=mesh,
        in_specs=placed,
        out_specs=(
            P(("dp", "tensor"), None),
            P(("dp", "tensor"), None),
            P(("dp", "tensor")),
            P(("dp", "tensor")),
            P(("dp", "tensor")),
            P(("dp", "tensor")),
            P("dp", "tensor"),
            P(("tensor", "dp")),
            P("dp", "tensor"),
            P(("dp", "tensor")),
            P("dp", "tensor"),
            P(("tensor", "dp")),
            P("dp", "tensor"),
            P(("dp", "tensor")),
        ),
        check_vma=False,
    )
```

time: 354 us -> 235 us (0.66)
  waiting for transfers between devices: 109 us -> 16.6 us
  blocking collectives: 70.5 us -> 0 us
  Pallas kernels: 92 us -> 134 us
  starting transfers between devices: 10.7 us -> 39.4 us
  other arithmetic: 31.3 us -> 8.11 us
  local copies, waits for them, and re-layouts: 25.6 us -> 17.7 us
    reduce_scatter x2 -> x1, waiting for transfers between devices: 78.5 us -> 0.01 us  [body(): lax.psum_scatter(feed_grads, 'dp', scatter_dimension=0, tiled=True)]
    all_gather x2 -> x0, blocking collectives: 70.5 us -> none  [the longest x1 36.3 us: body(): qkv_full = lax.all_gather(w_qkv, 'dp', axis=0, tiled=True)]
    pallas_call x4 -> x15, Pallas kernels: 65.5 us -> 103 us  [the longest x1 35.3 us: feed(): call(feed_kernel, (parts,), [whole_spec(item.shape) for item in (*x_all,...]
    ppermute x12 -> x30, starting transfers between devices: 7.06 us -> 39.3 us  [swap(): return lax.ppermute(value, axis, [(i, i ^ bits) for i in range(count)])]
    ppermute x12 -> x30, waiting for transfers between devices: 29.1 us -> 16.5 us  [swap(): return lax.ppermute(value, axis, [(i, i ^ bits) for i in range(count)])]
    another operation x4 -> x0, other arithmetic: 8.25 us -> none  [the longest x2 6.01 us: gather_group(): return jnp.stack([own, near, far, swap(far, 1)])]
    convert_element_type x5 -> x1, other arithmetic: 6.5 us -> 0.21 us  [scatter_group(): (slabs[2].astype(F32) + swap(slabs[3], 'tensor', 1).astype(F32)).astype(B...]
    broadcast_in_dim x6 -> x1, local copies, waits for them, and re-layouts: 5.52 us -> 0.59 us  [body(): bias = (b_dense + b_fc2)[None, :]]
  transfers between devices with their start and end apart: 17 -> 32, of which waited for: 5 -> 7; matrix products, arithmetic and copies ran while one was open for 14% -> 5% of each run, Pallas kernels for 6% -> 43%
where the time goes in v2:
time: 235 us; the launch traced here: 231 us
  Pallas kernels  134 us (57%)
  starting transfers between devices  39.4 us (17%)
  local copies, waits for them, and re-layouts  17.7 us (8%)
  waiting for transfers between devices  16.6 us (7%)
  between operations  14.7 us (6%)
  other arithmetic  8.11 us (3%)
    ppermute x30, starting transfers between devices, swap(): return lax.ppermute(value, axis, [(i, i ^ bits) for i in range(count)])  39.3 us
    pallas_call x1, Pallas kernels, feed(): call(feed_kernel, (parts,), [whole_spec(item.shape) for item in (*x_all,...  35.3 us
    pallas_call x3, Pallas kernels, attend_back(): call(attend_back_kernel, (heads,), [whole_spec(starts.shape), whole_spec(...  31 us
    pallas_call x3, Pallas kernels, attend(): call(functools.partial(attend_kernel, len(through)), (heads,), [whole_spe...  18 us
    ppermute x30, waiting for transfers between devices, swap(): return lax.ppermute(value, axis, [(i, i ^ bits) for i in range(count)])  16.5 us
    pallas_call x1, Pallas kernels, project_back(): call(functools.partial(project_back_kernel, len(pieces), len(mixed)), (pa...  16 us
    pallas_call x2, Pallas kernels, finish(): call(kernel, (count // part,), [pl.BlockSpec((width, part), lambda i, _:...  11 us
    unnamed x85, local copies, waits for them, and re-layouts  9.37 us
  transfers between devices with their start and end apart: 32, of which 7 were waited for; matrix products, arithmetic and copies ran while one was open for 5% of the time, Pallas kernels for 43%

profile of v2, /device:TPU:0, one launch (start us, length us, event | category | flops | bytes accessed | tf_op | source)
XLA Modules:
  0.0 230.7 jit_solution(2202599512729277932)
XLA Ops:
  7.2 1.8 pad_maximum_fusion
  9.1 1.2 broadcast_xor_fusion.order
  10.3 2.8 %turn.2.refs_0_ = bf16[768,512]{1,0:T(8,128)(2,1)} custom-call(s32[8]{0:T(128)} %broadcast_xor_fusion.order, bf16[512,768]{1,0:T(8,128)(2,1)} %rows_ref.7), custom_call_target="tpu_custom_call" | custom-call | tf_op jit(solution)/shard_map/turn/pallas_call | solution.py:117
  13.1 3.0 %collective-permute-start.1 = (bf16[768,512]{1,0:T(8,128)(2,1)}, bf16[768,512]{1,0:T(8,128)(2,1)S(1)}, u32[]{:S(2)}, u32[]{:S(2)}) collective-permute-start(bf16[768,512]{1,0:T(8,128)(2,1)} %turn.2.refs_0_), channel_id=1, source_target_pairs={{0,2},{1,3},{2,0},{3,1},{4,6},{5,7},{6,4},{7,5},{8,10},{9,11},{10,... | collective-permute-start | bytes 2359304 | tf_op jit(solution)/shard_map/ppermute | solution.py:635
  16.2 1.6 collective-permute-start.4
  17.7 2.6 %collective-permute-start.6 = (bf16[96,576]{1,0:T(8,128)(2,1)S(1)}, bf16[96,576]{1,0:T(8,128)(2,1)S(1)}, u32[]{:S(2)}, u32[]{:S(2)}) collective-permute-start(bf16[96,576]{1,0:T(8,128)(2,1)S(1)} %copy-done.9), channel_id=1, source_target_pairs={{0,16},{4,20},{8,24},{12,28},{16,0},{20,4},{24,8},{28,12},{1,17},{... | collective-permute-start | bytes 331784 | tf_op jit(solution)/shard_map/ppermute | solution.py:635
  20.5 1.5 collective-permute-start.3
  22.0 0.5 slice.37
  22.6 1.3 collective-permute-start.5
  23.9 10.2 %collective-permute-done.6.refs_6_ = bf16[96,576]{1,0:T(8,128)(2,1)S(1)} collective-permute-done((bf16[96,576]{1,0:T(8,128)(2,1)S(1)}, bf16[96,576]{1,0:T(8,128)(2,1)S(1)}, u32[]{:S(2)}, u32[]{:S(2)}) %collective-permute-start.6) | collective-permute-done | bytes 110624 | tf_op jit(solution)/shard_map/ppermute | solution.py:635
  34.1 1.4 collective-permute-start.7
  35.5 0.6 collective-permute-start.9
  36.1 1.3 select_reduce_fusion
  37.4 2.8 %turn.3.refs_0_ = bf16[768,512]{1,0:T(8,128)(2,1)} custom-call(s32[8]{0:T(128)} %broadcast_xor_fusion.order, bf16[512,768]{1,0:T(8,128)(2,1)} %dy_ref.1), custom_call_target="tpu_custom_call" | custom-call | tf_op jit(solution)/shard_map/turn/pallas_call | solution.py:117
  41.1 0.9 copy-done
  42.6 1.2 subtract_convert_fusion
  44.0 0.6 pad.9.rows_ref
  44.6 2.4 %stand.1.refs_12_.refs_16_ = f32[768,128]{1,0:T(8,128)} custom-call(s32[8]{0:T(128)} %broadcast_xor_fusion.order, f32[8,768]{1,0:T(8,128)} %pad.9.rows_ref), custom_call_target="tpu_custom_call" | custom-call | tf_op jit(solution)/shard_map/stand/pallas_call | solution.py:153
  47.0 1.0 multiply_sine_fusion
  48.3 0.9 copy-done.1
  49.5 8.5 %project.1.qkv_ref = bf16[576,2048]{1,0:T(8,128)(2,1)} custom-call(s32[1]{0:T(128)} %bitcast.place, bf16[768,512]{1,0:T(8,128)(2,1)} %turn.2.refs_0_, bf16[768,512]{1,0:T(8,128)(2,1)} %copy-done.1, bf16[768,512]{1,0:T(8,128)(2,1)} %copy-done, bf16[768,512]{1,0:T(8,128)(2,1)} %copy-done.2, bf16[96,576]{1,0:T(8,128)(2,1)} %refs_4_.3, ...), custom_call_target="tpu_custom_call" | custom-call | flops 1150000000 | tf_op jit(solution)/shard_map/project/pallas_call | solution.py:196
  58.0 6.0 %attend.3 = (bf16[64,2048]{1,0:T(8,128)(2,1)}, f32[1,1,2048]{2,1,0:T(1,128)}) custom-call(s32[1,2048]{1,0:T(1,128)} %bitcast.18, bf16[576,2048]{1,0:T(8,128)(2,1)} %project.1.qkv_ref), custom_call_target="tpu_custom_call" | custom-call | flops 1150000000 | tf_op jit(solution)/shard_map/attend/pallas_call | solution.py:248
  64.0 0.9 copy-done.30
  64.9 6.0 %attend.4 = (bf16[64,2048]{1,0:T(8,128)(2,1)}, f32[1,1,2048]{2,1,0:T(1,128)}, bf16[768,512]{1,0:T(8,128)(2,1)}) custom-call(s32[1,2048]{1,0:T(1,128)} %bitcast.19, bf16[576,2048]{1,0:T(8,128)(2,1)} %project.1.qkv_ref, bf16[768,512]{1,0:T(8,128)(2,1)} %copy-done.30, ...), custom_call_target="tpu_custom_call", output_to_operand_aliasing={{2}: (2, {})} | custom-call | flops 1150000000 | tf_op jit(solution)/shard_map/attend/pallas_call | solution.py:248
  71.1 6.0 %attend.5 = (bf16[64,2048]{1,0:T(8,128)(2,1)}, f32[1,1,2048]{2,1,0:T(1,128)}) custom-call(s32[1,2048]{1,0:T(1,128)} %bitcast.20, bf16[576,2048]{1,0:T(8,128)(2,1)} %project.1.qkv_ref, bf16[64,2048]{1,0:T(8,128)(2,1)} %get-tuple-element.47.refs_0_.refs_10_.out_ref), custom_call_target="tpu_custom_call" | custom-call | flops 1150000000 | tf_op jit(solution)/shard_map/attend/pallas_call | solution.py:248
  77.1 0.8 copy-done.32
  78.2 35.3 %feed.1 = (bf16[768,512]{1,0:T(8,128)(2,1)}, bf16[768,512]{1,0:T(8,128)(2,1)}, bf16[768,512]{1,0:T(8,128)(2,1)}, bf16[768,512]{1,0:T(8,128)(2,1)}, f32[4,768,512...) custom-call(s32[1]{0:T(128)} %bitcast.place, s32[8]{0:T(128)} %broadcast_xor_fusion.order, ...), custom_call_target="tpu_custom_call" | custom-call | flops 34500001792 | tf_op jit(solution)/shard_map/feed/pallas_call | solution.py:394
  114.1 10.2 %attend_back.3.refs_1_.refs_12_ = bf16[192,2048]{1,0:T(8,128)(2,1)} custom-call(s32[1,2048]{1,0:T(1,128)} %bitcast.21, f32[8,2048]{1,0:T(8,128)} %get-tuple-element.83.refs_13_.cos_ref, f32[8,2048]{1,0:T(8,128)} %get-tuple-element.82.refs_14_.sin_ref, bf16[576,2048]{1,0:T(8,128)(2,1)} %project.1.qkv_ref, bf16[192,2048]{1,0:T(8,128)(2,1)} %get-tuple-element.53.grad_ref, ...), custom_call_target="tpu_custom_call" | custom-call | flops 10350000128 | tf_op jit(solution)/shard_map/attend_back/pallas_call | solution.py:304
  124.5 1.6 collective-permute-start.15
  126.1 10.6 %attend_back.4.refs_0_.refs_13_ = bf16[192,2048]{1,0:T(8,128)(2,1)} custom-call(s32[1,2048]{1,0:T(1,128)} %bitcast.22, f32[8,2048]{1,0:T(8,128)} %get-tuple-element.83.refs_13_.cos_ref, f32[8,2048]{1,0:T(8,128)} %get-tuple-element.82.refs_14_.sin_ref, bf16[576,2048]{1,0:T(8,128)(2,1)} %project.1.qkv_ref, bf16[192,2048]{1,0:T(8,128)(2,1)} %get-tuple-element.53.grad_ref, ...), custom_call_target="tpu_custom_call" | custom-call | flops 10350000128 | tf_op jit(solution)/shard_map/attend_back/pallas_call | solution.py:304
  136.7 10.2 %attend_back.5.refs_14_ = bf16[192,2048]{1,0:T(8,128)(2,1)} custom-call(s32[1,2048]{1,0:T(1,128)} %bitcast.23, f32[8,2048]{1,0:T(8,128)} %get-tuple-element.83.refs_13_.cos_ref, f32[8,2048]{1,0:T(8,128)} %get-tuple-element.82.refs_14_.sin_ref, bf16[576,2048]{1,0:T(8,128)(2,1)} %project.1.qkv_ref, bf16[192,2048]{1,0:T(8,128)(2,1)} %get-tuple-element.53.grad_ref, ...), custom_call_target="tpu_custom_call" | custom-call | flops 10350000128 | tf_op jit(solution)/shard_map/attend_back/pallas_call | solution.py:304
  146.9 0.9 copy-done.26
  147.8 16.0 %project_back.1 = (bf16[768,512]{1,0:T(8,128)(2,1)}, bf16[768,512]{1,0:T(8,128)(2,1)}, bf16[768,512]{1,0:T(8,128)(2,1)}, bf16[768,512]{1,0:T(8,128)(2,1)}, bf16[...) custom-call(s32[1]{0:T(128)} %bitcast.place, s32[8]{0:T(128)} %broadcast_xor_fusion.order, ...), custom_call_target="tpu_custom_call" | custom-call | flops 14949999616 | tf_op jit(solution)/shard_map/project_back/pallas_call | solution.py:481
  163.9 1.3 collective-permute-start.19
  165.1 1.2 collective-permute-done.17.near_ref
  166.3 0.9 copy-done.34
  167.2 2.5 %share.1 = (bf16[768,512]{1,0:T(8,128)(2,1)}, f32[4,768]{1,0:T(4,128)}, f32[4,768]{1,0:T(4,128)}) custom-call(bf16[768,512]{1,0:T(8,128)(2,1)} %get-tuple-element.60.own_ref, bf16[768,512]{1,0:T(8,128)(2,1)} %copy-done.34, f32[8,768]{1,0:T(8,128)} %get-tuple-element.62.last_ref, f32[8,768]{1,0:T(8,128)} %get-tuple-element.63.first_ref), custom_call_target="tpu_custom_call" | custom-call | flops 1150000000 | tf_op jit(solution)/shard_map/share/pallas_call | solution.py:562
  169.8 0.7 collective-permute-start.24
  170.5 1.0 collective-permute-start.25
  172.0 0.7 collective-permute-start.18
  172.7 0.6 broadcast_in_dim.26.bias_ref
  173.9 0.7 add_add_fusion
  174.6 0.7 pad_maximum_fusion.1
  175.3 1.5 collective-permute-start.26
  176.8 1.3 collective-permute-done.19.came_ref
  178.1 0.8 copy-done.35
  178.9 2.0 halve.1
  180.9 9.9 %collective-permute-start.20 = (bf16[96,576]{1,0:T(8,128)(2,1)}, bf16[96,576]{1,0:T(8,128)(2,1)S(1)}, u32[]{:S(2)}, u32[]{:S(2)}) collective-permute-start(bf16[96,576]{1,0:T(8,128)(2,1)} %get-tuple-element.68), channel_id=1, source_target_pairs={{0,8},{4,12},{8,0},{12,4},{16,24},{20,28},{24,16},{28,20},{1,9},{5... | collective-permute-start | bytes 331784 | tf_op jit(solution)/shard_map/ppermute | solution.py:635
  190.8 2.2 collective-permute-start.21
  193.0 1.5 collective-permute-start.22
  194.5 3.1 %collective-permute-done.20.refs_0_ = bf16[96,576]{1,0:T(8,128)(2,1)S(1)} collective-permute-done((bf16[96,576]{1,0:T(8,128)(2,1)}, bf16[96,576]{1,0:T(8,128)(2,1)S(1)}, u32[]{:S(2)}, u32[]{:S(2)}) %collective-permute-start.20) | collective-permute-done | bytes 110624 | tf_op jit(solution)/shard_map/ppermute | solution.py:635
  197.6 2.0 collective-permute-start.28
  199.6 2.4 %collective-permute-start.29 = (f32[8,768]{1,0:T(8,128)S(1)}, f32[8,768]{1,0:T(8,128)S(1)}, u32[]{:S(2)}, u32[]{:S(2)}) collective-permute-start(f32[8,768]{1,0:T(8,128)S(1)} %fusion.2.refs_3_), channel_id=1, source_target_pairs={{0,24},{4,28},{8,16},{12,20},{16,8},{20,12},{24,0},{28,4},{1,25},{... | collective-permute-start | bytes 73736 | tf_op jit(solution)/shard_map/ppermute | solution.py:635
  201.9 6.0 %finish_grad.1.refs_0_.refs_7_ = f32[512,768]{1,0:T(8,128)} custom-call(s32[8]{0:T(128)} %broadcast_xor_fusion.order, bf16[768,512]{1,0:T(8,128)(2,1)} %get-tuple-element.58.own_ref, bf16[768,512]{1,0:T(8,128)(2,1)} %copy-done.28, bf16[768,512]{1,0:T(8,128)(2,1)} %copy-done.29, bf16[512,768]{1,0:T(8,128)(2,1)} %rows_ref.7, bf16[512,768]{1,0:T(8,128)(2,1)} %dy_ref.1), custom_call_target="tpu_custom_call" | custom-call | flops 5750000128 | tf_op jit(solution)/shard_map/finish_grad/pallas_call | solution.py:525
  208.8 1.9 total.1
  210.7 0.8 constant_dynamic-slice_fusion.2
  211.5 0.5 slice_bitcast_fusion
  212.0 0.8 fusion.4
  212.8 0.6 fusion
  213.4 0.6 fusion.1
  214.0 0.9 copy-done.31
  214.9 5.0 %finish_out.1 = bf16[512,768]{1,0:T(8,128)(2,1)} custom-call(s32[8]{0:T(128)} %broadcast_xor_fusion.order, bf16[768,512]{1,0:T(8,128)(2,1)} %get-tuple-element.49.own_ref, bf16[768,512]{1,0:T(8,128)(2,1)} %copy-done.31, bf16[768,512]{1,0:T(8,128)(2,1)} %copy-done.26, bf16[512,768]{1,0:T(8,128)(2,1)} %rows_ref.7, f32[1,768]{1,0:T(1,128)} %broadcast_in_dim.26.bias_ref, ...), custom_call_target="tpu_custom_call" | custom-call | flops 4600000000 | tf_op jit(solution)/shard_map/finish_out/pallas_call | solution.py:525
  219.9 1.8 fusion.3
  221.7 1.4 slice.49
  (134 shorter events, 6.2 us)
Async XLA Ops:
  7.2 9.0 %copy-start.9 = (bf16[96,576]{1,0:T(8,128)(2,1)S(1)}, bf16[96,576]{1,0:T(8,128)(2,1)}, u32[]{:S(2)}) copy-start(bf16[96,576]{1,0:T(8,128)(2,1)} %refs_4_.3) | copy-start | bytes 331780
  7.2 14.8 %copy-start.15 = (s32[2048]{0:T(1024)S(1)}, s32[2048]{0:T(1024)}, u32[]{:S(2)}) copy-start(s32[2048]{0:T(1024)} %param.17) | copy-start | bytes 24580
  7.2 69.9 %all-gather.2.cloned.1.call-start = ((), (), s32[]{:S(2)}) async-start(), calls=%async_computation.1 | async-start | bytes 3096576 | tf_op jit(solution)/shard_map/all_gather | solution.py:709
  9.1 210.8 %reduce-scatter.2.cloned.1.call-start = ((), (), s32[]{:S(2)}) async-start(), calls=%async_computation.2 | async-start | bytes 3096576 | tf_op jit(solution)/shard_map/reduce_scatter | solution.py:738
  13.1 30.7 %copy-start.23 = (f32[576]{0:T(1024)S(1)}, f32[576]{0:T(1024)}, u32[]{:S(2)}) copy-start(f32[576]{0:T(1024)} %param.23) | copy-start | bytes 6916
  13.1 30.7 %copy-start.18 = (f32[768]{0:T(1024)S(1)}, f32[768]{0:T(1024)}, u32[]{:S(2)}) copy-start(f32[768]{0:T(1024)} %param.18) | copy-start | bytes 9220
  13.1 30.8 %copy-start.19 = (f32[768]{0:T(1024)S(1)}, f32[768]{0:T(1024)}, u32[]{:S(2)}) copy-start(f32[768]{0:T(1024)} %param.19) | copy-start | bytes 9220
  13.1 30.8 %copy-start.20 = (f32[768]{0:T(1024)S(1)}, f32[768]{0:T(1024)}, u32[]{:S(2)}) copy-start(f32[768]{0:T(1024)} %param.20) | copy-start | bytes 9220
  13.1 30.8 %copy-start.21 = (f32[768]{0:T(1024)S(1)}, f32[768]{0:T(1024)}, u32[]{:S(2)}) copy-start(f32[768]{0:T(1024)} %param.21) | copy-start | bytes 9220
  13.1 30.8 %copy-start.22 = (f32[768]{0:T(1024)S(1)}, f32[768]{0:T(1024)}, u32[]{:S(2)}) copy-start(f32[768]{0:T(1024)} %param.27) | copy-start | bytes 9220
  13.1 27.3 %collective-permute-start.1 = (bf16[768,512]{1,0:T(8,128)(2,1)}, bf16[768,512]{1,0:T(8,128)(2,1)S(1)}, u32[]{:S(2)}, u32[]{:S(2)}) collective-permute-start(bf16[768,512]{1,0:T(8,128)(2,1)} %turn.2.refs_0_), channel_id=1, source_target_pairs={{0,2},{1,3},{2,0},{3,1},{4,6},{5,7},{6,4},{7,5},{8,10},{9,11},{10,... | collective-permute-start | bytes 2359304 | tf_op jit(solution)/shard_map/ppermute | solution.py:635
  16.2 6.4 %collective-permute-start.4 = (bf16[96,576]{1,0:T(8,128)(2,1)S(1)}, bf16[96,576]{1,0:T(8,128)(2,1)S(1)}, u32[]{:S(2)}, u32[]{:S(2)}) collective-permute-start(bf16[96,576]{1,0:T(8,128)(2,1)S(1)} %copy-done.9), channel_id=1, source_target_pairs={{0,8},{4,12},{8,0},{12,4},{16,24},{20,28},{24,16},{28,20},{1,9},{5... | collective-permute-start | bytes 331784 | tf_op jit(solution)/shard_map/ppermute | solution.py:635
  17.7 16.3 %collective-permute-start.6 = (bf16[96,576]{1,0:T(8,128)(2,1)S(1)}, bf16[96,576]{1,0:T(8,128)(2,1)S(1)}, u32[]{:S(2)}, u32[]{:S(2)}) collective-permute-start(bf16[96,576]{1,0:T(8,128)(2,1)S(1)} %copy-done.9), channel_id=1, source_target_pairs={{0,16},{4,20},{8,24},{12,28},{16,0},{20,4},{24,8},{28,12},{1,17},{... | collective-permute-start | bytes 331784 | tf_op jit(solution)/shard_map/ppermute | solution.py:635
  20.3 15.2 %collective-permute-start.8 = (bf16[96,576]{1,0:T(8,128)(2,1)S(1)}, bf16[96,576]{1,0:T(8,128)(2,1)S(1)}, u32[]{:S(2)}, u32[]{:S(2)}) collective-permute-start(bf16[96,576]{1,0:T(8,128)(2,1)S(1)} %copy-done.9), channel_id=1, source_target_pairs={{0,24},{4,28},{8,16},{12,20},{16,8},{20,12},{24,0},{28,4},{1,25},{... | collective-permute-start | bytes 331784 | tf_op jit(solution)/shard_map/ppermute | solution.py:635
  20.5 19.7 %collective-permute-start.3 = (bf16[96,576]{1,0:T(8,128)(2,1)S(1)}, bf16[96,576]{1,0:T(8,128)(2,1)S(1)}, u32[]{:S(2)}, u32[]{:S(2)}) collective-permute-start(bf16[96,576]{1,0:T(8,128)(2,1)S(1)} %copy-done.9), channel_id=1, source_target_pairs={{0,4},{4,0},{8,12},{12,8},{16,20},{20,16},{24,28},{28,24},{1,5},{5... | collective-permute-start | bytes 331784 | tf_op jit(solution)/shard_map/ppermute | solution.py:635
  22.6 24.4 %copy-start.10 = (bf16[96,576]{1,0:T(8,128)(2,1)}, bf16[96,576]{1,0:T(8,128)(2,1)S(1)}, u32[]{:S(2)}) copy-start(bf16[96,576]{1,0:T(8,128)(2,1)S(1)} %collective-permute-done.4.refs_5_) | copy-start | bytes 331780
  22.6 17.7 %collective-permute-start.5 = (bf16[96,576]{1,0:T(8,128)(2,1)S(1)}, bf16[96,576]{1,0:T(8,128)(2,1)S(1)}, u32[]{:S(2)}, u32[]{:S(2)}) collective-permute-start(bf16[96,576]{1,0:T(8,128)(2,1)S(1)} %collective-permute-done.4.refs_5_), channel_id=1, source_target_pairs={{0,4},{4,0},{8,12},{12,8},{16,20},{20,16},{24,28},{28,24},{1,5},{5... | collective-permute-start | bytes 331784 | tf_op jit(solution)/shard_map/ppermute | solution.py:635
  34.1 12.9 %copy-start.11 = (bf16[96,576]{1,0:T(8,128)(2,1)}, bf16[96,576]{1,0:T(8,128)(2,1)S(1)}, u32[]{:S(2)}) copy-start(bf16[96,576]{1,0:T(8,128)(2,1)S(1)} %collective-permute-done.6.refs_6_) | copy-start | bytes 331780
  34.1 6.2 %collective-permute-start.7 = (bf16[96,576]{1,0:T(8,128)(2,1)S(1)}, bf16[96,576]{1,0:T(8,128)(2,1)S(1)}, u32[]{:S(2)}, u32[]{:S(2)}) collective-permute-start(bf16[96,576]{1,0:T(8,128)(2,1)S(1)} %collective-permute-done.6.refs_6_), channel_id=1, source_target_pairs={{0,4},{4,0},{8,12},{12,8},{16,20},{20,16},{24,28},{28,24},{1,5},{5... | collective-permute-start | bytes 331784 | tf_op jit(solution)/shard_map/ppermute | solution.py:635
  35.5 11.4 %copy-start.12 = (bf16[96,576]{1,0:T(8,128)(2,1)}, bf16[96,576]{1,0:T(8,128)(2,1)S(1)}, u32[]{:S(2)}) copy-start(bf16[96,576]{1,0:T(8,128)(2,1)S(1)} %collective-permute-done.8.refs_7_) | copy-start | bytes 331780
  35.5 4.9 %collective-permute-start.9 = (bf16[96,576]{1,0:T(8,128)(2,1)S(1)}, bf16[96,576]{1,0:T(8,128)(2,1)S(1)}, u32[]{:S(2)}, u32[]{:S(2)}) collective-permute-start(bf16[96,576]{1,0:T(8,128)(2,1)S(1)} %collective-permute-done.8.refs_7_), channel_id=1, source_target_pairs={{0,4},{4,0},{8,12},{12,8},{16,20},{20,16},{24,28},{28,24},{1,5},{5... | collective-permute-start | bytes 331784 | tf_op jit(solution)/shard_map/ppermute | solution.py:635
  40.2 8.1 %collective-permute-start = (bf16[768,512]{1,0:T(8,128)(2,1)}, bf16[768,512]{1,0:T(8,128)(2,1)S(1)}, u32[]{:S(2)}, u32[]{:S(2)}) collective-permute-start(bf16[768,512]{1,0:T(8,128)(2,1)} %turn.2.refs_0_), channel_id=1, source_target_pairs={{0,1},{1,0},{2,3},{3,2},{4,5},{5,4},{6,7},{7,6},{8,9},{9,8},{10,11... | collective-permute-start | bytes 2359304 | tf_op jit(solution)/shard_map/ppermute | solution.py:635
  41.1 0.9 copy-start
  41.9 22.0 %collective-permute-start.11 = (bf16[768,512]{1,0:T(8,128)(2,1)}, bf16[768,512]{1,0:T(8,128)(2,1)S(1)}, u32[]{:S(2)}, u32[]{:S(2)}) collective-permute-start(bf16[768,512]{1,0:T(8,128)(2,1)} %gate.1.refs_15_.refs_4_), channel_id=1, source_target_pairs={{0,2},{1,3},{2,0},{3,1},{4,6},{5,7},{6,4},{7,5},{8,10},{9,11},{10,... | collective-permute-start | bytes 2359304 | tf_op jit(solution)/shard_map/ppermute | solution.py:635
  42.4 5.9 %collective-permute-start.2 = (bf16[768,512]{1,0:T(8,128)(2,1)}, bf16[768,512]{1,0:T(8,128)(2,1)S(1)}, u32[]{:S(2)}, u32[]{:S(2)}) collective-permute-start(bf16[768,512]{1,0:T(8,128)(2,1)} %copy-done), channel_id=1, source_target_pairs={{0,1},{1,0},{2,3},{3,2},{4,5},{5,4},{6,7},{7,6},{8,9},{9,8},{10,11... | collective-permute-start | bytes 2359304 | tf_op jit(solution)/shard_map/ppermute | solution.py:635
  47.9 29.1 %collective-permute-start.10 = (bf16[768,512]{1,0:T(8,128)(2,1)}, bf16[768,512]{1,0:T(8,128)(2,1)S(1)}, u32[]{:S(2)}, u32[]{:S(2)}) collective-permute-start(bf16[768,512]{1,0:T(8,128)(2,1)} %gate.1.refs_15_.refs_4_), channel_id=1, source_target_pairs={{0,1},{1,0},{2,3},{3,2},{4,5},{5,4},{6,7},{7,6},{8,9},{9,8},{10,11... | collective-permute-start | bytes 2359304 | tf_op jit(solution)/shard_map/ppermute | solution.py:635
  48.3 0.9 copy-start.1
  48.3 1.2 copy-start.2
  64.0 0.9 copy-start.30
  70.9 6.2 %collective-permute-start.12 = (bf16[768,512]{1,0:T(8,128)(2,1)}, bf16[768,512]{1,0:T(8,128)(2,1)S(1)}, u32[]{:S(2)}, u32[]{:S(2)}) collective-permute-start(bf16[768,512]{1,0:T(8,128)(2,1)} %get-tuple-element.46.refs_6_), channel_id=1, source_target_pairs={{0,1},{1,0},{2,3},{3,2},{4,5},{5,4},{6,7},{7,6},{8,9},{9,8},{10,11... | collective-permute-start | bytes 2359304 | tf_op jit(solution)/shard_map/ppermute | solution.py:635
  77.1 0.9 copy-start.32
  77.1 1.2 copy-start.33
  113.6 10.7 %collective-permute-start.14 = (bf16[768,512]{1,0:T(8,128)(2,1)}, bf16[768,512]{1,0:T(8,128)(2,1)S(1)}, u32[]{:S(2)}, u32[]{:S(2)}) collective-permute-start(bf16[768,512]{1,0:T(8,128)(2,1)} %get-tuple-element.52), channel_id=1, source_target_pairs={{0,1},{1,0},{2,3},{3,2},{4,5},{5,4},{6,7},{7,6},{8,9},{9,8},{10,11... | collective-permute-start | bytes 2359304 | tf_op jit(solution)/shard_map/ppermute | solution.py:635
  114.0 10.2 %copy-start.3 = (bf16[768,512]{1,0:T(8,128)(2,1)S(1)}, bf16[768,512]{1,0:T(8,128)(2,1)}, u32[]{:S(2)}) copy-start(bf16[768,512]{1,0:T(8,128)(2,1)} %get-tuple-element.51) | copy-start | bytes 2359300
  124.5 1.6 copy-start.4
  124.5 22.4 %collective-permute-start.15 = (bf16[768,512]{1,0:T(8,128)(2,1)S(1)}, bf16[768,512]{1,0:T(8,128)(2,1)S(1)}, u32[]{:S(2)}, u32[]{:S(2)}) collective-permute-start(bf16[768,512]{1,0:T(8,128)(2,1)S(1)} %add_convert_fusion.refs_0_), channel_id=1, source_target_pairs={{0,2},{1,3},{2,0},{3,1},{4,6},{5,7},{6,4},{7,5},{8,10},{9,11},{10,... | collective-permute-start | bytes 2359304 | tf_op jit(solution)/shard_map/ppermute | solution.py:635
  146.9 0.9 copy-start.26
  163.7 7.8 %copy-start.27 = (bf16[768,512]{1,0:T(8,128)(2,1)S(1)}, bf16[768,512]{1,0:T(8,128)(2,1)}, u32[]{:S(2)}) copy-start(bf16[768,512]{1,0:T(8,128)(2,1)} %get-tuple-element.59) | copy-start | bytes 2359300
  163.8 8.9 %copy-start.16 = (f32[768]{0:T(1024)S(1)}, f32[768]{0:T(1024)}, u32[]{:S(2)}) copy-start(f32[768]{0:T(1024)} %param.25) | copy-start | bytes 9220
  163.8 8.9 %copy-start.17 = (f32[768]{0:T(1024)S(1)}, f32[768]{0:T(1024)}, u32[]{:S(2)}) copy-start(f32[768]{0:T(1024)} %param.29) | copy-start | bytes 9220
  163.8 2.6 %collective-permute-start.17 = (bf16[768,512]{1,0:T(8,128)(2,1)}, bf16[768,512]{1,0:T(8,128)(2,1)S(1)}, u32[]{:S(2)}, u32[]{:S(2)}) collective-permute-start(bf16[768,512]{1,0:T(8,128)(2,1)} %get-tuple-element.61), channel_id=1, source_target_pairs={{0,1},{1,0},{2,3},{3,2},{4,5},{5,4},{6,7},{7,6},{8,9},{9,8},{10,11... | collective-permute-start | bytes 2359304 | tf_op jit(solution)/shard_map/ppermute | solution.py:635
  163.9 14.2 %collective-permute-start.19 = (bf16[384,576]{1,0:T(8,128)(2,1)}, bf16[384,576]{1,0:T(8,128)(2,1)S(1)}, u32[]{:S(2)}, u32[]{:S(2)}) collective-permute-start(bf16[384,576]{1,0:T(8,128)(2,1)} %get-tuple-element.66), channel_id=1, source_target_pairs={{0,4},{4,0},{8,12},{12,8},{16,20},{20,16},{24,28},{28,24},{1,5},{5... | collective-permute-start | bytes 1327112 | tf_op jit(solution)/shard_map/ppermute | solution.py:635
  166.3 0.9 copy-start.34
  169.7 2.3 collective-permute-start.23
  169.8 3.9 %collective-permute-start.24 = (f32[4,768]{1,0:T(4,128)}, f32[4,768]{1,0:T(4,128)S(1)}, u32[]{:S(2)}, u32[]{:S(2)}) collective-permute-start(f32[4,768]{1,0:T(4,128)} %get-tuple-element.71), channel_id=1, source_target_pairs={{0,2},{1,3},{2,0},{3,1},{4,6},{5,7},{6,4},{7,5},{8,10},{9,11},{10,... | collective-permute-start | bytes 36872 | tf_op jit(solution)/shard_map/ppermute | solution.py:635
  170.5 3.3 %collective-permute-start.25 = (f32[4,768]{1,0:T(4,128)}, f32[4,768]{1,0:T(4,128)S(1)}, u32[]{:S(2)}, u32[]{:S(2)}) collective-permute-start(f32[4,768]{1,0:T(4,128)} %get-tuple-element.71), channel_id=1, source_target_pairs={{0,3},{1,2},{2,1},{3,0},{4,7},{5,6},{6,5},{7,4},{8,11},{9,10},{10,... | collective-permute-start | bytes 36872 | tf_op jit(solution)/shard_map/ppermute | solution.py:635
  171.5 26.0 %collective-permute-start.16 = (bf16[768,512]{1,0:T(8,128)(2,1)S(1)}, bf16[768,512]{1,0:T(8,128)(2,1)S(1)}, u32[]{:S(2)}, u32[]{:S(2)}) collective-permute-start(bf16[768,512]{1,0:T(8,128)(2,1)S(1)} %copy-done.27), channel_id=1, source_target_pairs={{0,1},{1,0},{2,3},{3,2},{4,5},{5,4},{6,7},{7,6},{8,9},{9,8},{10,11... | collective-permute-start | bytes 2359304 | tf_op jit(solution)/shard_map/ppermute | solution.py:635
  172.0 27.6 %collective-permute-start.18 = (bf16[768,512]{1,0:T(8,128)(2,1)}, bf16[768,512]{1,0:T(8,128)(2,1)S(1)}, u32[]{:S(2)}, u32[]{:S(2)}) collective-permute-start(bf16[768,512]{1,0:T(8,128)(2,1)} %get-tuple-element.64), channel_id=1, source_target_pairs={{0,2},{1,3},{2,0},{3,1},{4,6},{5,7},{6,4},{7,5},{8,10},{9,11},{10,... | collective-permute-start | bytes 2359304 | tf_op jit(solution)/shard_map/ppermute | solution.py:635
  175.3 17.7 %collective-permute-start.26 = (f32[8,768]{1,0:T(8,128)S(1)}, f32[8,768]{1,0:T(8,128)S(1)}, u32[]{:S(2)}, u32[]{:S(2)}) collective-permute-start(f32[8,768]{1,0:T(8,128)S(1)} %pad_maximum_fusion.1), channel_id=1, source_target_pairs={{0,4},{4,0},{8,12},{12,8},{16,20},{20,16},{24,28},{28,24},{1,5},{5... | collective-permute-start | bytes 73736 | tf_op jit(solution)/shard_map/ppermute | solution.py:635
  178.9 15.6 %copy-start.13 = (f32[4,768]{1,0:T(4,128)S(1)}, f32[4,768]{1,0:T(4,128)}, u32[]{:S(2)}) copy-start(f32[4,768]{1,0:T(4,128)} %get-tuple-element.72) | copy-start | bytes 36868
  180.9 16.6 %collective-permute-start.20 = (bf16[96,576]{1,0:T(8,128)(2,1)}, bf16[96,576]{1,0:T(8,128)(2,1)S(1)}, u32[]{:S(2)}, u32[]{:S(2)}) collective-permute-start(bf16[96,576]{1,0:T(8,128)(2,1)} %get-tuple-element.68), channel_id=1, source_target_pairs={{0,8},{4,12},{8,0},{12,4},{16,24},{20,28},{24,16},{28,20},{1,9},{5... | collective-permute-start | bytes 331784 | tf_op jit(solution)/shard_map/ppermute | solution.py:635
  190.8 17.2 %collective-permute-start.21 = (bf16[96,576]{1,0:T(8,128)(2,1)}, bf16[96,576]{1,0:T(8,128)(2,1)S(1)}, u32[]{:S(2)}, u32[]{:S(2)}) collective-permute-start(bf16[96,576]{1,0:T(8,128)(2,1)} %get-tuple-element.69), channel_id=1, source_target_pairs={{0,16},{4,20},{8,24},{12,28},{16,0},{20,4},{24,8},{28,12},{1,17},{... | collective-permute-start | bytes 331784 | tf_op jit(solution)/shard_map/ppermute | solution.py:635
  193.0 15.1 %collective-permute-start.22 = (bf16[96,576]{1,0:T(8,128)(2,1)}, bf16[96,576]{1,0:T(8,128)(2,1)S(1)}, u32[]{:S(2)}, u32[]{:S(2)}) collective-permute-start(bf16[96,576]{1,0:T(8,128)(2,1)} %get-tuple-element.70), channel_id=1, source_target_pairs={{0,24},{4,28},{8,16},{12,20},{16,8},{20,12},{24,0},{28,4},{1,25},{... | collective-permute-start | bytes 331784 | tf_op jit(solution)/shard_map/ppermute | solution.py:635
  194.5 13.5 %copy-start.14 = (f32[8,768]{1,0:T(8,128)}, f32[8,768]{1,0:T(8,128)S(1)}, u32[]{:S(2)}) copy-start(f32[8,768]{1,0:T(8,128)S(1)} %fusion.2.refs_3_) | copy-start | bytes 73732
  197.5 10.4 %copy-start.36 = (bf16[96,576]{1,0:T(8,128)(2,1)}, bf16[96,576]{1,0:T(8,128)(2,1)S(1)}, u32[]{:S(2)}) copy-start(bf16[96,576]{1,0:T(8,128)(2,1)S(1)} %collective-permute-done.20.refs_0_) | copy-start | bytes 331780
  197.5 10.6 %collective-permute-start.27 = (f32[8,768]{1,0:T(8,128)S(1)}, f32[8,768]{1,0:T(8,128)S(1)}, u32[]{:S(2)}, u32[]{:S(2)}) collective-permute-start(f32[8,768]{1,0:T(8,128)S(1)} %fusion.2.refs_3_), channel_id=1, source_target_pairs={{0,8},{4,12},{8,0},{12,4},{16,24},{20,28},{24,16},{28,20},{1,9},{5... | collective-permute-start | bytes 73736 | tf_op jit(solution)/shard_map/ppermute | solution.py:635
  197.6 4.4 %copy-start.28 = (bf16[768,512]{1,0:T(8,128)(2,1)}, bf16[768,512]{1,0:T(8,128)(2,1)S(1)}, u32[]{:S(2)}) copy-start(bf16[768,512]{1,0:T(8,128)(2,1)S(1)} %collective-permute-done.16.near_ref) | copy-start | bytes 2359300
  197.6 10.6 %collective-permute-start.28 = (f32[8,768]{1,0:T(8,128)S(1)}, f32[8,768]{1,0:T(8,128)S(1)}, u32[]{:S(2)}, u32[]{:S(2)}) collective-permute-start(f32[8,768]{1,0:T(8,128)S(1)} %fusion.2.refs_3_), channel_id=1, source_target_pairs={{0,16},{4,20},{8,24},{12,28},{16,0},{20,4},{24,8},{28,12},{1,17},{... | collective-permute-start | bytes 73736 | tf_op jit(solution)/shard_map/ppermute | solution.py:635
  199.6 2.4 %copy-start.29 = (bf16[768,512]{1,0:T(8,128)(2,1)}, bf16[768,512]{1,0:T(8,128)(2,1)S(1)}, u32[]{:S(2)}) copy-start(bf16[768,512]{1,0:T(8,128)(2,1)S(1)} %collective-permute-done.18.far_ref) | copy-start | bytes 2359300
  199.6 8.6 %collective-permute-start.29 = (f32[8,768]{1,0:T(8,128)S(1)}, f32[8,768]{1,0:T(8,128)S(1)}, u32[]{:S(2)}, u32[]{:S(2)}) collective-permute-start(f32[8,768]{1,0:T(8,128)S(1)} %fusion.2.refs_3_), channel_id=1, source_target_pairs={{0,24},{4,28},{8,16},{12,20},{16,8},{20,12},{24,0},{28,4},{1,25},{... | collective-permute-start | bytes 73736 | tf_op jit(solution)/shard_map/ppermute | solution.py:635
  201.9 6.1 %copy-start.25 = (bf16[768,512]{1,0:T(8,128)(2,1)S(1)}, bf16[768,512]{1,0:T(8,128)(2,1)}, u32[]{:S(2)}) copy-start(bf16[768,512]{1,0:T(8,128)(2,1)} %get-tuple-element.50) | copy-start | bytes 2359300
  208.0 6.0 %collective-permute-start.13 = (bf16[768,512]{1,0:T(8,128)(2,1)S(1)}, bf16[768,512]{1,0:T(8,128)(2,1)S(1)}, u32[]{:S(2)}, u32[]{:S(2)}) collective-permute-start(bf16[768,512]{1,0:T(8,128)(2,1)S(1)} %copy-done.25), channel_id=1, source_target_pairs={{0,1},{1,0},{2,3},{3,2},{4,5},{5,4},{6,7},{7,6},{8,9},{9,8},{10,11... | collective-permute-start | bytes 2359304 | tf_op jit(solution)/shard_map/ppermute | solution.py:635
  212.0 11.2 %copy-start.24 = (f32[24]{0:T(128)}, f32[24]{0:T(128)S(1)}, u32[]{:S(2)}) copy-start(f32[24]{0:T(128)S(1)} %get-tuple-element.118) | copy-start | bytes 292
  214.0 0.9 copy-start.31
  (10 other events, 6.6 us)
Sparse Core Ops, SparseCore 0:
  10.2 64.5 all-gather.1
  114.2 79.8 reduce-scatter.1

commit v3 on v2

--- a/solution.py
+++ b/solution.py
@@ -19,6 +19,7 @@
 BF16 = jnp.bfloat16
 VMEM_LIMIT = 56 * 1024 * 1024
 MICROSECOND = 1_150_000_000
+CHUNK = 768
 
 
 def dot(left, right):
@@ -93,6 +94,10 @@
     return turn_back(order, held, total)[0:8, :]
 
 
+def by_unit(along, level, col_ref, index):
+    return (along - level * column(col_ref, index + 1)) / column(col_ref, index)
+
+
 def kept(items):
     return [pl.BlockSpec(memory_space=pl.ANY) for _ in items]
 
@@ -130,9 +135,6 @@
     for here, there in blocks_of(order, grads.shape[0]):
         held[there, :] = grads[here, :]
     return held[...].T
-
-
-NORM_ROWS = 4
 
 
 def stand_kernel(order, rows_ref, *refs):
@@ -145,7 +147,7 @@
     for index in range(count):
         first = pl.multiple_of(order[index] * size, size)
         here = slice(index * size, (index + 1) * size)
-        out_ref[here, :] = jnp.where(lane < NORM_ROWS, held[pl.ds(first, size), :], held[here, :])
+        out_ref[here, :] = jnp.where((lane < 4) | (lane == 6), held[pl.ds(first, size), :], held[here, :])
 
 
 def stand(order, rows, wait):
@@ -165,7 +167,7 @@
 def project_kernel(count, place, *refs):
     x_refs, pieces, refs = refs[:4], refs[4 : 4 + count], refs[4 + count :]
     col_ref, cos_ref, sin_ref = refs[:3]
-    out_ref, x_now, wt = refs[-3:]
+    out_ref, one_ref, two_ref, x_now, wt = refs[-5:]
     step = pl.program_id(0)
     cols = out_ref.shape[0]
 
@@ -175,10 +177,13 @@
 
     unit = standardize(choose(x_refs, step, x_now))
     normed = (unit * column(col_ref, 0) + column(col_ref, 1)).astype(BF16)
+    one_ref[0] = normed
+    two_ref[0] = (unit * column(col_ref, 2) + column(col_ref, 3)).astype(BF16)
     cosine, sine = cos_ref[...], sin_ref[...]
+    joined = dot(wt[...], normed) + col_ref[:cols, 5:6]
     for head in range(cols // (3 * HEAD)):
         base = head * 3 * HEAD
-        mixed = dot(wt[base : base + 3 * HEAD, :], normed) + col_ref[base : base + 3 * HEAD, 5:6]
+        mixed = joined[base : base + 3 * HEAD, :]
         for part, factor in ((0, SCALE), (HEAD, 1.0)):
             one, two = mixed[part : part + HALF], mixed[part + HALF : part + ROT]
             turned = jnp.concatenate(
@@ -198,8 +203,16 @@
         (len(x_all),),
         [whole_spec(item.shape) for item in (*x_all, *pieces, columns)]
         + [pl.BlockSpec((HALF, slab), by_place), pl.BlockSpec((HALF, slab), by_place), *kept(wait)],
-        pl.BlockSpec((cols, slab), by_place),
-        jax.ShapeDtypeStruct((cols, len(x_all) * slab), BF16),
+        [
+            pl.BlockSpec((cols, slab), by_place),
+            pl.BlockSpec((1, width, slab), lambda s, t: (s, 0, 0)),
+            pl.BlockSpec((1, width, slab), lambda s, t: (s, 0, 0)),
+        ],
+        [
+            jax.ShapeDtypeStruct((cols, len(x_all) * slab), BF16),
+            jax.ShapeDtypeStruct((len(x_all), width, slab), BF16),
+            jax.ShapeDtypeStruct((len(x_all), width, slab), BF16),
+        ],
         [pltpu.VMEM((width, slab), BF16), pltpu.VMEM((cols, width), BF16)],
         "project",
         prefetch=1,
@@ -219,6 +232,18 @@
     return jnp.where(allowed, scores, NEG)
 
 
+def key_parts(begin, block):
+    half = block // 2
+    parts = [(first, block, 0) for first in range(0, begin, block)]
+    return parts + [(begin, half, 0), (begin + half, half, half)]
+
+
+def widen(values, skip, fill):
+    if not skip:
+        return values
+    return jnp.concatenate([jnp.full((values.shape[0], skip), fill, values.dtype), values], axis=1)
+
+
 def attend_kernel(handed, start_ref, qkv_ref, *refs):
     out_ref, lse_ref = refs[-4 - handed : len(refs) - 2 - handed]
     keys, held = refs[-2:]
@@ -229,16 +254,17 @@
         here = slice(begin, begin + block)
         queries, starts = qkv_ref[0:HEAD, here], start_ref[0:1, here]
         top = jnp.full((1, block), NEG, F32)
-        for first in range(0, begin + block, block):
-            scores = masked(dot(keys[first : first + block, :], queries), first, begin, starts)
-            held[first : first + block, :] = scores
-            top = jnp.maximum(top, jnp.max(scores, axis=0, keepdims=True))
+        for first, count, skip in key_parts(begin, block):
+            scores = masked(dot(keys[first : first + count, :], queries[:, skip:]), first, begin + skip, starts[:, skip:])
+            held[first : first + count, skip:] = scores
+            top = jnp.maximum(top, widen(jnp.max(scores, axis=0, keepdims=True), skip, NEG))
         total = jnp.zeros((1, block), F32)
         result = jnp.zeros((HEAD, block), F32)
-        for first in range(0, begin + block, block):
-            expo = jnp.exp(held[first : first + block, :] - top)
-            total += jnp.sum(expo, axis=0, keepdims=True)
-            result += dot(qkv_ref[2 * HEAD : 3 * HEAD, first : first + block], expo.astype(BF16))
+        for first, count, skip in key_parts(begin, block):
+            expo = jnp.exp(held[first : first + count, skip:] - top[:, skip:])
+            total += widen(jnp.sum(expo, axis=0, keepdims=True), skip, 0.0)
+            part = dot(qkv_ref[2 * HEAD : 3 * HEAD, first : first + count], expo.astype(BF16))
+            result += widen(part, skip, 0.0)
         out_ref[:, here] = (result / total).astype(BF16)
         lse_ref[0, 0:1, here] = top + jnp.log(total)
 
@@ -285,14 +311,14 @@
         inner = jnp.sum(grads.astype(F32) * out_ref[:, here].astype(F32), axis=0, keepdims=True)
         query_rows, grad_rows = queries.T, grads.T
         query_sum = jnp.zeros((HEAD, block), F32)
-        for first in range(0, begin + block, block):
-            there = slice(first, first + block)
-            scores = masked(dot(keys[there, :], queries), first, begin, starts)
-            probs = jnp.exp(scores - lse)
-            score_grads = (probs * (dot(values[there, :], grads) - inner)).astype(BF16)
-            query_sum += dot(qkv_ref[HEAD : 2 * HEAD, there], score_grads)
-            key_sum[there, :] += dot(score_grads, query_rows)
-            value_sum[there, :] += dot(probs.astype(BF16), grad_rows)
+        for first, count, skip in key_parts(begin, block):
+            there = slice(first, first + count)
+            scores = masked(dot(keys[there, :], queries[:, skip:]), first, begin + skip, starts[:, skip:])
+            probs = jnp.exp(scores - lse[:, skip:])
+            score_grads = (probs * (dot(values[there, :], grads[:, skip:]) - inner[:, skip:])).astype(BF16)
+            query_sum += widen(dot(qkv_ref[HEAD : 2 * HEAD, there], score_grads), skip, 0.0)
+            key_sum[there, :] += dot(score_grads, query_rows[skip:, :])
+            value_sum[there, :] += dot(probs.astype(BF16), grad_rows[skip:, :])
         put_unrotated(0, here, query_sum * SCALE)
     put_unrotated(HEAD, slice(0, rows), key_sum[...].T)
     mixed_ref[2 * HEAD : 3 * HEAD, :] = value_sum[...].T.astype(BF16)
@@ -323,11 +349,11 @@
 
 
 def feed_kernel(place, order, *refs):
-    x_refs, dy_refs, refs = refs[:4], refs[4:8], refs[8:]
-    weight_ref, att_refs, refs = refs[0], refs[1:-22], refs[-22:]
+    dy_refs, refs = refs[:4], refs[4:]
+    two_ref, weight_ref, att_refs, refs = refs[0], refs[1], refs[2:-21], refs[-21:]
     col_ref, *refs = refs
     branch_refs, (normed_ref, att_grad_ref, weights_ref, vector_ref), refs = refs[:4], refs[4:8], refs[8:]
-    x_now, dy_now, up, down, dense, up_t, down_t, dense_t, active, hidden_grad, sums, vectors, held = refs
+    dy_now, up, down, dense, up_t, down_t, dense_t, active, hidden_grad, sums, vectors, held = refs
     step = pl.program_id(0)
     hidden_count = up.shape[1]
     dense_count = dense.shape[1]
@@ -344,12 +370,11 @@
         sums[...] = jnp.zeros_like(sums)
         vectors[...] = jnp.zeros_like(vectors)
 
-    unit = standardize(choose(x_refs, step, x_now))
     dy = choose(dy_refs, step, dy_now)
-    normed = (unit * column(col_ref, 2) + column(col_ref, 3)).astype(BF16)
+    normed = two_ref[0]
     attended = jnp.concatenate([ref[...] for ref in att_refs], axis=0)
     att_grad_ref[...] = dot(dense_t[...], dy).astype(BF16)
-    chunk = min(256, hidden_count)
+    chunk = min(CHUNK, hidden_count)
     for first in range(0, hidden_count, chunk):
         units = slice(first, first + chunk)
         hidden = dot(up_t[units, :], normed) + col_ref[units, 4:5]
@@ -371,8 +396,8 @@
             ref[...] = branch
 
     normed_grad = dot(up[...], hidden_grad[...])
-    normed_ref[0] = normed_grad * column(col_ref, 2)
-    vectors[0] += fold(normed_grad * unit)
+    normed_ref[0] = (normed_grad * column(col_ref, 2)).astype(BF16)
+    vectors[0] += fold(normed_grad * normed.astype(F32))
     vectors[1] += fold(normed_grad)
     vectors[2] += fold(dy.astype(F32))
 
@@ -380,13 +405,14 @@
     def _():
         for here, there in blocks_of(order, sums.shape[0]):
             weights_ref[there, :] = sums[here, :].astype(BF16)
-        rows = as_rows([vectors[0], vectors[1], vectors[2]], order, held)
+        gains = by_unit(vectors[0], vectors[1], col_ref, 2)
+        rows = as_rows([gains, vectors[1], vectors[2]], order, held)
         vector_ref[...] = jnp.concatenate([rows[0:3], as_rows([vectors[3]])[0:5]], axis=0)
 
 
-def feed(place, order, x_all, dy_all, weights, attended, columns):
-    width, slab = x_all[0].shape
-    parts = len(x_all)
+def feed(place, order, dy_all, normed, weights, attended, columns):
+    width, slab = dy_all[0].shape
+    parts = len(dy_all)
     dense_count = sum(item.shape[0] for item in attended)
     hidden_count = (weights.shape[1] - dense_count) // 2
     grad_cols = 2 * hidden_count + dense_count
@@ -394,7 +420,8 @@
     return call(
         feed_kernel,
         (parts,),
-        [whole_spec(item.shape) for item in (*x_all, *dy_all, weights)]
+        [whole_spec(item.shape) for item in dy_all]
+        + [pl.BlockSpec((1, width, slab), lambda s, *_: (s, 0, 0)), whole_spec(weights.shape)]
         + [pl.BlockSpec((item.shape[0], slab), by_place) for item in attended]
         + [whole_spec(columns.shape)],
         [whole_spec((width, slab))] * parts
@@ -406,13 +433,12 @@
         ],
         [jax.ShapeDtypeStruct((width, slab), BF16)] * parts
         + [
-            jax.ShapeDtypeStruct((parts, width, slab), F32),
+            jax.ShapeDtypeStruct((parts, width, slab), BF16),
             jax.ShapeDtypeStruct((dense_count, parts * slab), BF16),
             jax.ShapeDtypeStruct((width, grad_cols), BF16),
             jax.ShapeDtypeStruct((8, hidden_count), F32),
         ],
         [
-            pltpu.VMEM((width, slab), BF16),
             pltpu.VMEM((width, slab), BF16),
             pltpu.VMEM((width, hidden_count), BF16),
             pltpu.VMEM((width, hidden_count), BF16),
@@ -429,15 +455,15 @@
         "feed",
         prefetch=2,
         work=30 * MICROSECOND,
-    )(place, order, *x_all, *dy_all, weights, *attended, columns)
+    )(place, order, *dy_all, normed, weights, *attended, columns)
 
 
 def project_back_kernel(count, heads, place, order, *refs):
-    x_refs, pieces, refs = refs[:4], refs[4 : 4 + count], refs[4 + count :]
+    one_ref, pieces, refs = refs[0], refs[1 : 1 + count], refs[1 + count :]
     mixed_refs, refs = refs[:heads], refs[heads:]
-    part_ref, col_ref, refs = refs[0], refs[1], refs[-13:]
+    part_ref, col_ref, refs = refs[0], refs[1], refs[-12:]
     unit_refs, (own_ref, sent_ref, vector_ref), refs = refs[:4], refs[4:7], refs[7:]
-    x_now, w, sums, vectors, counts, held = refs
+    w, sums, vectors, counts, held = refs
     step = pl.program_id(0)
 
     @pl.when(step == 0)
@@ -447,20 +473,19 @@
         vectors[...] = jnp.zeros_like(vectors)
         counts[...] = jnp.zeros_like(counts)
 
-    unit = standardize(choose(x_refs, step, x_now))
-    normed = (unit * column(col_ref, 0) + column(col_ref, 1)).astype(BF16)
+    normed = one_ref[0]
     mixed = jnp.concatenate([ref[...] for ref in mixed_refs], axis=0)
     sums[...] += dot_nt(normed, mixed)
     counts[...] += fold(mixed.astype(F32))
     normed_grad = dot(w[...], mixed)
-    total = (part_ref[0] + normed_grad * column(col_ref, 0)).astype(BF16)
+    total = (part_ref[0].astype(F32) + normed_grad * column(col_ref, 0)).astype(BF16)
     for index, ref in enumerate(unit_refs):
 
         @pl.when(step == index)
         def _(ref=ref):
             ref[...] = total
 
-    vectors[0] += fold(normed_grad * unit)
+    vectors[0] += fold(normed_grad * normed.astype(F32))
     vectors[1] += fold(normed_grad)
 
     @pl.when(step == pl.num_programs(0) - 1)
@@ -468,20 +493,21 @@
         half = own_ref.shape[0]
         own_ref[...] = sums[:half, :].astype(BF16)
         sent_ref[...] = sums[half:, :].astype(BF16)
-        rows = as_rows([vectors[0], vectors[1]], order, held)
+        gains = by_unit(vectors[0], vectors[1], col_ref, 0)
+        rows = as_rows([gains, vectors[1]], order, held)
         tail = as_rows([counts[...]])[0:6]
         tail = jnp.concatenate([tail, jnp.zeros((6, rows.shape[1] - tail.shape[1]), F32)], axis=1)
         vector_ref[...] = jnp.concatenate([rows[0:2], tail], axis=0)
 
 
-def project_back(place, order, x_all, pieces, mixed, part, columns, wait):
-    width, slab = x_all[0].shape
-    parts = len(x_all)
+def project_back(place, order, normed, pieces, mixed, part, columns, wait):
+    parts, width, slab = normed.shape
     cols = sum(item.shape[0] for item in mixed)
     return call(
         functools.partial(project_back_kernel, len(pieces), len(mixed)),
         (parts,),
-        [whole_spec(item.shape) for item in (*x_all, *pieces)]
+        [pl.BlockSpec((1, width, slab), lambda s, *_: (s, 0, 0))]
+        + [whole_spec(item.shape) for item in pieces]
         + [pl.BlockSpec((item.shape[0], slab), lambda s, t, _: (0, s ^ t[0])) for item in mixed]
         + [pl.BlockSpec((1, width, slab), lambda s, *_: (s, 0, 0)), whole_spec(columns.shape)]
         + kept(wait),
@@ -498,7 +524,6 @@
             jax.ShapeDtypeStruct((8, width), F32),
         ],
         [
-            pltpu.VMEM((width, slab), BF16),
             pltpu.VMEM((width, cols), BF16),
             pltpu.VMEM((width, cols), F32),
             pltpu.VMEM((2, width, 128), F32),
@@ -508,67 +533,64 @@
         "project_back",
         prefetch=2,
         work=13 * MICROSECOND,
-    )(place, order, *x_all, *pieces, *mixed, part, columns, *wait)
-
-
-def finish_out_kernel(order, own_ref, near_ref, far_ref, rows_ref, bias_ref, *refs):
+    )(place, order, normed, *pieces, *mixed, part, columns, *wait)
+
+
+def finish_out_kernel(order, own_ref, near_ref, far_ref, x_ref, bias_ref, *refs):
     out_ref, held = refs[-2:]
     branch = own_ref[...].astype(F32) + near_ref[...].astype(F32) + far_ref[...].astype(F32)
-    branch = turn_back(order, held, branch)
-    out_ref[...] = (rows_ref[...].astype(F32) + branch + bias_ref[...]).astype(BF16)
-
-
-def finish(kernel, order, summands, rows, others, kind, name, work, wait=()):
-    count, width = rows.shape
-    part = min(128, count)
-    rows_block = pl.BlockSpec((part, width), lambda i, _: (i, 0))
+    out = (x_ref[...].astype(F32) + branch + column(bias_ref, 6)).astype(BF16)
+    out_ref[...] = turn_back(order, held, out)
+
+
+def finish_grad_kernel(order, own_ref, near_ref, far_ref, x_ref, dy_ref, *refs):
+    out_ref, held = refs[-2:]
+    grads = own_ref[...].astype(F32) + near_ref[...].astype(F32) + far_ref[...].astype(F32)
+    values = x_ref[...].astype(F32)
+    center = values - jnp.mean(values, axis=0, keepdims=True)
+    scale = lax.rsqrt(jnp.mean(center * center, axis=0, keepdims=True) + EPS)
+    unit = center * scale
+    along = jnp.mean(grads * unit, axis=0, keepdims=True)
+    level = jnp.mean(grads, axis=0, keepdims=True)
+    out = dy_ref[...].astype(F32) + scale * (grads - level - unit * along)
+    out_ref[...] = turn_back(order, held, out)
+
+
+def finish(kernel, order, summands, own, other, kind, name, work, wait=()):
+    width, count = own.shape
+    part = min(256, count)
+    block = pl.BlockSpec((width, part), lambda i, _: (0, i))
     return call(
         kernel,
         (count // part,),
-        [pl.BlockSpec((width, part), lambda i, _: (0, i))] * len(summands)
-        + [rows_block]
-        + [rows_block if item.shape == rows.shape else whole_spec(item.shape) for item in others]
+        [block] * (len(summands) + 1)
+        + [block if other.shape == own.shape else whole_spec(other.shape)]
         + kept(wait),
-        rows_block,
-        jax.ShapeDtypeStruct(rows.shape, kind),
-        [pltpu.VMEM((width, part), F32)],
+        pl.BlockSpec((part, width), lambda i, _: (i, 0)),
+        jax.ShapeDtypeStruct((count, width), kind),
+        [pltpu.VMEM((width, part), kind)],
         name,
         prefetch=1,
         work=work * MICROSECOND,
-    )(order, *summands, rows, *others, *wait)
-
-
-def finish_grad_kernel(order, own_ref, near_ref, far_ref, rows_ref, dy_ref, out_ref, held):
-    grads = own_ref[...].astype(F32) + near_ref[...].astype(F32) + far_ref[...].astype(F32)
-    grads = turn_back(order, held, grads)
-    rows = rows_ref[...].astype(F32)
-    center = rows - jnp.mean(rows, axis=1, keepdims=True)
-    scale = lax.rsqrt(jnp.mean(center * center, axis=1, keepdims=True) + EPS)
-    unit = center * scale
-    along = jnp.mean(grads * unit, axis=1, keepdims=True)
-    level = jnp.mean(grads, axis=1, keepdims=True)
-    out_ref[...] = dy_ref[...].astype(F32) + scale * (grads - level - unit * along)
-
-
-def share_kernel(own_ref, near_ref, last_ref, first_ref, *refs):
-    far_ref, norms_ref, others_ref = refs[-3:]
-    far_ref[...] = (own_ref[...].astype(F32) + near_ref[...].astype(F32)).astype(BF16)
-    norms_ref[...] = jnp.concatenate([last_ref[0:2, :], first_ref[0:2, :]], axis=0)
-    others_ref[...] = jnp.concatenate([first_ref[2:4, :], last_ref[2:4, :]], axis=0)
-
-
-def share(own, near, last, first, wait):
-    pair = (4, last.shape[1])
+    )(order, *summands, own, other, *wait)
+
+
+def share_kernel(own_ref, near_ref, *refs):
+    refs[-1][...] = (own_ref[...].astype(F32) + near_ref[...].astype(F32)).astype(BF16)
+
+
+def share(own, near, wait):
+    width, count = own.shape
+    block = pl.BlockSpec((width, count // 2), lambda i: (0, i))
     return call(
         share_kernel,
-        (1,),
-        [whole_spec(item.shape) for item in (own, near, last, first)] + kept(wait),
-        [whole_spec(own.shape), whole_spec(pair), whole_spec(pair)],
-        [jax.ShapeDtypeStruct(own.shape, BF16), jax.ShapeDtypeStruct(pair, F32), jax.ShapeDtypeStruct(pair, F32)],
+        (2,),
+        [block, block] + kept(wait),
+        block,
+        jax.ShapeDtypeStruct(own.shape, BF16),
         [],
         "share",
-        work=1 * MICROSECOND,
-    )(own, near, last, first, *wait)
+    )(own, near, *wait)
 
 
 def halve_kernel(own_ref, came_ref, *refs):
@@ -579,7 +601,7 @@
         ref[...] = (own_ref[rows, :].astype(F32) + came_ref[rows, :].astype(F32)).astype(ref.dtype)
 
 
-def halve(own, came, wait, work=2):
+def halve(own, came, wait):
     shape = (own.shape[0] // 4, own.shape[1])
     return call(
         halve_kernel,
@@ -589,45 +611,73 @@
         [jax.ShapeDtypeStruct(shape, kind) for kind in (F32, BF16, BF16, BF16)],
         [],
         "halve",
-        work=work * MICROSECOND,
     )(own, came, *wait)
 
 
-def total_kernel(kept_ref, *refs):
-    came, (kept_rows, *came_rows), refs = refs[:3], refs[3:7], refs[7:]
-    out_ref, rows_ref = refs[-2:]
+def parts_kernel(whole_ref, *refs):
+    at = 0
+    for ref in refs[-3:]:
+        ref[...] = whole_ref[:, at : at + ref.shape[1]].astype(F32)
+        at += ref.shape[1]
+
+
+def parts(whole, counts, wait):
+    shapes = [(whole.shape[0], count) for count in counts]
+    return call(
+        parts_kernel,
+        (1,),
+        [whole_spec(whole.shape)] + kept(wait),
+        [whole_spec(shape) for shape in shapes],
+        [jax.ShapeDtypeStruct(shape, F32) for shape in shapes],
+        [],
+        "parts",
+    )(whole, *wait)
+
+
+def total_kernel(at, kept_ref, *refs):
+    came, (kept_rows, *came_rows), refs = refs[:3], refs[3:7], refs[-9:]
+    out_ref, norm_refs, dy_sum_ref, hidden_ref, qkv_ref = refs[0], refs[1:5], refs[5], refs[6], refs[7]
     out_ref[...] = kept_ref[...] + sum(ref[...].astype(F32) for ref in came)
-    rows_ref[...] = kept_rows[...] + sum(ref[...] for ref in came_rows)
-
-
-def total(items, rows, wait):
+    rows = kept_rows[...] + sum(ref[...] for ref in came_rows)
+    width = rows.shape[1]
+    norms = pltpu.roll(rows, width - at[0], 1)
+    for index, ref in enumerate((*norm_refs, dy_sum_ref, refs[8])):
+        row = min(index, 4)
+        ref[...] = norms[row, 0 : ref.shape[0]]
+    hidden_ref[...] = pltpu.roll(rows, width - at[1], 1)[5, 0 : hidden_ref.shape[0]]
+    qkv_ref[...] = pltpu.roll(rows, width - at[2], 1)[6, 0 : qkv_ref.shape[0]]
+
+
+def total(at, items, rows, counts, wait):
+    norm, hidden, qkv = counts
+    shapes = [items[0].shape] + [(norm,)] * 5 + [(hidden,), (qkv,), (norm,)]
     return call(
         total_kernel,
         (1,),
         [whole_spec(item.shape) for item in (*items, *rows)] + kept(wait),
-        [whole_spec(items[0].shape), whole_spec(rows[0].shape)],
-        [jax.ShapeDtypeStruct(items[0].shape, F32), jax.ShapeDtypeStruct(rows[0].shape, F32)],
+        [whole_spec(shape) for shape in shapes],
+        [jax.ShapeDtypeStruct(shape, F32) for shape in shapes],
         [],
         "total",
-        work=1 * MICROSECOND,
-    )(*items, *rows, *wait)
+        prefetch=1,
+    )(at, *items, *rows, *wait)
 
 
 def gate_kernel(*refs):
     pass
 
 
-def gate(item, wait):
+def gate(items, wait):
     return call(
         gate_kernel,
         (1,),
-        kept((item, *wait)),
-        kept((item,))[0],
-        jax.ShapeDtypeStruct(item.shape, item.dtype),
+        kept((*items, *wait)),
+        kept(items),
+        [jax.ShapeDtypeStruct(item.shape, item.dtype) for item in items],
         [],
         "gate",
-        aliases={0: 0},
-    )(item, *wait)
+        aliases={index: index for index in range(len(items))},
+    )(*items, *wait)
 
 
 def swap(value, axis, bits):
@@ -672,7 +722,6 @@
 
 
 def vector_sums(norms, others):
-    norms = norms + swap(norms, "tensor", 1) + swap(norms, "tensor", 2) + swap(norms, "tensor", 3)
     rows = jnp.concatenate([norms, others], axis=0)
     rows = rows + swap(rows, "dp", 1)
     return (rows, *(swap(rows, "dp", bits) for bits in PARTNERS[1:4]))
@@ -707,9 +756,9 @@
     firsts = gather_rows(w_qkv)
     x_all = gather_group(turn(order, tokens))
     weights = lax.all_gather(jnp.concatenate([w_fc1, w_fc2, w_dense], axis=1), "dp", axis=0, tiled=True)
-    rows = jnp.stack([ln1_gain, ln1_bias, ln2_gain, ln2_bias, b_fc1, jnp.pad(b_qkv, (0, width - b_qkv.shape[0]))])
-    columns = stand(order, jnp.pad(rows, ((0, 2), (0, 0))), ())
-    dy_own = gate(turn(order, cotangent), (x_all[2], *firsts[4:]))
+    rows = jnp.stack([ln1_gain, ln1_bias, ln2_gain, ln2_bias, b_fc1, jnp.pad(b_qkv, (0, width - b_qkv.shape[0])), b_dense + b_fc2])
+    columns = stand(order, jnp.pad(rows, ((0, 1), (0, 0))), ())
+    (dy_own,) = gate([turn(order, cotangent)], (x_all[2], *firsts[4:]))
     dy_far, dy_near = swap(dy_own, "tensor", 2), swap(dy_own, "tensor", 1)
 
     row = jnp.arange(group_rows, dtype=jnp.int32)
@@ -721,7 +770,7 @@
     cosine, sine = jnp.cos(angles), jnp.sin(angles)
     starts = starts[None, :]
 
-    qkv = project(place, x_all, firsts, columns, cosine, sine, (dy_own,))
+    qkv, normed_one, normed_two = project(place, x_all, firsts, columns, cosine, sine, (dy_own,))
     heads = range(qkv.shape[0] // (3 * HEAD))
     attended, lse = [], []
     for head in heads:
@@ -733,9 +782,10 @@
             (dy_far,) = through
     dy_all = (dy_own, dy_near, dy_far, swap(dy_far, "tensor", 1))
     *branch, part, att_grad, feed_grads, feed_vectors = feed(
-        place, order, x_all, dy_all, weights, attended, columns
+        place, order, dy_all, normed_two, weights, attended, columns
     )
-    feed_grads = lax.psum_scatter(feed_grads, "dp", scatter_dimension=0, tiled=True).astype(F32)
+    feed_grads = lax.psum_scatter(feed_grads, "dp", scatter_dimension=0, tiled=True)
+    counts = (w_fc1.shape[1], w_fc2.shape[1], w_dense.shape[1])
     out_summands, branch_wait = scatter_group(branch)
 
     mixed_grad = []
@@ -745,48 +795,53 @@
             attend_back(starts, cosine, sine, qkv, att_grad, attended[head], lse[head], head, wait)
         )
     *unit_grad, qkv_own, qkv_sent, last_vectors = project_back(
-        place, order, x_all, firsts, mixed_grad, part, columns, out_summands[2:]
+        place, order, normed_one, firsts, mixed_grad, part, columns, out_summands[2:]
     )
-    far, norms, others = share(
-        unit_grad[2], swap(unit_grad[3], "tensor", 1), last_vectors, feed_vectors, ()
-    )
+    norms = jnp.concatenate([last_vectors[0:2], feed_vectors[0:2]], axis=0)
+    others = jnp.concatenate([feed_vectors[2:4], last_vectors[2:4]], axis=0)
+    if paired():
+        norms = norms + swap(norms, "tensor", 1) + swap(norms, "tensor", 2) + swap(norms, "tensor", 3)
+    else:
+        norms = lax.psum(norms, "tensor")
+    far = share(unit_grad[2], swap(unit_grad[3], "tensor", 1), (norms,))
     summands = (unit_grad[0], swap(unit_grad[1], "tensor", 1), swap(far, "tensor", 2))
     input_grad = finish(
-        finish_grad_kernel, order, summands, tokens, (cotangent,), F32, "finish_grad", 5
+        finish_grad_kernel, order, summands, x_all[0], dy_own, F32, "finish_grad", 0
     )
-    bias = (b_dense + b_fc2)[None, :]
     out = finish(
-        finish_out_kernel, order, out_summands, tokens, (bias,), BF16, "finish_out", 4, (input_grad,)
+        finish_out_kernel, order, out_summands, x_all[0], columns, BF16, "finish_out", 0, (far,)
     )
+    norm_count, bias_count = own_width // tensor_count, b_qkv.shape[0] // dp_count
+    at = lax.axis_index("dp").astype(jnp.int32) * jnp.array([own_width, own_width, bias_count], jnp.int32)
+    at = at + mine * jnp.array([norm_count, 0, 0], jnp.int32)
+    up_grad, down_grad, dense_grad = parts(feed_grads, counts, (input_grad,))
     if paired():
-        qkv_grads, vectors = total(
-            partner_sums(qkv_own, qkv_sent), vector_sums(norms, others), (input_grad,)
+        qkv_grads, *vectors = total(
+            at,
+            partner_sums(qkv_own, qkv_sent),
+            vector_sums(norms, others),
+            (norm_count, own_width, bias_count),
+            (input_grad,),
         )
     else:
         qkv_grads = jnp.concatenate([qkv_own, qkv_sent], axis=0)
         qkv_grads = lax.psum_scatter(qkv_grads, "dp", scatter_dimension=0, tiled=True).astype(F32)
-        vectors = lax.psum(jnp.concatenate([lax.psum(norms, "tensor"), others], axis=0), "dp")
-    at = lax.axis_index("dp") * own_width + mine * (own_width // tensor_count)
-    norm_grads = lax.dynamic_slice_in_dim(vectors[:5], at, own_width // tensor_count, 1)
-    hidden_bias = lax.dynamic_slice_in_dim(vectors[5], lax.axis_index("dp") * own_width, own_width, 0)
-    bias_own = b_qkv.shape[0] // dp_count
-    qkv_bias = lax.dynamic_slice_in_dim(vectors[6], lax.axis_index("dp") * bias_own, bias_own, 0)
-    hidden_count = w_fc1.shape[1]
+        rows = lax.psum(jnp.concatenate([norms, others], axis=0), "dp")
+        vectors = [lax.dynamic_slice_in_dim(rows[index], at[0], norm_count, 0) for index in range(5)]
+        vectors += [lax.dynamic_slice_in_dim(rows[5], at[1], own_width, 0)]
+        vectors += [lax.dynamic_slice_in_dim(rows[6], at[2], bias_count, 0), vectors[4]]
     return (
         out,
         input_grad,
-        norm_grads[0],
-        norm_grads[1],
-        norm_grads[2],
-        norm_grads[3],
+        *vectors[:4],
         qkv_grads,
-        qkv_bias,
-        feed_grads[:, 2 * hidden_count :],
-        norm_grads[4],
-        feed_grads[:, :hidden_count],
-        hidden_bias,
-        feed_grads[:, hidden_count : 2 * hidden_count],
-        norm_grads[4],
+        vectors[6],
+        dense_grad,
+        vectors[4],
+        up_grad,
+        vectors[5],
+        down_grad,
+        vectors[7],
     )
 
 

time: 235 us -> 227 us (0.966)
  waiting for transfers between devices: 16.6 us -> 29.4 us
  starting transfers between devices: 39.4 us -> 29 us
  local copies, waits for them, and re-layouts: 17.7 us -> 11.6 us
  Pallas kernels: 134 us -> 128 us
    ppermute x30, waiting for transfers between devices: 16.5 us -> 29.4 us  [swap(): return lax.ppermute(value, axis, [(i, i ^ bits) for i in range(count)])]
    ppermute x30, starting transfers between devices: 39.3 us -> 28.9 us  [swap(): return lax.ppermute(value, axis, [(i, i ^ bits) for i in range(count)])]
    pallas_call x5 -> x6, Pallas kernels: 48.8 us -> 44.4 us  [the longest x1 30.8 us: feed(): call(feed_kernel, (parts,), [whole_spec(item.shape) for item in dy_all] +...]
    slice x3 -> x2, local copies, waits for them, and re-layouts: 4.1 us -> 0.83 us  [body(): others = jnp.concatenate([feed_vectors[2:4], last_vectors[2:4]], axis=0)]
    unnamed x85 -> x80, local copies, waits for them, and re-layouts: 9.37 us -> 8.84 us
  transfers between devices with their start and end apart: 32 -> 32, of which waited for: 7 -> 5; matrix products, arithmetic and copies ran while one was open for 5% -> 5% of each run, Pallas kernels for 43% -> 43%
where the time goes in v3:
time: 227 us; the launch traced here: 223 us
  Pallas kernels  128 us (56%)
  waiting for transfers between devices  29.4 us (13%)
  starting transfers between devices  29 us (13%)
  between operations  14.8 us (7%)
  local copies, waits for them, and re-layouts  11.6 us (5%)
  other arithmetic  9.94 us (4%)
    pallas_call x1, Pallas kernels, feed(): call(feed_kernel, (parts,), [whole_spec(item.shape) for item in dy_all] +...  30.8 us
    pallas_call x3, Pallas kernels, attend_back(): call(attend_back_kernel, (heads,), [whole_spec(starts.shape), whole_spec(...  29.9 us
    ppermute x30, waiting for transfers between devices, swap(): return lax.ppermute(value, axis, [(i, i ^ bits) for i in range(count)])  29.4 us
    ppermute x30, starting transfers between devices, swap(): return lax.ppermute(value, axis, [(i, i ^ bits) for i in range(count)])  28.9 us
    pallas_call x3, Pallas kernels, attend(): call(functools.partial(attend_kernel, len(through)), (heads,), [whole_spe...  17.6 us
    pallas_call x1, Pallas kernels, project_back(): call(functools.partial(project_back_kernel, len(pieces), len(mixed)), (pa...  13.6 us
    pallas_call x1, Pallas kernels, project(): call(functools.partial(project_kernel, len(pieces)), (len(x_all),), [whol...  9.84 us
    pallas_call x2, Pallas kernels, finish(): call(kernel, (count // part,), [block] * (len(summands) + 1) + [block if...  9.27 us
  transfers between devices with their start and end apart: 32, of which 5 were waited for; matrix products, arithmetic and copies ran while one was open for 5% of the time, Pallas kernels for 43%

profile of v3, /device:TPU:0, one launch (start us, length us, event | category | flops | bytes accessed | tf_op | source)
XLA Modules:
  0.0 222.9 jit_solution(2749278190494280992)
XLA Ops:
  7.2 1.8 pad_maximum_fusion
  9.1 1.2 broadcast_xor_fusion.order
  10.3 3.0 %turn.3.refs_0_.x_ref = bf16[768,512]{1,0:T(8,128)(2,1)} custom-call(s32[8]{0:T(128)} %broadcast_xor_fusion.order, bf16[512,768]{1,0:T(8,128)(2,1)} %rows_ref.3), custom_call_target="tpu_custom_call" | custom-call | tf_op jit(solution)/shard_map/turn/pallas_call | solution.py:122
  13.3 3.0 %collective-permute-start = (bf16[768,512]{1,0:T(8,128)(2,1)}, bf16[768,512]{1,0:T(8,128)(2,1)S(1)}, u32[]{:S(2)}, u32[]{:S(2)}) collective-permute-start(bf16[768,512]{1,0:T(8,128)(2,1)} %turn.3.refs_0_.x_ref), channel_id=1, source_target_pairs={{0,2},{1,3},{2,0},{3,1},{4,6},{5,7},{6,4},{7,5},{8,10},{9,11},{10,... | collective-permute-start | bytes 2359304 | tf_op jit(solution)/shard_map/ppermute | solution.py:685
  16.2 3.6 %collective-permute-start.6 = (bf16[96,576]{1,0:T(8,128)(2,1)}, bf16[96,576]{1,0:T(8,128)(2,1)S(1)}, u32[]{:S(2)}, u32[]{:S(2)}) collective-permute-start(bf16[96,576]{1,0:T(8,128)(2,1)} %refs_1_.1), channel_id=1, source_target_pairs={{0,24},{4,28},{8,16},{12,20},{16,8},{20,12},{24,0},{28,4},{1,25},{... | collective-permute-start | bytes 331784 | tf_op jit(solution)/shard_map/ppermute | solution.py:685
  19.9 0.8 collective-permute-start.2
  20.6 1.5 collective-permute-start.1
  22.1 1.2 slice.15
  23.3 2.8 %collective-permute-done.6.refs_7_.refs_4_ = bf16[96,576]{1,0:T(8,128)(2,1)S(1)} collective-permute-done((bf16[96,576]{1,0:T(8,128)(2,1)}, bf16[96,576]{1,0:T(8,128)(2,1)S(1)}, u32[]{:S(2)}, u32[]{:S(2)}) %collective-permute-start.6) | collective-permute-done | bytes 110624 | tf_op jit(solution)/shard_map/ppermute | solution.py:685
  26.1 1.3 collective-permute-start.7
  27.4 13.2 %collective-permute-done.4.refs_6_.refs_3_ = bf16[96,576]{1,0:T(8,128)(2,1)S(1)} collective-permute-done((bf16[96,576]{1,0:T(8,128)(2,1)}, bf16[96,576]{1,0:T(8,128)(2,1)S(1)}, u32[]{:S(2)}, u32[]{:S(2)}) %collective-permute-start.4) | collective-permute-done | bytes 110624 | tf_op jit(solution)/shard_map/ppermute | solution.py:685
  40.6 1.5 collective-permute-start.5
  42.1 0.5 collective-permute-start.3
  42.6 2.0 select_reduce_fusion
  44.6 2.9 %turn.2.refs_0_ = bf16[768,512]{1,0:T(8,128)(2,1)} custom-call(s32[8]{0:T(128)} %broadcast_xor_fusion.order, bf16[512,768]{1,0:T(8,128)(2,1)} %rows_ref.2), custom_call_target="tpu_custom_call" | custom-call | tf_op jit(solution)/shard_map/turn/pallas_call | solution.py:122
  47.6 0.6 copy-done.11
  48.3 0.9 copy-done
  49.2 0.5 collective-permute-start.10
  49.7 1.2 subtract_convert_fusion
  51.1 0.6 pad.9.rows_ref
  51.8 2.4 %stand.1.refs_12_.refs_9_.refs_13_.bias_ref = f32[768,128]{1,0:T(8,128)} custom-call(s32[8]{0:T(128)} %broadcast_xor_fusion.order, f32[8,768]{1,0:T(8,128)} %pad.9.rows_ref), custom_call_target="tpu_custom_call" | custom-call | tf_op jit(solution)/shard_map/stand/pallas_call | solution.py:155
  54.2 1.0 multiply_sine_fusion
  55.2 0.8 copy-done.8
  56.3 9.8 %project.1 = (bf16[576,2048]{1,0:T(8,128)(2,1)}, bf16[4,768,512]{2,1,0:T(8,128)(2,1)}, bf16[4,768,512]{2,1,0:T(8,128)(2,1)}) custom-call(s32[1]{0:T(128)} %bitcast.place, bf16[768,512]{1,0:T(8,128)(2,1)} %turn.3.refs_0_.x_ref, bf16[768,512]{1,0:T(8,128)(2,1)} %copy-done.8, bf16[768,512]{1,0:T(8,128)(2,1)} %copy-done, bf16[768,512]{1,0:T(8,128)(2,1)} %copy-done.9, ...), custom_call_target="tpu_custom_call" | custom-call | flops 1150000000 | tf_op jit(solution)/shard_map/project/pallas_call | solution.py:201
  66.2 5.9 %attend.3 = (bf16[64,2048]{1,0:T(8,128)(2,1)}, f32[1,1,2048]{2,1,0:T(1,128)}) custom-call(s32[1,2048]{1,0:T(1,128)} %bitcast.3, bf16[576,2048]{1,0:T(8,128)(2,1)} %get-tuple-element.55.qkv_ref), custom_call_target="tpu_custom_call" | custom-call | flops 1150000000 | tf_op jit(solution)/shard_map/attend/pallas_call | solution.py:274
  72.0 0.9 copy-done.37
  72.9 5.8 %attend.4 = (bf16[64,2048]{1,0:T(8,128)(2,1)}, f32[1,1,2048]{2,1,0:T(1,128)}, bf16[768,512]{1,0:T(8,128)(2,1)}) custom-call(s32[1,2048]{1,0:T(1,128)} %bitcast.4, bf16[576,2048]{1,0:T(8,128)(2,1)} %get-tuple-element.55.qkv_ref, bf16[768,512]{1,0:T(8,128)(2,1)} %copy-done.37, ...), custom_call_target="tpu_custom_call", output_to_operand_aliasing={{2}: (2, {})} | custom-call | flops 1150000000 | tf_op jit(solution)/shard_map/attend/pallas_call | solution.py:274
  78.8 0.3 collective-permute-start.12
  79.1 5.9 %attend.5 = (bf16[64,2048]{1,0:T(8,128)(2,1)}, f32[1,1,2048]{2,1,0:T(1,128)}) custom-call(s32[1,2048]{1,0:T(1,128)} %bitcast.5, bf16[576,2048]{1,0:T(8,128)(2,1)} %get-tuple-element.55.qkv_ref, bf16[64,2048]{1,0:T(8,128)(2,1)} %get-tuple-element.59.refs_0_.refs_7_.out_ref), custom_call_target="tpu_custom_call" | custom-call | flops 1150000000 | tf_op jit(solution)/shard_map/attend/pallas_call | solution.py:274
  85.0 0.8 copy-done.39
  85.9 30.8 %feed.1 = (bf16[768,512]{1,0:T(8,128)(2,1)}, bf16[768,512]{1,0:T(8,128)(2,1)}, bf16[768,512]{1,0:T(8,128)(2,1)}, bf16[768,512]{1,0:T(8,128)(2,1)}, bf16[4,768,51...) custom-call(s32[1]{0:T(128)} %bitcast.place, ...), custom_call_target="tpu_custom_call" | custom-call | flops 34500001792 | tf_op jit(solution)/shard_map/feed/pallas_call | solution.py:420
  116.7 1.1 copy-done.38
  118.0 9.9 %attend_back.3.refs_1_.refs_9_ = bf16[192,2048]{1,0:T(8,128)(2,1)} custom-call(s32[1,2048]{1,0:T(1,128)} %bitcast.6, f32[8,2048]{1,0:T(8,128)} %get-tuple-element.103.refs_13_.cos_ref, f32[8,2048]{1,0:T(8,128)} %get-tuple-element.102.refs_14_.sin_ref, bf16[576,2048]{1,0:T(8,128)(2,1)} %get-tuple-element.55.qkv_ref, ...), custom_call_target="tpu_custom_call" | custom-call | flops 10350000128 | tf_op jit(solution)/shard_map/attend_back/pallas_call | solution.py:330
  128.2 2.0 collective-permute-start.15
  130.2 10.1 %attend_back.4.refs_0_.refs_10_ = bf16[192,2048]{1,0:T(8,128)(2,1)} custom-call(s32[1,2048]{1,0:T(1,128)} %bitcast.7, f32[8,2048]{1,0:T(8,128)} %get-tuple-element.103.refs_13_.cos_ref, f32[8,2048]{1,0:T(8,128)} %get-tuple-element.102.refs_14_.sin_ref, bf16[576,2048]{1,0:T(8,128)(2,1)} %get-tuple-element.55.qkv_ref, ...), custom_call_target="tpu_custom_call" | custom-call | flops 10350000128 | tf_op jit(solution)/shard_map/attend_back/pallas_call | solution.py:330
  140.3 9.9 %attend_back.5.refs_11_ = bf16[192,2048]{1,0:T(8,128)(2,1)} custom-call(s32[1,2048]{1,0:T(1,128)} %bitcast.8, f32[8,2048]{1,0:T(8,128)} %get-tuple-element.103.refs_13_.cos_ref, f32[8,2048]{1,0:T(8,128)} %get-tuple-element.102.refs_14_.sin_ref, bf16[576,2048]{1,0:T(8,128)(2,1)} %get-tuple-element.55.qkv_ref, bf16[192,2048]{1,0:T(8,128)(2,1)} %get-tuple-element.66.grad_ref, ...), custom_call_target="tpu_custom_call" | custom-call | flops 10350000128 | tf_op jit(solution)/shard_map/attend_back/pallas_call | solution.py:330
  150.2 0.9 copy-done.4
  151.1 13.6 %project_back.1 = (bf16[768,512]{1,0:T(8,128)(2,1)}, bf16[768,512]{1,0:T(8,128)(2,1)}, bf16[768,512]{1,0:T(8,128)(2,1)}, bf16[768,512]{1,0:T(8,128)(2,1)}, bf16[...) custom-call(s32[1]{0:T(128)} %bitcast.place, s32[8]{0:T(128)} %broadcast_xor_fusion.order, ...), custom_call_target="tpu_custom_call" | custom-call | flops 14949999616 | tf_op jit(solution)/shard_map/project_back/pallas_call | solution.py:506
  164.8 0.8 fusion.2
  165.7 0.9 collective-permute-start.18
  166.6 1.0 collective-permute-start.19
  168.1 1.3 collective-permute-done.18
  169.7 0.6 add_add_fusion.refs_0_
  170.4 0.9 copy-done.1
  171.2 2.4 %share.1.refs_0_ = bf16[768,512]{1,0:T(8,128)(2,1)} custom-call(bf16[768,512]{1,0:T(8,128)(2,1)} %get-tuple-element.71.own_ref, bf16[768,512]{1,0:T(8,128)(2,1)} %copy-done.1, f32[4,768]{1,0:T(4,128)} %add_add_fusion.refs_0_), custom_call_target="tpu_custom_call" | custom-call | tf_op jit(solution)/shard_map/share/pallas_call | solution.py:585
  173.7 1.0 collective-permute-start.21
  174.6 1.4 collective-permute-start.22
  176.0 0.7 pad_maximum_fusion.1
  176.7 0.7 collective-permute-start.26
  177.4 11.6 %collective-permute-done.26 = f32[8,768]{1,0:T(8,128)S(1)} collective-permute-done((f32[8,768]{1,0:T(8,128)S(1)}, f32[8,768]{1,0:T(8,128)S(1)}, u32[]{:S(2)}, u32[]{:S(2)}) %collective-permute-start.26) | collective-permute-done | bytes 24608 | tf_op jit(solution)/shard_map/ppermute | solution.py:685
  189.1 0.7 fusion.refs_3_
  189.8 3.4 %collective-permute-start.29 = (f32[8,768]{1,0:T(8,128)S(1)}, f32[8,768]{1,0:T(8,128)S(1)}, u32[]{:S(2)}, u32[]{:S(2)}) collective-permute-start(f32[8,768]{1,0:T(8,128)S(1)} %fusion.refs_3_), channel_id=1, source_target_pairs={{0,24},{4,28},{8,16},{12,20},{16,8},{20,12},{24,0},{28,4},{1,25},{... | collective-permute-start | bytes 73736 | tf_op jit(solution)/shard_map/ppermute | solution.py:685
  193.2 0.8 copy-done.10
  194.0 2.0 halve.1
  196.0 0.3 collective-permute-start.27
  196.4 1.7 collective-permute-start.23
  198.1 2.2 collective-permute-start.24
  200.3 0.5 collective-permute-start.25
  200.8 0.5 multiply_add_fusion.at
  201.3 3.9 %finish_out.1 = bf16[512,768]{1,0:T(8,128)(2,1)} custom-call(s32[8]{0:T(128)} %broadcast_xor_fusion.order, bf16[768,512]{1,0:T(8,128)(2,1)} %get-tuple-element.61.own_ref, bf16[768,512]{1,0:T(8,128)(2,1)} %copy-done.6, bf16[768,512]{1,0:T(8,128)(2,1)} %copy-done.4, bf16[768,512]{1,0:T(8,128)(2,1)} %turn.3.refs_0_.x_ref, ...), custom_call_target="tpu_custom_call" | custom-call | tf_op jit(solution)/shard_map/finish_out/pallas_call | solution.py:563
  205.2 5.3 %finish_grad.1.refs_7_.refs_0_ = f32[512,768]{1,0:T(8,128)} custom-call(s32[8]{0:T(128)} %broadcast_xor_fusion.order, bf16[768,512]{1,0:T(8,128)(2,1)} %get-tuple-element.75.own_ref, bf16[768,512]{1,0:T(8,128)(2,1)} %copy-done.5, bf16[768,512]{1,0:T(8,128)(2,1)} %copy-done.7, bf16[768,512]{1,0:T(8,128)(2,1)} %turn.3.refs_0_.x_ref, ...), custom_call_target="tpu_custom_call" | custom-call | tf_op jit(solution)/shard_map/finish_grad/pallas_call | solution.py:563
  210.7 0.5 copy-done.23
  211.3 2.6 %total.1 = (f32[96,576]{1,0:T(8,128)}, f32[24]{0:T(128)}, f32[24]{0:T(128)}, f32[24]{0:T(128)}, f32[24]{0:T(128)}, /*index=5*/f32[24]{0:T(128)}, f32[96]{0:T(128)}, f32[72]{0:T(128)}, f32[24]{0:T(128)}) custom-call(s32[3]{0:T(128)} %multiply_add_fusion.at, f32[96,576]{1,0:T(8,128)} %get-tuple-element.79.kept_ref, bf16[96,576]{1,0:T(8,128)(2,1)} %copy-done.18, ...), custom_call_target="tpu_custom_call" | custom-call | tf_op jit(solution)/shard_map/total/pallas_call | solution.py:654
  214.0 1.8 parts.1
  (127 shorter events, 2.4 us)
Async XLA Ops:
  7.2 77.8 %all-gather.2.cloned.1.call-start = ((), (), s32[]{:S(2)}) async-start(), calls=%async_computation.1 | async-start | bytes 3096576 | tf_op jit(solution)/shard_map/all_gather | solution.py:758
  9.0 204.9 %reduce-scatter.2.cloned.1.call-start = ((), (), s32[]{:S(2)}) async-start(), calls=%async_computation.2 | async-start | bytes 3096576 | tf_op jit(solution)/shard_map/reduce_scatter | solution.py:787
  10.3 40.7 %copy-start.28 = (f32[768]{0:T(1024)S(1)}, f32[768]{0:T(1024)}, u32[]{:S(2)}) copy-start(f32[768]{0:T(1024)} %param.20) | copy-start | bytes 9220
  10.3 40.7 %copy-start.29 = (f32[768]{0:T(1024)S(1)}, f32[768]{0:T(1024)}, u32[]{:S(2)}) copy-start(f32[768]{0:T(1024)} %param.21) | copy-start | bytes 9220
  10.3 40.7 %copy-start.30 = (f32[768]{0:T(1024)S(1)}, f32[768]{0:T(1024)}, u32[]{:S(2)}) copy-start(f32[768]{0:T(1024)} %param.22) | copy-start | bytes 9220
  10.3 40.7 %copy-start.31 = (f32[768]{0:T(1024)S(1)}, f32[768]{0:T(1024)}, u32[]{:S(2)}) copy-start(f32[768]{0:T(1024)} %param.23) | copy-start | bytes 9220
  10.3 40.7 %copy-start.32 = (f32[768]{0:T(1024)S(1)}, f32[768]{0:T(1024)}, u32[]{:S(2)}) copy-start(f32[768]{0:T(1024)} %param.29) | copy-start | bytes 9220
  10.3 40.7 %copy-start.33 = (f32[576]{0:T(1024)S(1)}, f32[576]{0:T(1024)}, u32[]{:S(2)}) copy-start(f32[576]{0:T(1024)} %param.25) | copy-start | bytes 6916
  10.3 40.8 %copy-start.26 = (f32[768]{0:T(1024)S(1)}, f32[768]{0:T(1024)}, u32[]{:S(2)}) copy-start(f32[768]{0:T(1024)} %param.27) | copy-start | bytes 9220
  10.3 40.8 %copy-start.27 = (f32[768]{0:T(1024)S(1)}, f32[768]{0:T(1024)}, u32[]{:S(2)}) copy-start(f32[768]{0:T(1024)} %param.31) | copy-start | bytes 9220
  13.3 34.3 %collective-permute-start = (bf16[768,512]{1,0:T(8,128)(2,1)}, bf16[768,512]{1,0:T(8,128)(2,1)S(1)}, u32[]{:S(2)}, u32[]{:S(2)}) collective-permute-start(bf16[768,512]{1,0:T(8,128)(2,1)} %turn.3.refs_0_.x_ref), channel_id=1, source_target_pairs={{0,2},{1,3},{2,0},{3,1},{4,6},{5,7},{6,4},{7,5},{8,10},{9,11},{10,... | collective-permute-start | bytes 2359304 | tf_op jit(solution)/shard_map/ppermute | solution.py:685
  16.2 9.9 %collective-permute-start.6 = (bf16[96,576]{1,0:T(8,128)(2,1)}, bf16[96,576]{1,0:T(8,128)(2,1)S(1)}, u32[]{:S(2)}, u32[]{:S(2)}) collective-permute-start(bf16[96,576]{1,0:T(8,128)(2,1)} %refs_1_.1), channel_id=1, source_target_pairs={{0,24},{4,28},{8,16},{12,20},{16,8},{20,12},{24,0},{28,4},{1,25},{... | collective-permute-start | bytes 331784 | tf_op jit(solution)/shard_map/ppermute | solution.py:685
  19.8 20.8 %collective-permute-start.4 = (bf16[96,576]{1,0:T(8,128)(2,1)}, bf16[96,576]{1,0:T(8,128)(2,1)S(1)}, u32[]{:S(2)}, u32[]{:S(2)}) collective-permute-start(bf16[96,576]{1,0:T(8,128)(2,1)} %refs_1_.1), channel_id=1, source_target_pairs={{0,16},{4,20},{8,24},{12,28},{16,0},{20,4},{24,8},{28,12},{1,17},{... | collective-permute-start | bytes 331784 | tf_op jit(solution)/shard_map/ppermute | solution.py:685
  19.9 22.3 %collective-permute-start.2 = (bf16[96,576]{1,0:T(8,128)(2,1)}, bf16[96,576]{1,0:T(8,128)(2,1)S(1)}, u32[]{:S(2)}, u32[]{:S(2)}) collective-permute-start(bf16[96,576]{1,0:T(8,128)(2,1)} %refs_1_.1), channel_id=1, source_target_pairs={{0,8},{4,12},{8,0},{12,4},{16,24},{20,28},{24,16},{28,20},{1,9},{5... | collective-permute-start | bytes 331784 | tf_op jit(solution)/shard_map/ppermute | solution.py:685
  20.6 26.9 %collective-permute-start.1 = (bf16[96,576]{1,0:T(8,128)(2,1)}, bf16[96,576]{1,0:T(8,128)(2,1)S(1)}, u32[]{:S(2)}, u32[]{:S(2)}) collective-permute-start(bf16[96,576]{1,0:T(8,128)(2,1)} %refs_1_.1), channel_id=1, source_target_pairs={{0,4},{4,0},{8,12},{12,8},{16,20},{20,16},{24,28},{28,24},{1,5},{5... | collective-permute-start | bytes 331784 | tf_op jit(solution)/shard_map/ppermute | solution.py:685
  26.1 29.1 %copy-start.15 = (bf16[96,576]{1,0:T(8,128)(2,1)}, bf16[96,576]{1,0:T(8,128)(2,1)S(1)}, u32[]{:S(2)}) copy-start(bf16[96,576]{1,0:T(8,128)(2,1)S(1)} %collective-permute-done.6.refs_7_.refs_4_) | copy-start | bytes 331780
  26.1 21.4 %collective-permute-start.7 = (bf16[96,576]{1,0:T(8,128)(2,1)S(1)}, bf16[96,576]{1,0:T(8,128)(2,1)S(1)}, u32[]{:S(2)}, u32[]{:S(2)}) collective-permute-start(bf16[96,576]{1,0:T(8,128)(2,1)S(1)} %collective-permute-done.6.refs_7_.refs_4_), channel_id=1, source_target_pairs={{0,4},{4,0},{8,12},{12,8},{16,20},{20,16},{24,28},{28,24},{1,5},{5... | collective-permute-start | bytes 331784 | tf_op jit(solution)/shard_map/ppermute | solution.py:685
  40.6 14.6 %copy-start.16 = (bf16[96,576]{1,0:T(8,128)(2,1)}, bf16[96,576]{1,0:T(8,128)(2,1)S(1)}, u32[]{:S(2)}) copy-start(bf16[96,576]{1,0:T(8,128)(2,1)S(1)} %collective-permute-done.4.refs_6_.refs_3_) | copy-start | bytes 331780
  40.6 6.9 %collective-permute-start.5 = (bf16[96,576]{1,0:T(8,128)(2,1)S(1)}, bf16[96,576]{1,0:T(8,128)(2,1)S(1)}, u32[]{:S(2)}, u32[]{:S(2)}) collective-permute-start(bf16[96,576]{1,0:T(8,128)(2,1)S(1)} %collective-permute-done.4.refs_6_.refs_3_), channel_id=1, source_target_pairs={{0,4},{4,0},{8,12},{12,8},{16,20},{20,16},{24,28},{28,24},{1,5},{5... | collective-permute-start | bytes 331784 | tf_op jit(solution)/shard_map/ppermute | solution.py:685
  42.1 13.1 %copy-start.17 = (bf16[96,576]{1,0:T(8,128)(2,1)}, bf16[96,576]{1,0:T(8,128)(2,1)S(1)}, u32[]{:S(2)}) copy-start(bf16[96,576]{1,0:T(8,128)(2,1)S(1)} %collective-permute-done.2.refs_5_.refs_2_) | copy-start | bytes 331780
  42.1 5.5 %collective-permute-start.3 = (bf16[96,576]{1,0:T(8,128)(2,1)S(1)}, bf16[96,576]{1,0:T(8,128)(2,1)S(1)}, u32[]{:S(2)}, u32[]{:S(2)}) collective-permute-start(bf16[96,576]{1,0:T(8,128)(2,1)S(1)} %collective-permute-done.2.refs_5_.refs_2_), channel_id=1, source_target_pairs={{0,4},{4,0},{8,12},{12,8},{16,20},{20,16},{24,28},{28,24},{1,5},{5... | collective-permute-start | bytes 331784 | tf_op jit(solution)/shard_map/ppermute | solution.py:685
  47.5 7.7 %collective-permute-start.9 = (bf16[768,512]{1,0:T(8,128)(2,1)}, bf16[768,512]{1,0:T(8,128)(2,1)S(1)}, u32[]{:S(2)}, u32[]{:S(2)}) collective-permute-start(bf16[768,512]{1,0:T(8,128)(2,1)} %turn.3.refs_0_.x_ref), channel_id=1, source_target_pairs={{0,1},{1,0},{2,3},{3,2},{4,5},{5,4},{6,7},{7,6},{8,9},{9,8},{10,11... | collective-permute-start | bytes 2359304 | tf_op jit(solution)/shard_map/ppermute | solution.py:685
  47.6 0.7 copy-start.14
  48.3 0.9 copy-start
  49.2 22.9 %collective-permute-start.11 = (bf16[768,512]{1,0:T(8,128)(2,1)}, bf16[768,512]{1,0:T(8,128)(2,1)S(1)}, u32[]{:S(2)}, u32[]{:S(2)}) collective-permute-start(bf16[768,512]{1,0:T(8,128)(2,1)} %gate.1.refs_15_.refs_0_.dy_ref), channel_id=1, source_target_pairs={{0,2},{1,3},{2,0},{3,1},{4,6},{5,7},{6,4},{7,5},{8,10},{9,11},{10,... | collective-permute-start | bytes 2359304 | tf_op jit(solution)/shard_map/ppermute | solution.py:685
  49.2 6.0 %collective-permute-start.10 = (bf16[768,512]{1,0:T(8,128)(2,1)}, bf16[768,512]{1,0:T(8,128)(2,1)S(1)}, u32[]{:S(2)}, u32[]{:S(2)}) collective-permute-start(bf16[768,512]{1,0:T(8,128)(2,1)} %copy-done), channel_id=1, source_target_pairs={{0,1},{1,0},{2,3},{3,2},{4,5},{5,4},{6,7},{7,6},{8,9},{9,8},{10,11... | collective-permute-start | bytes 2359304 | tf_op jit(solution)/shard_map/ppermute | solution.py:685
  55.1 29.8 %collective-permute-start.8 = (bf16[768,512]{1,0:T(8,128)(2,1)}, bf16[768,512]{1,0:T(8,128)(2,1)}, u32[]{:S(2)}, u32[]{:S(2)}) collective-permute-start(bf16[768,512]{1,0:T(8,128)(2,1)} %gate.1.refs_15_.refs_0_.dy_ref), channel_id=1, source_target_pairs={{0,1},{1,0},{2,3},{3,2},{4,5},{5,4},{6,7},{7,6},{8,9},{9,8},{10,11... | collective-permute-start | bytes 2359304 | tf_op jit(solution)/shard_map/ppermute | solution.py:685
  55.2 0.9 copy-start.8
  55.2 1.1 copy-start.9
  72.0 0.9 copy-start.37
  78.8 6.2 %collective-permute-start.12 = (bf16[768,512]{1,0:T(8,128)(2,1)}, bf16[768,512]{1,0:T(8,128)(2,1)S(1)}, u32[]{:S(2)}, u32[]{:S(2)}) collective-permute-start(bf16[768,512]{1,0:T(8,128)(2,1)} %get-tuple-element.57.refs_2_), channel_id=1, source_target_pairs={{0,1},{1,0},{2,3},{3,2},{4,5},{5,4},{6,7},{7,6},{8,9},{9,8},{10,11... | collective-permute-start | bytes 2359304 | tf_op jit(solution)/shard_map/ppermute | solution.py:685
  85.0 0.9 copy-start.39
  116.7 1.1 copy-start.38
  117.8 10.1 %collective-permute-start.14 = (bf16[768,512]{1,0:T(8,128)(2,1)S(1)}, bf16[768,512]{1,0:T(8,128)(2,1)S(1)}, u32[]{:S(2)}, u32[]{:S(2)}) collective-permute-start(bf16[768,512]{1,0:T(8,128)(2,1)S(1)} %copy-done.38), channel_id=1, source_target_pairs={{0,1},{1,0},{2,3},{3,2},{4,5},{5,4},{6,7},{7,6},{8,9},{9,8},{10,11... | collective-permute-start | bytes 2359304 | tf_op jit(solution)/shard_map/ppermute | solution.py:685
  118.0 9.9 %copy-start.2 = (bf16[768,512]{1,0:T(8,128)(2,1)S(1)}, bf16[768,512]{1,0:T(8,128)(2,1)}, u32[]{:S(2)}) copy-start(bf16[768,512]{1,0:T(8,128)(2,1)} %get-tuple-element.63) | copy-start | bytes 2359300
  128.1 2.0 copy-start.3
  128.2 22.0 %collective-permute-start.15 = (bf16[768,512]{1,0:T(8,128)(2,1)S(1)}, bf16[768,512]{1,0:T(8,128)(2,1)S(1)}, u32[]{:S(2)}, u32[]{:S(2)}) collective-permute-start(bf16[768,512]{1,0:T(8,128)(2,1)S(1)} %add_convert_fusion.refs_0_), channel_id=1, source_target_pairs={{0,2},{1,3},{2,0},{3,1},{4,6},{5,7},{6,4},{7,5},{8,10},{9,11},{10,... | collective-permute-start | bytes 2359304 | tf_op jit(solution)/shard_map/ppermute | solution.py:685
  150.2 0.9 copy-start.4
  151.1 13.7 %copy-start.25 = (f32[8,768]{1,0:T(8,128)S(1)}, f32[8,768]{1,0:T(8,128)}, u32[]{:S(2)}) copy-start(f32[8,768]{1,0:T(8,128)} %get-tuple-element.74) | copy-start | bytes 73732
  151.1 16.8 %copy-start.36 = (bf16[768,512]{1,0:T(8,128)(2,1)S(1)}, bf16[768,512]{1,0:T(8,128)(2,1)}, u32[]{:S(2)}) copy-start(bf16[768,512]{1,0:T(8,128)(2,1)} %get-tuple-element.62) | copy-start | bytes 2359300
  164.7 36.0 %copy-start.34 = (s32[3]{0:T(128)S(1)}, s32[3]{0:T(128)}, u32[]{:S(2)}) copy-start(s32[3]{0:T(128)} %constant.30.clone) | copy-start | bytes 40
  164.7 36.0 %copy-start.35 = (s32[3]{0:T(128)S(1)}, s32[3]{0:T(128)}, u32[]{:S(2)}) copy-start(s32[3]{0:T(128)} %constant.29.clone) | copy-start | bytes 40
  164.7 5.6 %collective-permute-start.16 = (bf16[768,512]{1,0:T(8,128)(2,1)}, bf16[768,512]{1,0:T(8,128)(2,1)S(1)}, u32[]{:S(2)}, u32[]{:S(2)}) collective-permute-start(bf16[768,512]{1,0:T(8,128)(2,1)} %get-tuple-element.72), channel_id=1, source_target_pairs={{0,1},{1,0},{2,3},{3,2},{4,5},{5,4},{6,7},{7,6},{8,9},{9,8},{10,11... | collective-permute-start | bytes 2359304 | tf_op jit(solution)/shard_map/ppermute | solution.py:685
  165.7 3.8 %collective-permute-start.18 = (f32[4,768]{1,0:T(4,128)S(1)}, f32[4,768]{1,0:T(4,128)S(1)}, u32[]{:S(2)}, u32[]{:S(2)}) collective-permute-start(f32[4,768]{1,0:T(4,128)S(1)} %pad_maximum_fusion.2), channel_id=1, source_target_pairs={{0,2},{1,3},{2,0},{3,1},{4,6},{5,7},{6,4},{7,5},{8,10},{9,11},{10,... | collective-permute-start | bytes 36872 | tf_op jit(solution)/shard_map/ppermute | solution.py:685
  166.6 3.1 %collective-permute-start.19 = (f32[4,768]{1,0:T(4,128)S(1)}, f32[4,768]{1,0:T(4,128)S(1)}, u32[]{:S(2)}, u32[]{:S(2)}) collective-permute-start(f32[4,768]{1,0:T(4,128)S(1)} %pad_maximum_fusion.2), channel_id=1, source_target_pairs={{0,3},{1,2},{2,1},{3,0},{4,7},{5,6},{6,5},{7,4},{8,11},{9,10},{10,... | collective-permute-start | bytes 36872 | tf_op jit(solution)/shard_map/ppermute | solution.py:685
  167.6 2.2 collective-permute-start.17
  167.9 28.1 %collective-permute-start.13 = (bf16[768,512]{1,0:T(8,128)(2,1)S(1)}, bf16[768,512]{1,0:T(8,128)(2,1)S(1)}, u32[]{:S(2)}, u32[]{:S(2)}) collective-permute-start(bf16[768,512]{1,0:T(8,128)(2,1)S(1)} %copy-done.36), channel_id=1, source_target_pairs={{0,1},{1,0},{2,3},{3,2},{4,5},{5,4},{6,7},{7,6},{8,9},{9,8},{10,11... | collective-permute-start | bytes 2359304 | tf_op jit(solution)/shard_map/ppermute | solution.py:685
  169.4 28.7 %collective-permute-start.20 = (bf16[768,512]{1,0:T(8,128)(2,1)}, bf16[768,512]{1,0:T(8,128)(2,1)S(1)}, u32[]{:S(2)}, u32[]{:S(2)}) collective-permute-start(bf16[768,512]{1,0:T(8,128)(2,1)} %get-tuple-element.76), channel_id=1, source_target_pairs={{0,1},{1,0},{2,3},{3,2},{4,5},{5,4},{6,7},{7,6},{8,9},{9,8},{10,11... | collective-permute-start | bytes 2359304 | tf_op jit(solution)/shard_map/ppermute | solution.py:685
  170.4 0.9 copy-start.1
  173.7 26.6 %collective-permute-start.21 = (bf16[768,512]{1,0:T(8,128)(2,1)}, bf16[768,512]{1,0:T(8,128)(2,1)S(1)}, u32[]{:S(2)}, u32[]{:S(2)}) collective-permute-start(bf16[768,512]{1,0:T(8,128)(2,1)} %share.1.refs_0_), channel_id=1, source_target_pairs={{0,2},{1,3},{2,0},{3,1},{4,6},{5,7},{6,4},{7,5},{8,10},{9,11},{10,... | collective-permute-start | bytes 2359304 | tf_op jit(solution)/shard_map/ppermute | solution.py:685
  174.6 18.6 %collective-permute-start.22 = (bf16[384,576]{1,0:T(8,128)(2,1)}, bf16[384,576]{1,0:T(8,128)(2,1)S(1)}, u32[]{:S(2)}, u32[]{:S(2)}) collective-permute-start(bf16[384,576]{1,0:T(8,128)(2,1)} %get-tuple-element.78), channel_id=1, source_target_pairs={{0,4},{4,0},{8,12},{12,8},{16,20},{20,16},{24,28},{28,24},{1,5},{5... | collective-permute-start | bytes 1327112 | tf_op jit(solution)/shard_map/ppermute | solution.py:685
  176.7 12.4 %collective-permute-start.26 = (f32[8,768]{1,0:T(8,128)S(1)}, f32[8,768]{1,0:T(8,128)S(1)}, u32[]{:S(2)}, u32[]{:S(2)}) collective-permute-start(f32[8,768]{1,0:T(8,128)S(1)} %pad_maximum_fusion.1), channel_id=1, source_target_pairs={{0,4},{4,0},{8,12},{12,8},{16,20},{20,16},{24,28},{28,24},{1,5},{5... | collective-permute-start | bytes 73736 | tf_op jit(solution)/shard_map/ppermute | solution.py:685
  189.8 20.9 %copy-start.21 = (f32[8,768]{1,0:T(8,128)}, f32[8,768]{1,0:T(8,128)S(1)}, u32[]{:S(2)}) copy-start(f32[8,768]{1,0:T(8,128)S(1)} %fusion.refs_3_) | copy-start | bytes 73732
  189.8 6.5 %collective-permute-start.29 = (f32[8,768]{1,0:T(8,128)S(1)}, f32[8,768]{1,0:T(8,128)S(1)}, u32[]{:S(2)}, u32[]{:S(2)}) collective-permute-start(f32[8,768]{1,0:T(8,128)S(1)} %fusion.refs_3_), channel_id=1, source_target_pairs={{0,24},{4,28},{8,16},{12,20},{16,8},{20,12},{24,0},{28,4},{1,25},{... | collective-permute-start | bytes 73736 | tf_op jit(solution)/shard_map/ppermute | solution.py:685
  193.2 0.8 copy-start.10
  193.2 17.3 %collective-permute-start.28 = (f32[8,768]{1,0:T(8,128)S(1)}, f32[8,768]{1,0:T(8,128)S(1)}, u32[]{:S(2)}, u32[]{:S(2)}) collective-permute-start(f32[8,768]{1,0:T(8,128)S(1)} %fusion.refs_3_), channel_id=1, source_target_pairs={{0,16},{4,20},{8,24},{12,28},{16,0},{20,4},{24,8},{28,12},{1,17},{... | collective-permute-start | bytes 73736 | tf_op jit(solution)/shard_map/ppermute | solution.py:685
  196.0 5.3 %copy-start.6 = (bf16[768,512]{1,0:T(8,128)(2,1)}, bf16[768,512]{1,0:T(8,128)(2,1)S(1)}, u32[]{:S(2)}) copy-start(bf16[768,512]{1,0:T(8,128)(2,1)S(1)} %collective-permute-done.13.near_ref) | copy-start | bytes 2359300
  196.0 14.6 %collective-permute-start.27 = (f32[8,768]{1,0:T(8,128)S(1)}, f32[8,768]{1,0:T(8,128)S(1)}, u32[]{:S(2)}, u32[]{:S(2)}) collective-permute-start(f32[8,768]{1,0:T(8,128)S(1)} %fusion.refs_3_), channel_id=1, source_target_pairs={{0,8},{4,12},{8,0},{12,4},{16,24},{20,28},{24,16},{28,20},{1,9},{5... | collective-permute-start | bytes 73736 | tf_op jit(solution)/shard_map/ppermute | solution.py:685
  196.3 14.2 %copy-start.22 = (f32[8,768]{1,0:T(8,128)}, f32[8,768]{1,0:T(8,128)S(1)}, u32[]{:S(2)}) copy-start(f32[8,768]{1,0:T(8,128)S(1)} %collective-permute-done.29.refs_6_) | copy-start | bytes 73732
  196.4 14.2 %collective-permute-start.23 = (bf16[96,576]{1,0:T(8,128)(2,1)}, bf16[96,576]{1,0:T(8,128)(2,1)S(1)}, u32[]{:S(2)}, u32[]{:S(2)}) collective-permute-start(bf16[96,576]{1,0:T(8,128)(2,1)} %get-tuple-element.80), channel_id=1, source_target_pairs={{0,8},{4,12},{8,0},{12,4},{16,24},{20,28},{24,16},{28,20},{1,9},{5... | collective-permute-start | bytes 331784 | tf_op jit(solution)/shard_map/ppermute | solution.py:685
  198.1 7.1 %copy-start.5 = (bf16[768,512]{1,0:T(8,128)(2,1)}, bf16[768,512]{1,0:T(8,128)(2,1)S(1)}, u32[]{:S(2)}) copy-start(bf16[768,512]{1,0:T(8,128)(2,1)S(1)} %collective-permute-done.20.near_ref) | copy-start | bytes 2359300
  198.1 12.5 %collective-permute-start.24 = (bf16[96,576]{1,0:T(8,128)(2,1)}, bf16[96,576]{1,0:T(8,128)(2,1)S(1)}, u32[]{:S(2)}, u32[]{:S(2)}) collective-permute-start(bf16[96,576]{1,0:T(8,128)(2,1)} %get-tuple-element.81), channel_id=1, source_target_pairs={{0,16},{4,20},{8,24},{12,28},{16,0},{20,4},{24,8},{28,12},{1,17},{... | collective-permute-start | bytes 331784 | tf_op jit(solution)/shard_map/ppermute | solution.py:685
  200.3 5.0 %copy-start.7 = (bf16[768,512]{1,0:T(8,128)(2,1)}, bf16[768,512]{1,0:T(8,128)(2,1)S(1)}, u32[]{:S(2)}) copy-start(bf16[768,512]{1,0:T(8,128)(2,1)S(1)} %collective-permute-done.21.far_ref) | copy-start | bytes 2359300
  200.3 10.4 %collective-permute-start.25 = (bf16[96,576]{1,0:T(8,128)(2,1)}, bf16[96,576]{1,0:T(8,128)(2,1)S(1)}, u32[]{:S(2)}, u32[]{:S(2)}) collective-permute-start(bf16[96,576]{1,0:T(8,128)(2,1)} %get-tuple-element.82), channel_id=1, source_target_pairs={{0,24},{4,28},{8,16},{12,20},{16,8},{20,12},{24,0},{28,4},{1,25},{... | collective-permute-start | bytes 331784 | tf_op jit(solution)/shard_map/ppermute | solution.py:685
  (8 other events, 5.2 us)
Sparse Core Ops, SparseCore 0:
  10.2 63.6 all-gather.1
  116.8 73.3 reduce-scatter.1

commit v4 on v3

--- a/solution.py
+++ b/solution.py
@@ -721,8 +721,8 @@
     return (kept_block, *(swap(half, "dp", bits) for half, bits in zip(outward, PARTNERS[1:4])))
 
 
-def vector_sums(norms, others):
-    rows = jnp.concatenate([norms, others], axis=0)
+def vector_sums(norms, others, wait):
+    (rows,) = gate([jnp.concatenate([norms, others], axis=0)], wait)
     rows = rows + swap(rows, "dp", 1)
     return (rows, *(swap(rows, "dp", bits) for bits in PARTNERS[1:4]))
 
@@ -819,7 +819,7 @@
         qkv_grads, *vectors = total(
             at,
             partner_sums(qkv_own, qkv_sent),
-            vector_sums(norms, others),
+            vector_sums(norms, others, (out,)),
             (norm_count, own_width, bias_count),
             (input_grad,),
         )

time: 227 us -> 232 us (1.022)
    unnamed x80 -> x86, local copies, waits for them, and re-layouts: 8.84 us -> 9.71 us
  transfers between devices with their start and end apart: 32 -> 32, of which waited for: 5 -> 6; matrix products, arithmetic and copies ran while one was open for 5% -> 5% of each run, Pallas kernels for 43% -> 42%
where the time goes in v4:
time: 232 us; the launch traced here: 228 us
  Pallas kernels  128 us (55%)
  waiting for transfers between devices  31.7 us (14%)
  starting transfers between devices  30.7 us (13%)
  between operations  14.8 us (6%)
  local copies, waits for them, and re-layouts  12.4 us (5%)
  other arithmetic  9.84 us (4%)
    ppermute x30, waiting for transfers between devices, swap(): return lax.ppermute(value, axis, [(i, i ^ bits) for i in range(count)])  31.6 us
    pallas_call x1, Pallas kernels, feed(): call(feed_kernel, (parts,), [whole_spec(item.shape) for item in dy_all] +...  30.9 us
    ppermute x30, starting transfers between devices, swap(): return lax.ppermute(value, axis, [(i, i ^ bits) for i in range(count)])  30.6 us
    pallas_call x3, Pallas kernels, attend_back(): call(attend_back_kernel, (heads,), [whole_spec(starts.shape), whole_spec(...  29.9 us
    pallas_call x3, Pallas kernels, attend(): call(functools.partial(attend_kernel, len(through)), (heads,), [whole_spe...  17.5 us
    pallas_call x1, Pallas kernels, project_back(): call(functools.partial(project_back_kernel, len(pieces), len(mixed)), (pa...  13.6 us
    pallas_call x1, Pallas kernels, project(): call(functools.partial(project_kernel, len(pieces)), (len(x_all),), [whol...  9.77 us
    unnamed x86, local copies, waits for them, and re-layouts  9.71 us
  transfers between devices with their start and end apart: 32, of which 6 were waited for; matrix products, arithmetic and copies ran while one was open for 5% of the time, Pallas kernels for 42%

profile of v4, /device:TPU:0, one launch (start us, length us, event | category | flops | bytes accessed | tf_op | source)
XLA Modules:
  0.0 227.7 jit_solution(10032765316634499646)
XLA Ops:
  7.2 1.8 pad_maximum_fusion
  9.1 1.2 broadcast_xor_fusion.order
  10.3 3.0 %turn.3.refs_0_.x_ref = bf16[768,512]{1,0:T(8,128)(2,1)} custom-call(s32[8]{0:T(128)} %broadcast_xor_fusion.order, bf16[512,768]{1,0:T(8,128)(2,1)} %rows_ref.3), custom_call_target="tpu_custom_call" | custom-call | tf_op jit(solution)/shard_map/turn/pallas_call | solution.py:122
  13.3 3.0 %collective-permute-start = (bf16[768,512]{1,0:T(8,128)(2,1)}, bf16[768,512]{1,0:T(8,128)(2,1)S(1)}, u32[]{:S(2)}, u32[]{:S(2)}) collective-permute-start(bf16[768,512]{1,0:T(8,128)(2,1)} %turn.3.refs_0_.x_ref), channel_id=1, source_target_pairs={{0,2},{1,3},{2,0},{3,1},{4,6},{5,7},{6,4},{7,5},{8,10},{9,11},{10,... | collective-permute-start | bytes 2359304 | tf_op jit(solution)/shard_map/ppermute | solution.py:685
  16.2 3.6 %collective-permute-start.6 = (bf16[96,576]{1,0:T(8,128)(2,1)}, bf16[96,576]{1,0:T(8,128)(2,1)S(1)}, u32[]{:S(2)}, u32[]{:S(2)}) collective-permute-start(bf16[96,576]{1,0:T(8,128)(2,1)} %refs_1_.1), channel_id=1, source_target_pairs={{0,24},{4,28},{8,16},{12,20},{16,8},{20,12},{24,0},{28,4},{1,25},{... | collective-permute-start | bytes 331784 | tf_op jit(solution)/shard_map/ppermute | solution.py:685
  19.9 0.8 collective-permute-start.2
  20.6 1.5 collective-permute-start.1
  22.1 1.2 slice.15
  23.3 2.8 %collective-permute-done.6.refs_7_.refs_4_ = bf16[96,576]{1,0:T(8,128)(2,1)S(1)} collective-permute-done((bf16[96,576]{1,0:T(8,128)(2,1)}, bf16[96,576]{1,0:T(8,128)(2,1)S(1)}, u32[]{:S(2)}, u32[]{:S(2)}) %collective-permute-start.6) | collective-permute-done | bytes 110624 | tf_op jit(solution)/shard_map/ppermute | solution.py:685
  26.1 1.3 collective-permute-start.7
  27.4 13.2 %collective-permute-done.4.refs_6_.refs_3_ = bf16[96,576]{1,0:T(8,128)(2,1)S(1)} collective-permute-done((bf16[96,576]{1,0:T(8,128)(2,1)}, bf16[96,576]{1,0:T(8,128)(2,1)S(1)}, u32[]{:S(2)}, u32[]{:S(2)}) %collective-permute-start.4) | collective-permute-done | bytes 110624 | tf_op jit(solution)/shard_map/ppermute | solution.py:685
  40.6 1.5 collective-permute-start.5
  42.1 0.5 collective-permute-start.3
  42.6 2.0 select_reduce_fusion
  44.6 2.9 %turn.2.refs_0_ = bf16[768,512]{1,0:T(8,128)(2,1)} custom-call(s32[8]{0:T(128)} %broadcast_xor_fusion.order, bf16[512,768]{1,0:T(8,128)(2,1)} %rows_ref.2), custom_call_target="tpu_custom_call" | custom-call | tf_op jit(solution)/shard_map/turn/pallas_call | solution.py:122
  47.6 0.6 copy-done.11
  48.3 0.9 copy-done
  49.7 1.2 subtract_convert_fusion
  51.2 0.6 pad.9.rows_ref
  51.8 2.4 %stand.1.refs_12_.refs_9_.refs_13_.bias_ref = f32[768,128]{1,0:T(8,128)} custom-call(s32[8]{0:T(128)} %broadcast_xor_fusion.order, f32[8,768]{1,0:T(8,128)} %pad.9.rows_ref), custom_call_target="tpu_custom_call" | custom-call | tf_op jit(solution)/shard_map/stand/pallas_call | solution.py:155
  54.2 1.0 multiply_sine_fusion
  55.3 0.8 copy-done.7
  56.4 9.8 %project.1 = (bf16[576,2048]{1,0:T(8,128)(2,1)}, bf16[4,768,512]{2,1,0:T(8,128)(2,1)}, bf16[4,768,512]{2,1,0:T(8,128)(2,1)}) custom-call(s32[1]{0:T(128)} %bitcast.place, bf16[768,512]{1,0:T(8,128)(2,1)} %turn.3.refs_0_.x_ref, bf16[768,512]{1,0:T(8,128)(2,1)} %copy-done.7, bf16[768,512]{1,0:T(8,128)(2,1)} %copy-done, bf16[768,512]{1,0:T(8,128)(2,1)} %copy-done.9, ...), custom_call_target="tpu_custom_call" | custom-call | flops 1150000000 | tf_op jit(solution)/shard_map/project/pallas_call | solution.py:201
  66.1 5.9 %attend.3 = (bf16[64,2048]{1,0:T(8,128)(2,1)}, f32[1,1,2048]{2,1,0:T(1,128)}) custom-call(s32[1,2048]{1,0:T(1,128)} %bitcast.3, bf16[576,2048]{1,0:T(8,128)(2,1)} %get-tuple-element.55.qkv_ref), custom_call_target="tpu_custom_call" | custom-call | flops 1150000000 | tf_op jit(solution)/shard_map/attend/pallas_call | solution.py:274
  72.0 0.9 copy-done.38
  72.9 5.8 %attend.4 = (bf16[64,2048]{1,0:T(8,128)(2,1)}, f32[1,1,2048]{2,1,0:T(1,128)}, bf16[768,512]{1,0:T(8,128)(2,1)}) custom-call(s32[1,2048]{1,0:T(1,128)} %bitcast.4, bf16[576,2048]{1,0:T(8,128)(2,1)} %get-tuple-element.55.qkv_ref, bf16[768,512]{1,0:T(8,128)(2,1)} %copy-done.38, ...), custom_call_target="tpu_custom_call", output_to_operand_aliasing={{2}: (2, {})} | custom-call | flops 1150000000 | tf_op jit(solution)/shard_map/attend/pallas_call | solution.py:274
  79.1 5.8 %attend.5 = (bf16[64,2048]{1,0:T(8,128)(2,1)}, f32[1,1,2048]{2,1,0:T(1,128)}) custom-call(s32[1,2048]{1,0:T(1,128)} %bitcast.5, bf16[576,2048]{1,0:T(8,128)(2,1)} %get-tuple-element.55.qkv_ref, bf16[64,2048]{1,0:T(8,128)(2,1)} %get-tuple-element.59.refs_0_.refs_7_.out_ref), custom_call_target="tpu_custom_call" | custom-call | flops 1150000000 | tf_op jit(solution)/shard_map/attend/pallas_call | solution.py:274
  85.0 0.8 copy-done.40
  85.9 30.9 %feed.1 = (bf16[768,512]{1,0:T(8,128)(2,1)}, bf16[768,512]{1,0:T(8,128)(2,1)}, bf16[768,512]{1,0:T(8,128)(2,1)}, bf16[768,512]{1,0:T(8,128)(2,1)}, bf16[4,768,51...) custom-call(s32[1]{0:T(128)} %bitcast.place, ...), custom_call_target="tpu_custom_call" | custom-call | flops 34500001792 | tf_op jit(solution)/shard_map/feed/pallas_call | solution.py:420
  116.8 1.1 copy-done.39
  117.9 9.9 %attend_back.3.refs_1_.refs_9_ = bf16[192,2048]{1,0:T(8,128)(2,1)} custom-call(s32[1,2048]{1,0:T(1,128)} %bitcast.6, f32[8,2048]{1,0:T(8,128)} %get-tuple-element.103.refs_13_.cos_ref, f32[8,2048]{1,0:T(8,128)} %get-tuple-element.102.refs_14_.sin_ref, bf16[576,2048]{1,0:T(8,128)(2,1)} %get-tuple-element.55.qkv_ref, ...), custom_call_target="tpu_custom_call" | custom-call | flops 10350000128 | tf_op jit(solution)/shard_map/attend_back/pallas_call | solution.py:330
  128.1 2.0 collective-permute-start.15
  130.2 10.1 %attend_back.4.refs_0_.refs_10_ = bf16[192,2048]{1,0:T(8,128)(2,1)} custom-call(s32[1,2048]{1,0:T(1,128)} %bitcast.7, f32[8,2048]{1,0:T(8,128)} %get-tuple-element.103.refs_13_.cos_ref, f32[8,2048]{1,0:T(8,128)} %get-tuple-element.102.refs_14_.sin_ref, bf16[576,2048]{1,0:T(8,128)(2,1)} %get-tuple-element.55.qkv_ref, ...), custom_call_target="tpu_custom_call" | custom-call | flops 10350000128 | tf_op jit(solution)/shard_map/attend_back/pallas_call | solution.py:330
  140.2 9.9 %attend_back.5.refs_11_ = bf16[192,2048]{1,0:T(8,128)(2,1)} custom-call(s32[1,2048]{1,0:T(1,128)} %bitcast.8, f32[8,2048]{1,0:T(8,128)} %get-tuple-element.103.refs_13_.cos_ref, f32[8,2048]{1,0:T(8,128)} %get-tuple-element.102.refs_14_.sin_ref, bf16[576,2048]{1,0:T(8,128)(2,1)} %get-tuple-element.55.qkv_ref, bf16[192,2048]{1,0:T(8,128)(2,1)} %get-tuple-element.66.grad_ref, ...), custom_call_target="tpu_custom_call" | custom-call | flops 10350000128 | tf_op jit(solution)/shard_map/attend_back/pallas_call | solution.py:330
  150.1 0.9 copy-done.4
  151.1 13.6 %project_back.1 = (bf16[768,512]{1,0:T(8,128)(2,1)}, bf16[768,512]{1,0:T(8,128)(2,1)}, bf16[768,512]{1,0:T(8,128)(2,1)}, bf16[768,512]{1,0:T(8,128)(2,1)}, bf16[...) custom-call(s32[1]{0:T(128)} %bitcast.place, s32[8]{0:T(128)} %broadcast_xor_fusion.order, ...), custom_call_target="tpu_custom_call" | custom-call | flops 14949999616 | tf_op jit(solution)/shard_map/project_back/pallas_call | solution.py:506
  164.8 0.8 fusion.1
  165.6 1.1 collective-permute-start.18
  166.7 0.8 collective-permute-start.19
  168.0 1.3 collective-permute-done.18
  169.8 0.6 add_add_fusion.refs_0_
  170.4 0.9 copy-done.1
  171.3 2.4 %share.1.refs_0_ = bf16[768,512]{1,0:T(8,128)(2,1)} custom-call(bf16[768,512]{1,0:T(8,128)(2,1)} %get-tuple-element.71.own_ref, bf16[768,512]{1,0:T(8,128)(2,1)} %copy-done.1, f32[4,768]{1,0:T(4,128)} %add_add_fusion.refs_0_), custom_call_target="tpu_custom_call" | custom-call | tf_op jit(solution)/shard_map/share/pallas_call | solution.py:585
  173.7 0.8 collective-permute-start.21
  174.5 1.4 collective-permute-start.22
  175.9 12.7 %collective-permute-done.22.came_ref = bf16[384,576]{1,0:T(8,128)(2,1)S(1)} collective-permute-done((bf16[384,576]{1,0:T(8,128)(2,1)}, bf16[384,576]{1,0:T(8,128)(2,1)S(1)}, u32[]{:S(2)}, u32[]{:S(2)}) %collective-permute-start.22) | collective-permute-done | bytes 442400 | tf_op jit(solution)/shard_map/ppermute | solution.py:685
  188.6 0.8 copy-done.10
  189.4 2.0 halve.1
  191.4 1.5 collective-permute-start.23
  192.9 0.6 pad_maximum_fusion.1.refs_0_
  193.5 0.9 copy-done.8
  194.4 4.1 %finish_out.1.refs_1_ = bf16[512,768]{1,0:T(8,128)(2,1)} custom-call(s32[8]{0:T(128)} %broadcast_xor_fusion.order, bf16[768,512]{1,0:T(8,128)(2,1)} %get-tuple-element.61.own_ref, bf16[768,512]{1,0:T(8,128)(2,1)} %copy-done.8, bf16[768,512]{1,0:T(8,128)(2,1)} %copy-done.4, bf16[768,512]{1,0:T(8,128)(2,1)} %turn.3.refs_0_.x_ref, ...), custom_call_target="tpu_custom_call" | custom-call | tf_op jit(solution)/shard_map/finish_out/pallas_call | solution.py:563
  198.5 0.6 collective-permute-start.26
  199.0 2.4 %collective-permute-start.24 = (bf16[96,576]{1,0:T(8,128)(2,1)S(1)}, bf16[96,576]{1,0:T(8,128)(2,1)S(1)}, u32[]{:S(2)}, u32[]{:S(2)}) collective-permute-start(bf16[96,576]{1,0:T(8,128)(2,1)S(1)} %copy-done.42), channel_id=1, source_target_pairs={{0,16},{4,20},{8,24},{12,28},{16,0},{20,4},{24,8},{28,12},{1,17},{... | collective-permute-start | bytes 331784 | tf_op jit(solution)/shard_map/ppermute | solution.py:685
  201.4 1.1 collective-permute-done.26
  202.5 1.8 collective-permute-start.25
  204.3 0.7 add.33.refs_3_
  205.1 2.0 collective-permute-start.29
  207.2 0.6 collective-permute-start.28
  207.8 1.8 collective-permute-start.27
  210.1 5.3 %finish_grad.1.refs_7_.refs_0_ = f32[512,768]{1,0:T(8,128)} custom-call(s32[8]{0:T(128)} %broadcast_xor_fusion.order, bf16[768,512]{1,0:T(8,128)(2,1)} %get-tuple-element.75.own_ref, bf16[768,512]{1,0:T(8,128)(2,1)} %copy-done.5, bf16[768,512]{1,0:T(8,128)(2,1)} %copy-done.6, bf16[768,512]{1,0:T(8,128)(2,1)} %turn.3.refs_0_.x_ref, ...), custom_call_target="tpu_custom_call" | custom-call | tf_op jit(solution)/shard_map/finish_grad/pallas_call | solution.py:563
  215.5 0.5 copy-done.19
  216.1 2.6 %total.1 = (f32[96,576]{1,0:T(8,128)}, f32[24]{0:T(128)}, f32[24]{0:T(128)}, f32[24]{0:T(128)}, f32[24]{0:T(128)}, /*index=5*/f32[24]{0:T(128)}, f32[96]{0:T(128)}, f32[72]{0:T(128)}, f32[24]{0:T(128)}) custom-call(s32[3]{0:T(128)} %multiply_add_fusion.at, f32[96,576]{1,0:T(8,128)} %get-tuple-element.79.kept_ref, bf16[96,576]{1,0:T(8,128)(2,1)} %copy-done.18, ...), custom_call_target="tpu_custom_call" | custom-call | tf_op jit(solution)/shard_map/total/pallas_call | solution.py:654
  218.8 1.8 parts.1
  (134 shorter events, 3.7 us)
Async XLA Ops:
  7.2 77.8 %all-gather.2.cloned.1.call-start = ((), (), s32[]{:S(2)}) async-start(), calls=%async_computation.1 | async-start | bytes 3096576 | tf_op jit(solution)/shard_map/all_gather | solution.py:758
  9.0 209.7 %reduce-scatter.2.cloned.1.call-start = ((), (), s32[]{:S(2)}) async-start(), calls=%async_computation.2 | async-start | bytes 3096576 | tf_op jit(solution)/shard_map/reduce_scatter | solution.py:787
  10.3 40.7 %copy-start.29 = (f32[768]{0:T(1024)S(1)}, f32[768]{0:T(1024)}, u32[]{:S(2)}) copy-start(f32[768]{0:T(1024)} %param.20) | copy-start | bytes 9220
  10.3 40.7 %copy-start.30 = (f32[768]{0:T(1024)S(1)}, f32[768]{0:T(1024)}, u32[]{:S(2)}) copy-start(f32[768]{0:T(1024)} %param.21) | copy-start | bytes 9220
  10.3 40.7 %copy-start.31 = (f32[768]{0:T(1024)S(1)}, f32[768]{0:T(1024)}, u32[]{:S(2)}) copy-start(f32[768]{0:T(1024)} %param.22) | copy-start | bytes 9220
  10.3 40.7 %copy-start.32 = (f32[768]{0:T(1024)S(1)}, f32[768]{0:T(1024)}, u32[]{:S(2)}) copy-start(f32[768]{0:T(1024)} %param.23) | copy-start | bytes 9220
  10.3 40.8 %copy-start.33 = (f32[768]{0:T(1024)S(1)}, f32[768]{0:T(1024)}, u32[]{:S(2)}) copy-start(f32[768]{0:T(1024)} %param.29) | copy-start | bytes 9220
  10.3 40.8 %copy-start.34 = (f32[576]{0:T(1024)S(1)}, f32[576]{0:T(1024)}, u32[]{:S(2)}) copy-start(f32[576]{0:T(1024)} %param.25) | copy-start | bytes 6916
  10.3 40.8 %copy-start.27 = (f32[768]{0:T(1024)S(1)}, f32[768]{0:T(1024)}, u32[]{:S(2)}) copy-start(f32[768]{0:T(1024)} %param.27) | copy-start | bytes 9220
  10.3 40.8 %copy-start.28 = (f32[768]{0:T(1024)S(1)}, f32[768]{0:T(1024)}, u32[]{:S(2)}) copy-start(f32[768]{0:T(1024)} %param.31) | copy-start | bytes 9220
  13.3 34.3 %collective-permute-start = (bf16[768,512]{1,0:T(8,128)(2,1)}, bf16[768,512]{1,0:T(8,128)(2,1)S(1)}, u32[]{:S(2)}, u32[]{:S(2)}) collective-permute-start(bf16[768,512]{1,0:T(8,128)(2,1)} %turn.3.refs_0_.x_ref), channel_id=1, source_target_pairs={{0,2},{1,3},{2,0},{3,1},{4,6},{5,7},{6,4},{7,5},{8,10},{9,11},{10,... | collective-permute-start | bytes 2359304 | tf_op jit(solution)/shard_map/ppermute | solution.py:685
  16.2 9.9 %collective-permute-start.6 = (bf16[96,576]{1,0:T(8,128)(2,1)}, bf16[96,576]{1,0:T(8,128)(2,1)S(1)}, u32[]{:S(2)}, u32[]{:S(2)}) collective-permute-start(bf16[96,576]{1,0:T(8,128)(2,1)} %refs_1_.1), channel_id=1, source_target_pairs={{0,24},{4,28},{8,16},{12,20},{16,8},{20,12},{24,0},{28,4},{1,25},{... | collective-permute-start | bytes 331784 | tf_op jit(solution)/shard_map/ppermute | solution.py:685
  19.9 20.8 %collective-permute-start.4 = (bf16[96,576]{1,0:T(8,128)(2,1)}, bf16[96,576]{1,0:T(8,128)(2,1)S(1)}, u32[]{:S(2)}, u32[]{:S(2)}) collective-permute-start(bf16[96,576]{1,0:T(8,128)(2,1)} %refs_1_.1), channel_id=1, source_target_pairs={{0,16},{4,20},{8,24},{12,28},{16,0},{20,4},{24,8},{28,12},{1,17},{... | collective-permute-start | bytes 331784 | tf_op jit(solution)/shard_map/ppermute | solution.py:685
  19.9 22.3 %collective-permute-start.2 = (bf16[96,576]{1,0:T(8,128)(2,1)}, bf16[96,576]{1,0:T(8,128)(2,1)S(1)}, u32[]{:S(2)}, u32[]{:S(2)}) collective-permute-start(bf16[96,576]{1,0:T(8,128)(2,1)} %refs_1_.1), channel_id=1, source_target_pairs={{0,8},{4,12},{8,0},{12,4},{16,24},{20,28},{24,16},{28,20},{1,9},{5... | collective-permute-start | bytes 331784 | tf_op jit(solution)/shard_map/ppermute | solution.py:685
  20.6 26.9 %collective-permute-start.1 = (bf16[96,576]{1,0:T(8,128)(2,1)}, bf16[96,576]{1,0:T(8,128)(2,1)S(1)}, u32[]{:S(2)}, u32[]{:S(2)}) collective-permute-start(bf16[96,576]{1,0:T(8,128)(2,1)} %refs_1_.1), channel_id=1, source_target_pairs={{0,4},{4,0},{8,12},{12,8},{16,20},{20,16},{24,28},{28,24},{1,5},{5... | collective-permute-start | bytes 331784 | tf_op jit(solution)/shard_map/ppermute | solution.py:685
  26.1 29.1 %copy-start.15 = (bf16[96,576]{1,0:T(8,128)(2,1)}, bf16[96,576]{1,0:T(8,128)(2,1)S(1)}, u32[]{:S(2)}) copy-start(bf16[96,576]{1,0:T(8,128)(2,1)S(1)} %collective-permute-done.6.refs_7_.refs_4_) | copy-start | bytes 331780
  26.1 21.4 %collective-permute-start.7 = (bf16[96,576]{1,0:T(8,128)(2,1)S(1)}, bf16[96,576]{1,0:T(8,128)(2,1)S(1)}, u32[]{:S(2)}, u32[]{:S(2)}) collective-permute-start(bf16[96,576]{1,0:T(8,128)(2,1)S(1)} %collective-permute-done.6.refs_7_.refs_4_), channel_id=1, source_target_pairs={{0,4},{4,0},{8,12},{12,8},{16,20},{20,16},{24,28},{28,24},{1,5},{5... | collective-permute-start | bytes 331784 | tf_op jit(solution)/shard_map/ppermute | solution.py:685
  40.6 14.6 %copy-start.16 = (bf16[96,576]{1,0:T(8,128)(2,1)}, bf16[96,576]{1,0:T(8,128)(2,1)S(1)}, u32[]{:S(2)}) copy-start(bf16[96,576]{1,0:T(8,128)(2,1)S(1)} %collective-permute-done.4.refs_6_.refs_3_) | copy-start | bytes 331780
  40.6 7.0 %collective-permute-start.5 = (bf16[96,576]{1,0:T(8,128)(2,1)S(1)}, bf16[96,576]{1,0:T(8,128)(2,1)S(1)}, u32[]{:S(2)}, u32[]{:S(2)}) collective-permute-start(bf16[96,576]{1,0:T(8,128)(2,1)S(1)} %collective-permute-done.4.refs_6_.refs_3_), channel_id=1, source_target_pairs={{0,4},{4,0},{8,12},{12,8},{16,20},{20,16},{24,28},{28,24},{1,5},{5... | collective-permute-start | bytes 331784 | tf_op jit(solution)/shard_map/ppermute | solution.py:685
  42.1 13.1 %copy-start.17 = (bf16[96,576]{1,0:T(8,128)(2,1)}, bf16[96,576]{1,0:T(8,128)(2,1)S(1)}, u32[]{:S(2)}) copy-start(bf16[96,576]{1,0:T(8,128)(2,1)S(1)} %collective-permute-done.2.refs_5_.refs_2_) | copy-start | bytes 331780
  42.1 5.5 %collective-permute-start.3 = (bf16[96,576]{1,0:T(8,128)(2,1)S(1)}, bf16[96,576]{1,0:T(8,128)(2,1)S(1)}, u32[]{:S(2)}, u32[]{:S(2)}) collective-permute-start(bf16[96,576]{1,0:T(8,128)(2,1)S(1)} %collective-permute-done.2.refs_5_.refs_2_), channel_id=1, source_target_pairs={{0,4},{4,0},{8,12},{12,8},{16,20},{20,16},{24,28},{28,24},{1,5},{5... | collective-permute-start | bytes 331784 | tf_op jit(solution)/shard_map/ppermute | solution.py:685
  47.5 7.7 %collective-permute-start.9 = (bf16[768,512]{1,0:T(8,128)(2,1)}, bf16[768,512]{1,0:T(8,128)(2,1)S(1)}, u32[]{:S(2)}, u32[]{:S(2)}) collective-permute-start(bf16[768,512]{1,0:T(8,128)(2,1)} %turn.3.refs_0_.x_ref), channel_id=1, source_target_pairs={{0,1},{1,0},{2,3},{3,2},{4,5},{5,4},{6,7},{7,6},{8,9},{9,8},{10,11... | collective-permute-start | bytes 2359304 | tf_op jit(solution)/shard_map/ppermute | solution.py:685
  49.2 22.8 %collective-permute-start.11 = (bf16[768,512]{1,0:T(8,128)(2,1)}, bf16[768,512]{1,0:T(8,128)(2,1)S(1)}, u32[]{:S(2)}, u32[]{:S(2)}) collective-permute-start(bf16[768,512]{1,0:T(8,128)(2,1)} %gate.2.refs_15_.refs_0_.dy_ref), channel_id=1, source_target_pairs={{0,2},{1,3},{2,0},{3,1},{4,6},{5,7},{6,4},{7,5},{8,10},{9,11},{10,... | collective-permute-start | bytes 2359304 | tf_op jit(solution)/shard_map/ppermute | solution.py:685
  49.2 6.0 %collective-permute-start.10 = (bf16[768,512]{1,0:T(8,128)(2,1)}, bf16[768,512]{1,0:T(8,128)(2,1)S(1)}, u32[]{:S(2)}, u32[]{:S(2)}) collective-permute-start(bf16[768,512]{1,0:T(8,128)(2,1)} %copy-done), channel_id=1, source_target_pairs={{0,1},{1,0},{2,3},{3,2},{4,5},{5,4},{6,7},{7,6},{8,9},{9,8},{10,11... | collective-permute-start | bytes 2359304 | tf_op jit(solution)/shard_map/ppermute | solution.py:685
  55.2 29.8 %collective-permute-start.8 = (bf16[768,512]{1,0:T(8,128)(2,1)}, bf16[768,512]{1,0:T(8,128)(2,1)}, u32[]{:S(2)}, u32[]{:S(2)}) collective-permute-start(bf16[768,512]{1,0:T(8,128)(2,1)} %gate.2.refs_15_.refs_0_.dy_ref), channel_id=1, source_target_pairs={{0,1},{1,0},{2,3},{3,2},{4,5},{5,4},{6,7},{7,6},{8,9},{9,8},{10,11... | collective-permute-start | bytes 2359304 | tf_op jit(solution)/shard_map/ppermute | solution.py:685
  55.2 0.9 copy-start.7
  55.2 1.1 copy-start.9
  72.0 0.9 copy-start.38
  78.7 6.3 %collective-permute-start.12 = (bf16[768,512]{1,0:T(8,128)(2,1)}, bf16[768,512]{1,0:T(8,128)(2,1)S(1)}, u32[]{:S(2)}, u32[]{:S(2)}) collective-permute-start(bf16[768,512]{1,0:T(8,128)(2,1)} %get-tuple-element.57.refs_2_), channel_id=1, source_target_pairs={{0,1},{1,0},{2,3},{3,2},{4,5},{5,4},{6,7},{7,6},{8,9},{9,8},{10,11... | collective-permute-start | bytes 2359304 | tf_op jit(solution)/shard_map/ppermute | solution.py:685
  85.0 0.9 copy-start.40
  116.7 1.1 copy-start.39
  117.9 10.0 %collective-permute-start.14 = (bf16[768,512]{1,0:T(8,128)(2,1)S(1)}, bf16[768,512]{1,0:T(8,128)(2,1)S(1)}, u32[]{:S(2)}, u32[]{:S(2)}) collective-permute-start(bf16[768,512]{1,0:T(8,128)(2,1)S(1)} %copy-done.39), channel_id=1, source_target_pairs={{0,1},{1,0},{2,3},{3,2},{4,5},{5,4},{6,7},{7,6},{8,9},{9,8},{10,11... | collective-permute-start | bytes 2359304 | tf_op jit(solution)/shard_map/ppermute | solution.py:685
  117.9 10.0 %copy-start.2 = (bf16[768,512]{1,0:T(8,128)(2,1)S(1)}, bf16[768,512]{1,0:T(8,128)(2,1)}, u32[]{:S(2)}) copy-start(bf16[768,512]{1,0:T(8,128)(2,1)} %get-tuple-element.63) | copy-start | bytes 2359300
  128.1 2.1 copy-start.3
  128.1 22.0 %collective-permute-start.15 = (bf16[768,512]{1,0:T(8,128)(2,1)S(1)}, bf16[768,512]{1,0:T(8,128)(2,1)S(1)}, u32[]{:S(2)}, u32[]{:S(2)}) collective-permute-start(bf16[768,512]{1,0:T(8,128)(2,1)S(1)} %add_convert_fusion.refs_0_), channel_id=1, source_target_pairs={{0,2},{1,3},{2,0},{3,1},{4,6},{5,7},{6,4},{7,5},{8,10},{9,11},{10,... | collective-permute-start | bytes 2359304 | tf_op jit(solution)/shard_map/ppermute | solution.py:685
  150.1 0.9 copy-start.4
  151.1 13.7 %copy-start.26 = (f32[8,768]{1,0:T(8,128)S(1)}, f32[8,768]{1,0:T(8,128)}, u32[]{:S(2)}) copy-start(f32[8,768]{1,0:T(8,128)} %get-tuple-element.74) | copy-start | bytes 73732
  151.1 16.8 %copy-start.37 = (bf16[768,512]{1,0:T(8,128)(2,1)S(1)}, bf16[768,512]{1,0:T(8,128)(2,1)}, u32[]{:S(2)}) copy-start(bf16[768,512]{1,0:T(8,128)(2,1)} %get-tuple-element.62) | copy-start | bytes 2359300
  164.7 5.8 %collective-permute-start.16 = (bf16[768,512]{1,0:T(8,128)(2,1)}, bf16[768,512]{1,0:T(8,128)(2,1)S(1)}, u32[]{:S(2)}, u32[]{:S(2)}) collective-permute-start(bf16[768,512]{1,0:T(8,128)(2,1)} %get-tuple-element.72), channel_id=1, source_target_pairs={{0,1},{1,0},{2,3},{3,2},{4,5},{5,4},{6,7},{7,6},{8,9},{9,8},{10,11... | collective-permute-start | bytes 2359304 | tf_op jit(solution)/shard_map/ppermute | solution.py:685
  165.6 3.8 %collective-permute-start.18 = (f32[4,768]{1,0:T(4,128)S(1)}, f32[4,768]{1,0:T(4,128)S(1)}, u32[]{:S(2)}, u32[]{:S(2)}) collective-permute-start(f32[4,768]{1,0:T(4,128)S(1)} %pad_maximum_fusion.2), channel_id=1, source_target_pairs={{0,2},{1,3},{2,0},{3,1},{4,6},{5,7},{6,4},{7,5},{8,10},{9,11},{10,... | collective-permute-start | bytes 36872 | tf_op jit(solution)/shard_map/ppermute | solution.py:685
  166.7 3.1 %collective-permute-start.19 = (f32[4,768]{1,0:T(4,128)S(1)}, f32[4,768]{1,0:T(4,128)S(1)}, u32[]{:S(2)}, u32[]{:S(2)}) collective-permute-start(f32[4,768]{1,0:T(4,128)S(1)} %pad_maximum_fusion.2), channel_id=1, source_target_pairs={{0,3},{1,2},{2,1},{3,0},{4,7},{5,6},{6,5},{7,4},{8,11},{9,10},{10,... | collective-permute-start | bytes 36872 | tf_op jit(solution)/shard_map/ppermute | solution.py:685
  167.5 2.3 %collective-permute-start.17 = (f32[4,768]{1,0:T(4,128)S(1)}, f32[4,768]{1,0:T(4,128)S(1)}, u32[]{:S(2)}, u32[]{:S(2)}) collective-permute-start(f32[4,768]{1,0:T(4,128)S(1)} %pad_maximum_fusion.2), channel_id=1, source_target_pairs={{0,1},{1,0},{2,3},{3,2},{4,5},{5,4},{6,7},{7,6},{8,9},{9,8},{10,11... | collective-permute-start | bytes 36872 | tf_op jit(solution)/shard_map/ppermute | solution.py:685
  167.8 25.7 %collective-permute-start.13 = (bf16[768,512]{1,0:T(8,128)(2,1)S(1)}, bf16[768,512]{1,0:T(8,128)(2,1)S(1)}, u32[]{:S(2)}, u32[]{:S(2)}) collective-permute-start(bf16[768,512]{1,0:T(8,128)(2,1)S(1)} %copy-done.37), channel_id=1, source_target_pairs={{0,1},{1,0},{2,3},{3,2},{4,5},{5,4},{6,7},{7,6},{8,9},{9,8},{10,11... | collective-permute-start | bytes 2359304 | tf_op jit(solution)/shard_map/ppermute | solution.py:685
  169.4 37.8 %collective-permute-start.20 = (bf16[768,512]{1,0:T(8,128)(2,1)}, bf16[768,512]{1,0:T(8,128)(2,1)S(1)}, u32[]{:S(2)}, u32[]{:S(2)}) collective-permute-start(bf16[768,512]{1,0:T(8,128)(2,1)} %get-tuple-element.76), channel_id=1, source_target_pairs={{0,1},{1,0},{2,3},{3,2},{4,5},{5,4},{6,7},{7,6},{8,9},{9,8},{10,11... | collective-permute-start | bytes 2359304 | tf_op jit(solution)/shard_map/ppermute | solution.py:685
  170.4 22.4 %copy-start.21 = (f32[4,768]{1,0:T(4,128)S(1)}, f32[4,768]{1,0:T(4,128)}, u32[]{:S(2)}) copy-start(f32[4,768]{1,0:T(4,128)} %add_add_fusion.refs_0_) | copy-start | bytes 36868
  170.4 0.9 copy-start.1
  173.7 34.0 %collective-permute-start.21 = (bf16[768,512]{1,0:T(8,128)(2,1)}, bf16[768,512]{1,0:T(8,128)(2,1)S(1)}, u32[]{:S(2)}, u32[]{:S(2)}) collective-permute-start(bf16[768,512]{1,0:T(8,128)(2,1)} %share.1.refs_0_), channel_id=1, source_target_pairs={{0,2},{1,3},{2,0},{3,1},{4,6},{5,7},{6,4},{7,5},{8,10},{9,11},{10,... | collective-permute-start | bytes 2359304 | tf_op jit(solution)/shard_map/ppermute | solution.py:685
  174.5 14.0 %collective-permute-start.22 = (bf16[384,576]{1,0:T(8,128)(2,1)}, bf16[384,576]{1,0:T(8,128)(2,1)S(1)}, u32[]{:S(2)}, u32[]{:S(2)}) collective-permute-start(bf16[384,576]{1,0:T(8,128)(2,1)} %get-tuple-element.78), channel_id=1, source_target_pairs={{0,4},{4,0},{8,12},{12,8},{16,20},{20,16},{24,28},{28,24},{1,5},{5... | collective-permute-start | bytes 1327112 | tf_op jit(solution)/shard_map/ppermute | solution.py:685
  191.4 13.7 %collective-permute-start.23 = (bf16[96,576]{1,0:T(8,128)(2,1)}, bf16[96,576]{1,0:T(8,128)(2,1)S(1)}, u32[]{:S(2)}, u32[]{:S(2)}) collective-permute-start(bf16[96,576]{1,0:T(8,128)(2,1)} %get-tuple-element.80), channel_id=1, source_target_pairs={{0,8},{4,12},{8,0},{12,4},{16,24},{20,28},{24,16},{28,20},{1,9},{5... | collective-permute-start | bytes 331784 | tf_op jit(solution)/shard_map/ppermute | solution.py:685
  193.5 0.9 copy-start.8
  194.4 4.6 %copy-start.42 = (bf16[96,576]{1,0:T(8,128)(2,1)S(1)}, bf16[96,576]{1,0:T(8,128)(2,1)}, u32[]{:S(2)}) copy-start(bf16[96,576]{1,0:T(8,128)(2,1)} %get-tuple-element.81) | copy-start | bytes 331780
  194.4 8.1 %copy-start.41 = (bf16[96,576]{1,0:T(8,128)(2,1)S(1)}, bf16[96,576]{1,0:T(8,128)(2,1)}, u32[]{:S(2)}) copy-start(bf16[96,576]{1,0:T(8,128)(2,1)} %get-tuple-element.82) | copy-start | bytes 331780
  194.4 15.2 %copy-start.35 = (s32[3]{0:T(128)S(1)}, s32[3]{0:T(128)}, u32[]{:S(2)}) copy-start(s32[3]{0:T(128)} %constant.30.clone) | copy-start | bytes 40
  194.4 15.2 %copy-start.36 = (s32[3]{0:T(128)S(1)}, s32[3]{0:T(128)}, u32[]{:S(2)}) copy-start(s32[3]{0:T(128)} %constant.29.clone) | copy-start | bytes 40
  198.5 4.0 %collective-permute-start.26 = (f32[8,768]{1,0:T(8,128)}, f32[8,768]{1,0:T(8,128)S(1)}, u32[]{:S(2)}, u32[]{:S(2)}) collective-permute-start(f32[8,768]{1,0:T(8,128)} %gate.3), channel_id=1, source_target_pairs={{0,4},{4,0},{8,12},{12,8},{16,20},{20,16},{24,28},{28,24},{1,5},{5... | collective-permute-start | bytes 73736 | tf_op jit(solution)/shard_map/ppermute | solution.py:685
  199.0 16.4 %collective-permute-start.24 = (bf16[96,576]{1,0:T(8,128)(2,1)S(1)}, bf16[96,576]{1,0:T(8,128)(2,1)S(1)}, u32[]{:S(2)}, u32[]{:S(2)}) collective-permute-start(bf16[96,576]{1,0:T(8,128)(2,1)S(1)} %copy-done.42), channel_id=1, source_target_pairs={{0,16},{4,20},{8,24},{12,28},{16,0},{20,4},{24,8},{28,12},{1,17},{... | collective-permute-start | bytes 331784 | tf_op jit(solution)/shard_map/ppermute | solution.py:685
  202.5 12.9 %collective-permute-start.25 = (bf16[96,576]{1,0:T(8,128)(2,1)S(1)}, bf16[96,576]{1,0:T(8,128)(2,1)S(1)}, u32[]{:S(2)}, u32[]{:S(2)}) collective-permute-start(bf16[96,576]{1,0:T(8,128)(2,1)S(1)} %copy-done.41), channel_id=1, source_target_pairs={{0,24},{4,28},{8,16},{12,20},{16,8},{20,12},{24,0},{28,4},{1,25},{... | collective-permute-start | bytes 331784 | tf_op jit(solution)/shard_map/ppermute | solution.py:685
  205.1 10.4 %copy-start.22 = (f32[8,768]{1,0:T(8,128)}, f32[8,768]{1,0:T(8,128)S(1)}, u32[]{:S(2)}) copy-start(f32[8,768]{1,0:T(8,128)S(1)} %add.33.refs_3_) | copy-start | bytes 73732
  205.1 10.4 %copy-start.18 = (bf16[96,576]{1,0:T(8,128)(2,1)}, bf16[96,576]{1,0:T(8,128)(2,1)S(1)}, u32[]{:S(2)}) copy-start(bf16[96,576]{1,0:T(8,128)(2,1)S(1)} %collective-permute-done.23.refs_0_) | copy-start | bytes 331780
  205.1 10.3 %collective-permute-start.29 = (f32[8,768]{1,0:T(8,128)S(1)}, f32[8,768]{1,0:T(8,128)S(1)}, u32[]{:S(2)}, u32[]{:S(2)}) collective-permute-start(f32[8,768]{1,0:T(8,128)S(1)} %add.33.refs_3_), channel_id=1, source_target_pairs={{0,24},{4,28},{8,16},{12,20},{16,8},{20,12},{24,0},{28,4},{1,25},{... | collective-permute-start | bytes 73736 | tf_op jit(solution)/shard_map/ppermute | solution.py:685
  207.2 2.9 %copy-start.5 = (bf16[768,512]{1,0:T(8,128)(2,1)}, bf16[768,512]{1,0:T(8,128)(2,1)S(1)}, u32[]{:S(2)}) copy-start(bf16[768,512]{1,0:T(8,128)(2,1)S(1)} %collective-permute-done.20.near_ref) | copy-start | bytes 2359300
  207.2 8.3 %collective-permute-start.28 = (f32[8,768]{1,0:T(8,128)S(1)}, f32[8,768]{1,0:T(8,128)S(1)}, u32[]{:S(2)}, u32[]{:S(2)}) collective-permute-start(f32[8,768]{1,0:T(8,128)S(1)} %add.33.refs_3_), channel_id=1, source_target_pairs={{0,16},{4,20},{8,24},{12,28},{16,0},{20,4},{24,8},{28,12},{1,17},{... | collective-permute-start | bytes 73736 | tf_op jit(solution)/shard_map/ppermute | solution.py:685
  207.8 2.3 %copy-start.6 = (bf16[768,512]{1,0:T(8,128)(2,1)}, bf16[768,512]{1,0:T(8,128)(2,1)S(1)}, u32[]{:S(2)}) copy-start(bf16[768,512]{1,0:T(8,128)(2,1)S(1)} %collective-permute-done.21.far_ref) | copy-start | bytes 2359300
  207.8 7.7 %collective-permute-start.27 = (f32[8,768]{1,0:T(8,128)S(1)}, f32[8,768]{1,0:T(8,128)S(1)}, u32[]{:S(2)}, u32[]{:S(2)}) collective-permute-start(f32[8,768]{1,0:T(8,128)S(1)} %add.33.refs_3_), channel_id=1, source_target_pairs={{0,8},{4,12},{8,0},{12,4},{16,24},{20,28},{24,16},{28,20},{1,9},{5... | collective-permute-start | bytes 73736 | tf_op jit(solution)/shard_map/ppermute | solution.py:685
  (11 other events, 7.7 us)
Sparse Core Ops, SparseCore 0:
  10.2 63.6 all-gather.1
  116.9 73.3 reduce-scatter.1
